TPU v7x, 512 devices: a whole 4x4x16 slice. The times are simulated.
512 devices in a mesh: seq: 64 (over y, z_lo, core), head: 8 (over x, z_hi).
Axes of the slice: x: 4, y: 4, z: 16 (z_hi: 2, z_lo: 8; z = z_hi * 8 + z_lo), core: 2. Of those that a mesh axis runs over, the one named last changes fastest.
Arguments:
- query_content: bfloat16 [4096, 64, 128], P('seq', 'head'), may hold values from -15 to 15
- query_rotary: bfloat16 [4096, 4096], P('seq', 'head'), may hold values from -70 to 70
- key_cache: bfloat16 [576, 8192], P(None, 'seq'), may hold values from -5 to 5
- key_up: bfloat16 [512, 64, 128], P(None, 'head'), may hold values from -0.25 to 0.25
- value_up: bfloat16 [512, 64, 128], P(None, 'head'), may hold values from -0.25 to 0.25
- output_weight: bfloat16 [8192, 7168], P('head', 'seq'), may hold values from -0.0625 to 0.0625
- query_start: int32 [1], replicated, may hold values from 3840 to 4096
- key_limit: int32 [1], replicated, may hold values from 7681 to 8192
- block_order: int32 [128], P('seq'), may hold values from 0 to 127, each once
Outputs:
- projected: bfloat16 [4096, 7168], P(('seq', 'head'))
Inputs may be any that keep to these rules, and one draw needn't show every extreme that they name: `block_order`: every block number appears in exactly one slot.
All inputs are finite; a program needn't handle non-finite values.
Results may differ from a plain program's by a relative error of at most 0.02.
Values may be sent and summed in bfloat16 or wider, within the bound.
No kernel may reach another device: no remote copies, remote signals or barrier semaphores. Data moves between devices by JAX's collectives and lax.ppermute only.
A program may use at most 64 MiB of HBM per device.

v0:
```python
import math

import jax
import jax.numpy as jnp
from jax import lax
from jax.sharding import PartitionSpec as P

NEG_FILL = -1e30


def largest_divisor(width, ceiling):
    best_step = 1
    for candidate in range(1, min(width, ceiling) + 1):
        if width % candidate == 0:
            best_step = candidate
    return best_step


def attend_block(
    carry, keys_block, key_positions, query_rows, query_positions, limit, scale, latent_dim
):
    best, total, mixed = carry
    scores = jnp.dot(query_rows, keys_block, preferred_element_type=jnp.float32) * scale
    visible = (key_positions[None, :] <= query_positions[:, None]) & (
        key_positions[None, :] < limit
    )
    scores = jnp.where(visible, scores, NEG_FILL)
    fresh = jnp.maximum(best, jnp.max(scores, axis=1))
    weights = jnp.where(visible, jnp.exp(scores - fresh[:, None]), 0.0)
    factor = jnp.exp(best - fresh)
    total = total * factor + jnp.sum(weights, axis=1)
    values = lax.dot_general(
        weights.astype(jnp.bfloat16),
        keys_block[:latent_dim],
        (((1,), (1,)), ((), ())),
        preferred_element_type=jnp.float32,
    )
    mixed = mixed * factor[:, None] + values
    return (fresh, total, mixed)


def per_device(
    query_content,
    query_rotary,
    key_cache,
    key_up,
    value_up,
    output_weight,
    query_start,
    key_limit,
    block_order,
):
    tokens_here, heads_here, nope_dim = query_content.shape
    latent_dim = key_up.shape[0]
    rope_dim = query_rotary.shape[1] // heads_here
    value_dim = value_up.shape[2]
    seq_count = lax.axis_size("seq")
    head_count = lax.axis_size("head")
    half_rows = tokens_here // 2
    scale = 1.0 / math.sqrt(nope_dim + rope_dim)
    token_ids = jnp.arange(tokens_here, dtype=jnp.int32)
    block_ids = jnp.where(token_ids < half_rows, block_order[0], block_order[1])
    token_positions = query_start[0] + block_ids * half_rows + token_ids % half_rows
    query_positions = jnp.repeat(token_positions, heads_here)
    limit = key_limit[0]
    latent_query = jnp.einsum(
        "thd,chd->thc", query_content, key_up, preferred_element_type=jnp.float32
    ).astype(jnp.bfloat16)
    row_count = tokens_here * heads_here
    query_rows = jnp.concatenate(
        [latent_query, query_rotary.reshape(tokens_here, heads_here, rope_dim)], axis=2
    ).reshape(row_count, latent_dim + rope_dim)
    initial = (
        jnp.full((row_count,), NEG_FILL, jnp.float32),
        jnp.zeros((row_count,), jnp.float32),
        jnp.zeros((row_count, latent_dim), jnp.float32),
    )
    piece = lax.all_gather(key_cache, "seq", axis=1, tiled=True)
    start = jnp.int32(0)
    piece_width = piece.shape[1]
    step_width = largest_divisor(piece_width, 512)

    def advance(position, state):
        offset = position * step_width
        keys_block = lax.dynamic_slice_in_dim(piece, offset, step_width, 1)
        key_positions = start + offset + jnp.arange(step_width, dtype=jnp.int32)
        return attend_block(
            state, keys_block, key_positions, query_rows, query_positions, limit, scale, latent_dim
        )

    best, total, mixed = lax.fori_loop(0, piece_width // step_width, advance, initial)
    mixed_latent = (
        (mixed / total[:, None]).astype(jnp.bfloat16).reshape(tokens_here, heads_here, latent_dim)
    )
    head_values = jnp.einsum(
        "thc,chv->thv", mixed_latent, value_up, preferred_element_type=jnp.float32
    ).astype(jnp.bfloat16)
    flat_values = head_values.reshape(tokens_here, heads_here * value_dim)
    column_part = jnp.dot(
        lax.all_gather(flat_values, "seq", axis=0, tiled=True),
        output_weight,
        preferred_element_type=jnp.float32,
    )
    column_width = output_weight.shape[1]
    rows_share = tokens_here // head_count
    sectioned = column_part.reshape(seq_count, head_count, rows_share, column_width)
    summed = lax.psum_scatter(
        sectioned.astype(jnp.bfloat16), "head", scatter_dimension=1, tiled=True
    ).astype(jnp.float32)
    rounded = summed.reshape(seq_count, rows_share, column_width).astype(jnp.bfloat16)
    regrouped = lax.all_to_all(rounded, "seq", split_axis=0, concat_axis=2, tiled=True)
    return regrouped.reshape(rows_share, seq_count * column_width)


def solution(mesh):
    in_specs = (
        P("seq", "head", None),
        P("seq", "head"),
        P(None, "seq"),
        P(None, "head", None),
        P(None, "head", None),
        P("head", "seq"),
        P(),
        P(),
        P("seq"),
    )
    out_specs = P(("seq", "head"), None)
    return jax.shard_map(
        per_device, mesh=mesh, in_specs=in_specs, out_specs=out_specs, check_vma=False
    )
```

profile of v0, /device:TPU:1, one launch (start us, length us, event | category | flops | bytes accessed | tf_op | source)
XLA Modules:
  0.0 627.5 jit_solution(1306723930941238080)
XLA Ops:
  14.7 143.5 %all-gather.3.cloned.1.call-done = bf16[576,8192]{1,0:T(8,128)(2,1)} async-done(((bf16[576,128]{1,0:T(8,128)(2,1)}), bf16[576,8192]{1,0:T(8,128)(2,1)}) %all-gather.3.cloned.1.call-update) | async-done | bytes 9437200 | tf_op jit(solution)/shard_map/all_gather | solution.py:78
  158.1 81.7 %while.18 = (s32[]{:T(128)}, f32[512]{0:T(512)S(1)}, f32[512]{0:T(512)S(1)}, f32[512,512]{1,0:T(8,128)S(1)}, s32[]{:T(128)}, /*index=5*/bf16[576,8192]{1,0:T(8,1...) while((s32[]{:T(128)}, f32[512]{0:T(512)S(1)}, ...), condition=%wide.region_3.4_spmd.clone, body=%wide.region_0.3_spmd.clone.sunk | while | flops 575148032 | bytes 7068099 | solution.py:91
  159.0 2.0 fusion.42
  161.4 1.8 convolution_add_fusion.2
  164.1 2.0 fusion.42
  169.2 2.0 fusion.42
  171.6 1.8 convolution_add_fusion.2
  174.3 2.0 fusion.42
  179.4 2.0 fusion.42
  181.8 1.8 convolution_add_fusion.2
  184.5 2.0 fusion.42
  186.9 1.8 convolution_add_fusion.2
  189.6 2.0 fusion.42
  192.0 1.8 convolution_add_fusion.2
  194.7 2.0 fusion.42
  197.1 1.8 convolution_add_fusion.2
  199.8 2.0 fusion.42
  202.2 1.8 convolution_add_fusion.2
  204.9 2.0 fusion.42
  210.0 2.0 fusion.42
  212.4 1.8 convolution_add_fusion.2
  215.1 2.0 fusion.42
  220.2 2.0 fusion.42
  222.6 1.8 convolution_add_fusion.2
  225.4 2.0 fusion.42
  230.5 2.0 fusion.42
  232.8 1.8 convolution_add_fusion.2
  235.6 2.0 fusion.42
  241.2 124.0 %all-gather.5.cloned.1.call-done = bf16[4096,1024]{1,0:T(8,128)(2,1)} async-done(((bf16[64,1024]{1,0:T(8,128)(2,1)}), bf16[4096,1024]{1,0:T(8,128)(2,1)}) %all-gather.5.cloned.1.call-update) | async-done | bytes 8388624 | tf_op jit(solution)/shard_map/all_gather | solution.py:100
  365.1 6.2 convolution_convert_fusion
  373.9 219.9 %all-reduce.3.cloned.1.call-done = bf16[64,8,8,112]{3,2,1,0:T(8,128)(2,1)} async-done(((bf16[64,8,8,112]{3,2,1,0:T(8,128)(2,1)}), bf16[64,8,8,112]{3,2,1,0:T(8,128)(2,1)}) %all-reduce.3.cloned.1.call-update) | async-done | bytes 917520
  595.4 24.7 %all_to_all.15 = bf16[64,8,112]{2,1,0:T(8,128)(2,1)S(1)} all-to-all(bf16[64,8,112]{2,1,0:T(8,128)(2,1)S(1)} %dynamic-slice_bitcast_fusion), channel_id=1, replica_groups=mesh['seq'=64,'head'=8] {'seq'}, dimensions={0} | all-to-all | bytes 229376 | tf_op jit(solution)/shard_map/all_to_all | solution.py:111
  (161 shorter events, 44.1 us)
Async XLA Ops:
  6.5 233.4 %copy-start = (bf16[512,8,128]{2,1,0:T(8,128)(2,1)S(1)}, bf16[512,8,128]{2,1,0:T(8,128)(2,1)}, u32[]{:S(2)}) copy-start(bf16[512,8,128]{2,1,0:T(8,128)(2,1)} %param.15) | copy-start | bytes 3145732
  6.5 151.6 %all-gather.3.cloned.1.call-start = ((), (), s32[]{:S(2)}) async-start(), calls=%async_computation.1 | async-start | bytes 9584640 | tf_op jit(solution)/shard_map/all_gather | solution.py:78
  7.3 357.9 %all-gather.5.cloned.1.call-start = ((), (), s32[]{:S(2)}) async-start(), calls=%async_computation.2 | async-start | bytes 8519680 | tf_op jit(solution)/shard_map/all_gather | solution.py:100
  158.1 207.0 %copy-start.1 = (bf16[1024,112]{0,1:T(8,128)(2,1)S(1)}, bf16[1024,112]{0,1:T(8,128)(2,1)}, u32[]{:S(2)}) copy-start(bf16[1024,112]{0,1:T(8,128)(2,1)} %param.16) | copy-start | bytes 688132
  241.1 352.7 %all-reduce.3.cloned.1.call-start = ((), (), s32[]{:S(2)}) async-start(), calls=%async_computation.3 | async-start | bytes 2097152
Sparse Core Ops, SparseCore 0:
  9.4 148.6 all-gather.2
  241.3 123.8 all-gather.4
  372.8 220.9 all-reduce.2
where the time goes:
time: 629 us; the launch traced here: 628 us
  waiting for transfers between devices  488 us (78%)
  matrix products  69.6 us (11%)
  blocking collectives  24.7 us (4%)
  other arithmetic  19.1 us (3%)
  between operations  13.9 us (2%)
  local copies, waits for them, and re-layouts  11 us (2%)
    unnamed x4, waiting for transfers between devices  221 us
    all_gather x1, waiting for transfers between devices, per_device(): piece = lax.all_gather(key_cache, 'seq', axis=1, tiled=True)  143 us
    all_gather x1, waiting for transfers between devices, per_device(): lax.all_gather(flat_values, 'seq', axis=0, tiled=True)  124 us
    dot_general x16, matrix products, attend_block(): jnp.dot(query_rows, keys_block, preferred_element_type=jnp.float32) * scale  31.9 us
    dot_general x16, matrix products, attend_block(): lax.dot_general(weights.astype(jnp.bfloat16), keys_block[:latent_dim], ((...  29.3 us
    all_to_all x1, blocking collectives, per_device(): lax.all_to_all(rounded, 'seq', split_axis=0, concat_axis=2, tiled=True)  24.7 us
  transfers between devices with their start and end apart: 3, of which 3 were waited for; matrix products, arithmetic and copies ran while one was open for 1% of the time, Pallas kernels for 0%

commit v1 on v0

v1 whole, which is shorter than its diff:
```python
import functools
import math

import jax
import jax.numpy as jnp
import numpy as np
from jax import lax
from jax.experimental import pallas as pl
from jax.experimental.pallas import tpu as pltpu
from jax.sharding import Mesh, PartitionSpec as P

NEG = -1e30
LOG2E = 1.4426950408889634
SIZES = {"y": 4, "z": 8, "c": 2, "x": 4, "h": 2}
NAMES = tuple(SIZES)
SHIFTS = (1, -1, 2, -2, 3, -3, 4)
STATS = 128


def permute(x, names, move):
    dims = [SIZES[n] for n in names]
    pairs = []
    for place in np.ndindex(*dims):
        target = move(dict(zip(names, place)))
        pairs.append(
            (
                int(np.ravel_multi_index(place, dims)),
                int(np.ravel_multi_index([target[n] for n in names], dims)),
            )
        )
    return lax.ppermute(x, names, pairs)


def along_z(x, step):
    def move(at):
        place = (at["h"] * 8 + at["z"] + step) % 16
        return {"h": place // 8, "z": place % 8}

    return permute(x, ("z", "h"), move)


def other_core(x):
    return permute(x, ("c",), lambda at: {"c": 1 - at["c"]})


def query_kernel(content, rotary, key_up, out):
    head = pl.program_id(0)
    latent = lax.dot_general(
        content[...], key_up[...], (((1,), (1,)), ((), ())), preferred_element_type=jnp.float32
    )
    out[0, :, : latent.shape[1]] = latent.astype(out.dtype)
    pair = rotary[...]
    half = pair.shape[1] // 2
    out[0, :, latent.shape[1] :] = jnp.where(head % 2 == 0, pair[:, :half], pair[:, half:])


def latent_queries(payload, key_up, heads, nope, rope):
    rows = payload.shape[0]
    latent = key_up.shape[0]
    return pl.pallas_call(
        query_kernel,
        grid=(heads,),
        in_specs=[
            pl.BlockSpec((rows, nope), lambda i: (0, i)),
            pl.BlockSpec((rows, 2 * rope), lambda i: (0, heads * nope // (2 * rope) + i // 2)),
            pl.BlockSpec((latent, nope), lambda i: (0, i)),
        ],
        out_specs=pl.BlockSpec((1, rows, latent + rope), lambda i: (i, 0, 0)),
        out_shape=jax.ShapeDtypeStruct((heads, rows, latent + rope), jnp.bfloat16),
    )(payload, payload, key_up)


def attend_kernel(
    starts, bases, limit_ref, query, *rest, shards, coef, latent, block, heads, groups
):
    keys, value_up, out, mixed = rest[:shards], rest[shards], rest[shards + 1], rest[shards + 2]
    group = pl.program_id(0)
    rows = heads * block
    width = keys[0].shape[1]
    limit = limit_ref[0]
    lowest, highest = bases[0], bases[0]
    for i in range(1, shards):
        lowest = jnp.minimum(lowest, bases[i])
        highest = jnp.maximum(highest, bases[i])

    def write(half, normal, lse):
        at = pl.ds(group * 2 * block + half * block, block)
        mixed[:, at, :] = normal.astype(mixed.dtype).reshape(heads, block, latent)
        lane = lax.broadcasted_iota(jnp.int32, (block, STATS), 1)
        parts = []
        left = lse
        for _ in range(3):
            part = left.astype(jnp.bfloat16).astype(jnp.float32)
            parts.append(part)
            left = left - part
        stats = jnp.zeros((block, STATS), jnp.float32)
        for k, part in enumerate(parts):
            for h in range(heads):
                stats = jnp.where(
                    lane == k * heads + h, part[h * block : (h + 1) * block, :], stats
                )
        out[at, out.shape[1] - STATS :] = stats.astype(out.dtype)

    def run(half, masked):
        rows_q = query[:, half * block : (half + 1) * block, :].reshape(rows, -1)
        k = jnp.concatenate([r[...] for r in keys], axis=1)
        s = jnp.dot(rows_q, k, preferred_element_type=jnp.float32)
        if masked:
            token = lax.broadcasted_iota(jnp.int32, (rows, width), 0) % block
            last = jnp.minimum(starts[group * 2 + half] + token, limit - 1)
            lane = lax.broadcasted_iota(jnp.int32, (rows, width), 1)
            s = jnp.concatenate(
                [
                    jnp.where(lane + bases[i] <= last, s[:, i * width : (i + 1) * width], NEG)
                    for i in range(shards)
                ],
                axis=1,
            )
        top = jnp.max(s, axis=1, keepdims=True)
        if masked:
            top = jnp.maximum(top, NEG / 10)
        weights = jnp.exp2(s * coef - top * coef)
        total = jnp.sum(weights, axis=1, keepdims=True)
        values = lax.dot_general(
            weights.astype(jnp.bfloat16),
            k[:latent],
            (((1,), (1,)), ((), ())),
            preferred_element_type=jnp.float32,
        )
        if masked:
            some = total > 0
            safe = jnp.where(some, total, 1.0)
            write(half, values / safe, jnp.where(some, top * coef + jnp.log2(safe), NEG))
        else:
            write(half, values / total, top * coef + jnp.log2(total))

    for half in range(2):
        start = starts[group * 2 + half]
        sure = highest + width - 1 <= jnp.minimum(start, limit - 1)
        some = lowest <= jnp.minimum(start + block - 1, limit - 1)

        @pl.when(sure)
        def _():
            run(half, False)

        @pl.when(jnp.logical_and(some, jnp.logical_not(sure)))
        def _():
            run(half, True)

        @pl.when(jnp.logical_not(some))
        def _():
            write(half, jnp.zeros((rows, latent), jnp.float32), jnp.full((rows, 1), NEG))

    @pl.when(group == groups - 1)
    def _():
        for h in range(heads):
            cols = slice(h * 128, (h + 1) * 128)
            out[:, cols] = jnp.dot(
                mixed[h], value_up[:, cols], preferred_element_type=jnp.float32
            ).astype(out.dtype)


def attend(starts, bases, limit, query, keys, value_up, scale):
    heads, tokens, depth = query.shape
    latent, value_width = value_up.shape
    shards = len(keys)
    groups = starts.shape[0] // 2
    per_group = tokens // groups
    whole = lambda shape: pl.BlockSpec(shape, lambda i, *_: (0, 0))
    kernel = functools.partial(
        attend_kernel,
        shards=shards,
        coef=scale * LOG2E,
        latent=latent,
        block=per_group // 2,
        heads=heads,
        groups=groups,
    )
    return pl.pallas_call(
        kernel,
        grid_spec=pltpu.PrefetchScalarGridSpec(
            num_scalar_prefetch=3,
            grid=(groups,),
            in_specs=[pl.BlockSpec((heads, per_group, depth), lambda i, *_: (0, i, 0))]
            + [whole(k.shape) for k in keys]
            + [whole(value_up.shape)],
            out_specs=whole((tokens, value_width + STATS)),
            scratch_shapes=[pltpu.VMEM((heads, tokens, latent), jnp.bfloat16)],
        ),
        out_shape=jax.ShapeDtypeStruct((tokens, value_width + STATS), jnp.bfloat16),
        compiler_params=pltpu.CompilerParams(vmem_limit_bytes=48 * 1024 * 1024),
    )(starts, bases, limit, query, *keys, value_up)


def merge_kernel(parts, out, *, heads, sources):
    width = out.shape[1]
    each = width // heads
    lses = []
    for s in range(sources):
        stats = parts[s, :, width:].astype(jnp.float32)
        lses.append(
            stats[:, :heads] + stats[:, heads : 2 * heads] + stats[:, 2 * heads : 3 * heads]
        )
    top = functools.reduce(jnp.maximum, lses)
    weights = [jnp.exp2(v - top) for v in lses]
    total = functools.reduce(jnp.add, weights)
    weights = [w / total for w in weights]
    for h in range(heads):
        cols = slice(h * each, (h + 1) * each)
        value = functools.reduce(
            jnp.add,
            [
                weights[s][:, h : h + 1] * parts[s, :, cols].astype(jnp.float32)
                for s in range(sources)
            ],
        )
        out[:, cols] = value.astype(out.dtype)


def merge(parts, heads):
    sources, tokens, width = parts.shape
    return pl.pallas_call(
        functools.partial(merge_kernel, heads=heads, sources=sources),
        out_shape=jax.ShapeDtypeStruct((tokens, width - STATS), jnp.bfloat16),
    )(parts)


def per_device(
    query_content,
    query_rotary,
    key_cache,
    key_up,
    value_up,
    output_weight,
    query_start,
    key_limit,
    block_order,
):
    tokens, heads, nope = query_content.shape
    latent = key_up.shape[0]
    rope = query_rotary.shape[1] // heads
    value_dim = value_up.shape[2]
    columns = output_weight.shape[1]
    block = tokens // 2
    scale = 1.0 / math.sqrt(nope + rope)
    shard = key_cache.shape[1]
    y, z, c = lax.axis_index("y"), lax.axis_index("z"), lax.axis_index("c")

    shards = [key_cache] + [along_z(key_cache, s) for s in SHIFTS]
    offsets = jnp.array((0,) + SHIFTS, jnp.int32)
    bases = ((y * 8 + (z - offsets) % 8) * 2 + c).astype(jnp.int32) * shard

    weight = lax.all_gather(output_weight.T, ("z", "c"), axis=0, tiled=True)

    numbers = jnp.repeat(block_order, block, total_repeat_length=tokens).astype(jnp.bfloat16)
    payload = jnp.concatenate(
        [
            query_content.reshape(tokens, heads * nope),
            query_rotary,
            jnp.broadcast_to(numbers[:, None], (tokens, STATS)),
        ],
        axis=1,
    )
    payload = lax.all_gather(payload, "y", axis=0)
    partner = other_core(payload)
    first = jnp.where(c == 0, payload, partner)
    second = jnp.where(c == 0, partner, payload)
    payload = jnp.stack([first, second], axis=1).reshape(8 * tokens, -1)
    starts = query_start[0] + payload[::block, -1].astype(jnp.int32) * block

    queries = latent_queries(payload, key_up.reshape(latent, heads * nope), heads, nope, rope)
    partial = attend(
        starts,
        bases,
        key_limit,
        queries,
        shards,
        value_up.reshape(latent, heads * value_dim),
        scale,
    )
    partial = lax.all_to_all(
        partial.reshape(8, tokens, -1), ("y", "c"), split_axis=0, concat_axis=0, tiled=True
    )
    values = merge(partial, heads)

    rows = lax.all_gather(values, "y", axis=0, tiled=True)
    product = lax.dot_general(
        rows, weight, (((1,), (1,)), ((), ())), preferred_element_type=jnp.float32
    ).astype(jnp.bfloat16)
    share = tokens // 8
    width = 16 * columns
    product = lax.all_to_all(
        product.reshape(32, share, width), ("y", "x", "h"), split_axis=0, concat_axis=0, tiled=True
    )
    summed = jnp.sum(product.reshape(4, 8, share, width).astype(jnp.float32), axis=1)
    return summed.astype(jnp.bfloat16).transpose(1, 0, 2).reshape(share, 4 * width)


def solution(mesh):
    fine = Mesh(mesh.devices.reshape(tuple(SIZES.values())), NAMES)
    seq, head = ("y", "z", "c"), ("x", "h")
    in_specs = (
        P(seq, head, None),
        P(seq, head),
        P(None, seq),
        P(None, head, None),
        P(None, head, None),
        P(head, seq),
        P(),
        P(),
        P(seq),
    )
    return jax.shard_map(
        per_device, mesh=fine, in_specs=in_specs, out_specs=P(seq + head, None), check_vma=False
    )
```

time: 629 us -> 217 us (0.34)
  the two profiles are of different devices: /device:TPU:1 before, /device:TPU:64 now
where the time goes in v1:
time: 217 us; the launch traced here: 216 us
  blocking collectives  107 us (49%)
  starting transfers between devices  35.2 us (16%)
  Pallas kernels  32.2 us (15%)
  between operations  14.9 us (7%)
  waiting for transfers between devices  10.8 us (5%)
  other arithmetic  6.39 us (3%)
  local copies, waits for them, and re-layouts  6.09 us (3%)
  matrix products  3.2 us (1%)
    all_to_all x1, blocking collectives, per_device(): lax.all_to_all(product.reshape(32, share, width), ('y', 'x', 'h'), split_...  58.5 us
    ppermute x8, starting transfers between devices, permute(): return lax.ppermute(x, names, pairs)  35.2 us
    pallas_call x1, Pallas kernels, attend(): pl.pallas_call(kernel, grid_spec=pltpu.PrefetchScalarGridSpec(num_scalar_...  21.4 us
    all_to_all x1, blocking collectives, per_device(): lax.all_to_all(partial.reshape(8, tokens, -1), ('y', 'c'), split_axis=0,...  20.9 us
    all_gather x1, blocking collectives, per_device(): payload = lax.all_gather(payload, 'y', axis=0)  14 us
    all_gather x1, blocking collectives, per_device(): rows = lax.all_gather(values, 'y', axis=0, tiled=True)  13.7 us
    ppermute x8, waiting for transfers between devices, permute(): return lax.ppermute(x, names, pairs)  10.1 us
    pallas_call x1, Pallas kernels, latent_queries(): pl.pallas_call(query_kernel, grid=(heads,), in_specs=[pl.BlockSpec((rows,...  8.02 us
  transfers between devices with their start and end apart: 9, of which 1 were waited for; matrix products, arithmetic and copies ran while one was open for 5% of the time, Pallas kernels for 15%

profile of v1, /device:TPU:64, one launch (start us, length us, event | category | flops | bytes accessed | tf_op | source)
XLA Modules:
  0.0 215.8 jit_solution(6777759905068180136)
XLA Ops:
  6.5 0.7 all-gather.3.cloned.1.call-update
  7.3 0.9 copy.21
  8.2 1.3 fusion.6
  9.5 1.9 select_convert_fusion
  11.4 0.1 broadcast_in_dim.6
  11.5 0.9 pad_maximum_fusion.1
  12.4 14.0 %all-gather = bf16[256,1664]{1,0:T(8,128)(2,1)S(1)} all-gather(bf16[64,1664]{1,0:T(8,128)(2,1)S(1)} %pad_maximum_fusion.1), channel_id=2, replica_groups=mesh['y'=4,'z'=8,'c'=2,'x'=4,'h'=2] {'y'}, dimensions={0}, use_global_device_ids=true | all-gather | bytes 1064960 | tf_op jit(solution)/shard_map/all_gather | solution.py:264
  26.4 1.9 collective-permute-start
  28.3 3.8 %collective-permute-start.1 = (bf16[576,128]{1,0:T(8,128)(2,1)S(1)}, bf16[576,128]{1,0:T(8,128)(2,1)S(1)}, u32[]{:S(2)}, u32[]{:S(2)}) collective-permute-start(bf16[576,128]{1,0:T(8,128)(2,1)S(1)} %copy-done), channel_id=1, source_target_pairs={{0,16},{1,17},{16,32},{17,33},{32,48},{33,49},{48,64},{49,65},{64,... | collective-permute-start | bytes 442376 | tf_op jit(solution)/shard_map/ppermute | solution.py:31
  32.1 2.0 collective-permute-start.2
  34.1 7.6 %collective-permute-start.3 = (bf16[576,128]{1,0:T(8,128)(2,1)S(1)}, bf16[576,128]{1,0:T(8,128)(2,1)S(1)}, u32[]{:S(2)}, u32[]{:S(2)}) collective-permute-start(bf16[576,128]{1,0:T(8,128)(2,1)S(1)} %copy-done), channel_id=1, source_target_pairs={{0,32},{1,33},{16,48},{17,49},{32,64},{33,65},{48,80},{49,81},{64,... | collective-permute-start | bytes 442376 | tf_op jit(solution)/shard_map/ppermute | solution.py:31
  41.7 3.4 %collective-permute-start.4 = (bf16[576,128]{1,0:T(8,128)(2,1)S(1)}, bf16[576,128]{1,0:T(8,128)(2,1)S(1)}, u32[]{:S(2)}, u32[]{:S(2)}) collective-permute-start(bf16[576,128]{1,0:T(8,128)(2,1)S(1)} %copy-done), channel_id=1, source_target_pairs={{0,97},{1,96},{16,113},{17,112},{32,0},{33,1},{48,16},{49,17},{64,... | collective-permute-start | bytes 442376 | tf_op jit(solution)/shard_map/ppermute | solution.py:31
  45.1 0.0 copy-start.2
  45.1 1.3 copy.20
  47.1 1.5 copy.19
  49.3 5.0 %collective-permute-start.5 = (bf16[576,128]{1,0:T(8,128)(2,1)S(1)}, bf16[576,128]{1,0:T(8,128)(2,1)S(1)}, u32[]{:S(2)}, u32[]{:S(2)}) collective-permute-start(bf16[576,128]{1,0:T(8,128)(2,1)S(1)} %copy-done), channel_id=1, source_target_pairs={{0,48},{1,49},{16,64},{17,65},{32,80},{33,81},{48,96},{49,97},{64,... | collective-permute-start | bytes 442376 | tf_op jit(solution)/shard_map/ppermute | solution.py:31
  54.3 1.3 select_bitcast_fusion.1
  55.6 0.0 collective-permute-done.1.rest_1_
  55.6 3.9 %collective-permute-start.6 = (bf16[576,128]{1,0:T(8,128)(2,1)S(1)}, bf16[576,128]{1,0:T(8,128)(2,1)S(1)}, u32[]{:S(2)}, u32[]{:S(2)}) collective-permute-start(bf16[576,128]{1,0:T(8,128)(2,1)S(1)} %copy-done), channel_id=1, source_target_pairs={{0,81},{1,80},{16,97},{17,96},{32,113},{33,112},{48,0},{49,1},{64,... | collective-permute-start | bytes 442376 | tf_op jit(solution)/shard_map/ppermute | solution.py:31
  59.5 7.7 %collective-permute-start.7 = (bf16[576,128]{1,0:T(8,128)(2,1)S(1)}, bf16[576,128]{1,0:T(8,128)(2,1)S(1)}, u32[]{:S(2)}, u32[]{:S(2)}) collective-permute-start(bf16[576,128]{1,0:T(8,128)(2,1)S(1)} %copy-done), channel_id=1, source_target_pairs={{0,64},{1,65},{16,80},{17,81},{32,96},{33,97},{48,112},{49,113},{6... | collective-permute-start | bytes 442376 | tf_op jit(solution)/shard_map/ppermute | solution.py:31
  67.1 1.4 pad_maximum_fusion
  68.5 1.0 slice.16
  69.5 8.0 %shard_map.100.query = bf16[8,512,576]{2,1,0:T(8,128)(2,1)} custom-call(bf16[512,1664]{1,0:T(8,128)(2,1)} %bitcast.38, bf16[512,1664]{1,0:T(8,128)(2,1)} %bitcast.39, bf16[512,1024]{1,0:T(8,128)(2,1)} %bitcast.40), custom_call_target="tpu_custom_call" | custom-call | tf_op jit(solution)/shard_map/pallas_call | solution.py:60
  77.6 0.1 add_reduce_fusion.starts
  77.7 10.1 %collective-permute-done.7.rest_7_ = bf16[576,128]{1,0:T(8,128)(2,1)S(1)} collective-permute-done((bf16[576,128]{1,0:T(8,128)(2,1)S(1)}, bf16[576,128]{1,0:T(8,128)(2,1)S(1)}, u32[]{:S(2)}, u32[]{:S(2)}) %collective-permute-start.7) | collective-permute-done | bytes 147488 | tf_op jit(solution)/shard_map/ppermute | solution.py:31
  87.8 21.4 %shard_map.101 = bf16[512,1152]{1,0:T(8,128)(2,1)S(1)} custom-call(s32[16]{0:T(128)S(1)} %add_reduce_fusion.starts, s32[8]{0:T(128)S(1)} %fusion.5.bases, s32[1]{0:T(128)S(6)} %copy.23.limit_ref, bf16[8,512,576]{2,1,0:T(8,128)(2,1)} %shard_map.100.query, bf16[576,128]{1,0:T(8,128)(2,1)S(1)} %copy-done, bf16[576,128]{1,0:T(8,128)(2,1)S(1)} %collective-permute-done.1.rest_1_, ...), custom_call_target="tpu_custom_call" | custom-call | tf_op jit(solution)/shard_map/pallas_call | solution.py:179
  109.2 20.9 %all_to_all.10.parts = bf16[8,64,1152]{2,1,0:T(8,128)(2,1)} all-to-all(bf16[8,64,1152]{2,1,0:T(8,128)(2,1)S(1)} %bitcast.35), channel_id=1, replica_groups=mesh['y'=4,'z'=8,'c'=2,'x'=4,'h'=2] {'y','c'}, dimensions={0} | all-to-all | bytes 2359296 | tf_op jit(solution)/shard_map/all_to_all | solution.py:281
  130.1 2.8 %shard_map.102 = bf16[64,1024]{1,0:T(8,128)(2,1)} custom-call(bf16[8,64,1152]{2,1,0:T(8,128)(2,1)} %all_to_all.10.parts), custom_call_target="tpu_custom_call" | custom-call | tf_op jit(solution)/shard_map/pallas_call | solution.py:222
  132.9 13.7 %all_gather.14 = bf16[256,1024]{1,0:T(8,128)(2,1)S(1)} all-gather(bf16[64,1024]{1,0:T(8,128)(2,1)} %shard_map.102), channel_id=1, replica_groups=mesh['y'=4,'z'=8,'c'=2,'x'=4,'h'=2] {'y'}, dimensions={0}, use_global_device_ids=true | all-gather | bytes 655360 | tf_op jit(solution)/shard_map/all_gather | solution.py:286
  146.5 3.2 %fusion = bf16[32,8,1792]{2,1,0:T(8,128)(2,1)S(1)} fusion(bf16[256,1024]{1,0:T(8,128)(2,1)S(1)} %all_gather.14, bf16[1792,1024]{1,0:T(8,128)(2,1)} %all-gather.3.cloned.1.call-done), kind=kOutput, calls=%fused_computation.1 | convolution fusion | flops 939982848 | bytes 5111808 | tf_op jit(solution)/shard_map/dot_general | solution.py:287
  149.7 58.5 %all_to_all.11 = bf16[32,8,1792]{2,1,0:T(8,128)(2,1)S(1)} all-to-all(bf16[32,8,1792]{2,1,0:T(8,128)(2,1)S(1)} %fusion), channel_id=1, replica_groups=mesh['y'=4,'z'=8,'c'=2,'x'=4,'h'=2] {'y','x','h'}, dimensions={0} | all-to-all | bytes 1835008 | tf_op jit(solution)/shard_map/all_to_all | solution.py:292
  208.2 0.8 bitcast_reduce_fusion
  (14 shorter events, 0.0 us)
Async XLA Ops:
  6.5 21.7 %copy-start = (bf16[576,128]{1,0:T(8,128)(2,1)S(1)}, bf16[576,128]{1,0:T(8,128)(2,1)}, u32[]{:S(2)}) copy-start(bf16[576,128]{1,0:T(8,128)(2,1)} %rest_0_.1) | copy-start | bytes 442372
  6.5 38.6 %copy-start.1 = (bf16[512,8,128]{2,1,0:T(8,128)(2,1)S(1)}, bf16[512,8,128]{2,1,0:T(8,128)(2,1)}, u32[]{:S(2)}) copy-start(bf16[512,8,128]{2,1,0:T(8,128)(2,1)} %param.15) | copy-start | bytes 3145732
  6.5 140.0 %all-gather.3.cloned.1.call-start = ((), (), s32[]{:S(2)}) async-start(), calls=%async_computation.2 | async-start | bytes 3899392 | tf_op jit(solution)/shard_map/all_gather | solution.py:253
  26.4 22.9 %collective-permute-start = (bf16[4,64,1664]{2,1,0:T(8,128)(2,1)S(1)}, bf16[4,64,1664]{2,1,0:T(8,128)(2,1)}, u32[]{:S(2)}, u32[]{:S(2)}) collective-permute-start(bf16[4,64,1664]{2,1,0:T(8,128)(2,1)S(1)} %bitcast.41), channel_id=1, source_target_pairs={{0,8},{8,0},{1,9},{9,1},{2,10},{10,2},{3,11},{11,3},{4,12},{12,4},... | collective-permute-start | bytes 2555912 | tf_op jit(solution)/shard_map/ppermute | solution.py:31
  28.3 27.3 %collective-permute-start.1 = (bf16[576,128]{1,0:T(8,128)(2,1)S(1)}, bf16[576,128]{1,0:T(8,128)(2,1)S(1)}, u32[]{:S(2)}, u32[]{:S(2)}) collective-permute-start(bf16[576,128]{1,0:T(8,128)(2,1)S(1)} %copy-done), channel_id=1, source_target_pairs={{0,16},{1,17},{16,32},{17,33},{32,48},{33,49},{48,64},{49,65},{64,... | collective-permute-start | bytes 442376 | tf_op jit(solution)/shard_map/ppermute | solution.py:31
  32.1 27.4 %collective-permute-start.2 = (bf16[576,128]{1,0:T(8,128)(2,1)S(1)}, bf16[576,128]{1,0:T(8,128)(2,1)S(1)}, u32[]{:S(2)}, u32[]{:S(2)}) collective-permute-start(bf16[576,128]{1,0:T(8,128)(2,1)S(1)} %copy-done), channel_id=1, source_target_pairs={{0,113},{1,112},{16,0},{17,1},{32,16},{33,17},{48,32},{49,33},{64,... | collective-permute-start | bytes 442376 | tf_op jit(solution)/shard_map/ppermute | solution.py:31
  34.1 43.5 %collective-permute-start.3 = (bf16[576,128]{1,0:T(8,128)(2,1)S(1)}, bf16[576,128]{1,0:T(8,128)(2,1)S(1)}, u32[]{:S(2)}, u32[]{:S(2)}) collective-permute-start(bf16[576,128]{1,0:T(8,128)(2,1)S(1)} %copy-done), channel_id=1, source_target_pairs={{0,32},{1,33},{16,48},{17,49},{32,64},{33,65},{48,80},{49,81},{64,... | collective-permute-start | bytes 442376 | tf_op jit(solution)/shard_map/ppermute | solution.py:31
  41.7 35.9 %collective-permute-start.4 = (bf16[576,128]{1,0:T(8,128)(2,1)S(1)}, bf16[576,128]{1,0:T(8,128)(2,1)S(1)}, u32[]{:S(2)}, u32[]{:S(2)}) collective-permute-start(bf16[576,128]{1,0:T(8,128)(2,1)S(1)} %copy-done), channel_id=1, source_target_pairs={{0,97},{1,96},{16,113},{17,112},{32,0},{33,1},{48,16},{49,17},{64,... | collective-permute-start | bytes 442376 | tf_op jit(solution)/shard_map/ppermute | solution.py:31
  45.1 4.1 %copy-start.2 = (s32[8]{0:T(128)S(1)}, s32[8]{0:T(128)}, u32[]{:S(2)}) copy-start(s32[8]{0:T(128)} %constant.121) | copy-start | bytes 100
  49.3 28.4 %collective-permute-start.5 = (bf16[576,128]{1,0:T(8,128)(2,1)S(1)}, bf16[576,128]{1,0:T(8,128)(2,1)S(1)}, u32[]{:S(2)}, u32[]{:S(2)}) collective-permute-start(bf16[576,128]{1,0:T(8,128)(2,1)S(1)} %copy-done), channel_id=1, source_target_pairs={{0,48},{1,49},{16,64},{17,65},{32,80},{33,81},{48,96},{49,97},{64,... | collective-permute-start | bytes 442376 | tf_op jit(solution)/shard_map/ppermute | solution.py:31
  55.6 22.1 %collective-permute-start.6 = (bf16[576,128]{1,0:T(8,128)(2,1)S(1)}, bf16[576,128]{1,0:T(8,128)(2,1)S(1)}, u32[]{:S(2)}, u32[]{:S(2)}) collective-permute-start(bf16[576,128]{1,0:T(8,128)(2,1)S(1)} %copy-done), channel_id=1, source_target_pairs={{0,81},{1,80},{16,97},{17,96},{32,113},{33,112},{48,0},{49,1},{64,... | collective-permute-start | bytes 442376 | tf_op jit(solution)/shard_map/ppermute | solution.py:31
  59.5 28.3 %collective-permute-start.7 = (bf16[576,128]{1,0:T(8,128)(2,1)S(1)}, bf16[576,128]{1,0:T(8,128)(2,1)S(1)}, u32[]{:S(2)}, u32[]{:S(2)}) collective-permute-start(bf16[576,128]{1,0:T(8,128)(2,1)S(1)} %copy-done), channel_id=1, source_target_pairs={{0,64},{1,65},{16,80},{17,81},{32,96},{33,97},{48,112},{49,113},{6... | collective-permute-start | bytes 442376 | tf_op jit(solution)/shard_map/ppermute | solution.py:31
Sparse Core Ops, SparseCore 0:
  9.4 105.6 all-gather.2

commit v2 on v1

--- a/solution.py
+++ b/solution.py
@@ -13,7 +13,6 @@
 LOG2E = 1.4426950408889634
 SIZES = {"y": 4, "z": 8, "c": 2, "x": 4, "h": 2}
 NAMES = tuple(SIZES)
-SHIFTS = (1, -1, 2, -2, 3, -3, 4)
 STATS = 128
 
 
@@ -33,14 +32,41 @@
 
 def along_z(x, step):
     def move(at):
-        place = (at["h"] * 8 + at["z"] + step) % 16
-        return {"h": place // 8, "z": place % 8}
-
-    return permute(x, ("z", "h"), move)
+        place = (at["h"] * 8 + at["z"] + (step if at["c"] == 0 else -step)) % 16
+        return {"z": place % 8, "c": at["c"], "h": place // 8}
+
+    return permute(x, ("z", "c", "h"), move)
 
 
 def other_core(x):
     return permute(x, ("c",), lambda at: {"c": 1 - at["c"]})
+
+
+def to_all_y(x):
+    return lax.all_to_all(
+        jnp.broadcast_to(x[None], (4,) + x.shape), "y", split_axis=0, concat_axis=0, tiled=True
+    )
+
+
+def pack_kernel(order, content, rotary, out, *, block):
+    left = content.shape[1]
+    out[:, :left] = content[...]
+    out[:, left : left + rotary.shape[1]] = rotary[...]
+    row = lax.broadcasted_iota(jnp.int32, (out.shape[0], STATS), 0)
+    number = jnp.where(row < block, order[0], order[1])
+    out[:, left + rotary.shape[1] :] = number.astype(jnp.float32).astype(out.dtype)
+
+
+def pack(order, content, rotary, block):
+    rows = content.shape[0]
+    width = content.shape[1] + rotary.shape[1] + STATS
+    vmem = pl.BlockSpec(memory_space=pltpu.VMEM)
+    return pl.pallas_call(
+        functools.partial(pack_kernel, block=block),
+        in_specs=[pl.BlockSpec(memory_space=pltpu.SMEM), vmem, vmem],
+        out_specs=vmem,
+        out_shape=jax.ShapeDtypeStruct((rows, width), jnp.bfloat16),
+    )(order, content, rotary)
 
 
 def query_kernel(content, rotary, key_up, out):
@@ -73,10 +99,10 @@
 def attend_kernel(
     starts, bases, limit_ref, query, *rest, shards, coef, latent, block, heads, groups
 ):
-    keys, value_up, out, mixed = rest[:shards], rest[shards], rest[shards + 1], rest[shards + 2]
+    *keys, value_up, out, mixed = rest
     group = pl.program_id(0)
     rows = heads * block
-    width = keys[0].shape[1]
+    width = keys[0].shape[2]
     limit = limit_ref[0]
     lowest, highest = bases[0], bases[0]
     for i in range(1, shards):
@@ -103,7 +129,7 @@
 
     def run(half, masked):
         rows_q = query[:, half * block : (half + 1) * block, :].reshape(rows, -1)
-        k = jnp.concatenate([r[...] for r in keys], axis=1)
+        k = jnp.concatenate([r[i] for r in keys for i in range(r.shape[0])], axis=1)
         s = jnp.dot(rows_q, k, preferred_element_type=jnp.float32)
         if masked:
             token = lax.broadcasted_iota(jnp.int32, (rows, width), 0) % block
@@ -163,10 +189,10 @@
 def attend(starts, bases, limit, query, keys, value_up, scale):
     heads, tokens, depth = query.shape
     latent, value_width = value_up.shape
-    shards = len(keys)
+    shards = sum(k.shape[0] for k in keys)
     groups = starts.shape[0] // 2
     per_group = tokens // groups
-    whole = lambda shape: pl.BlockSpec(shape, lambda i, *_: (0, 0))
+    whole = lambda shape: pl.BlockSpec(shape, lambda i, *_: (0,) * len(shape))
     kernel = functools.partial(
         attend_kernel,
         shards=shards,
@@ -244,28 +270,23 @@
     block = tokens // 2
     scale = 1.0 / math.sqrt(nope + rope)
     shard = key_cache.shape[1]
-    y, z, c = lax.axis_index("y"), lax.axis_index("z"), lax.axis_index("c")
-
-    shards = [key_cache] + [along_z(key_cache, s) for s in SHIFTS]
-    offsets = jnp.array((0,) + SHIFTS, jnp.int32)
-    bases = ((y * 8 + (z - offsets) % 8) * 2 + c).astype(jnp.int32) * shard
-
-    weight = lax.all_gather(output_weight.T, ("z", "c"), axis=0, tiled=True)
-
-    numbers = jnp.repeat(block_order, block, total_repeat_length=tokens).astype(jnp.bfloat16)
-    payload = jnp.concatenate(
-        [
-            query_content.reshape(tokens, heads * nope),
-            query_rotary,
-            jnp.broadcast_to(numbers[:, None], (tokens, STATS)),
-        ],
-        axis=1,
-    )
-    payload = lax.all_gather(payload, "y", axis=0)
-    partner = other_core(payload)
-    first = jnp.where(c == 0, payload, partner)
-    second = jnp.where(c == 0, partner, payload)
-    payload = jnp.stack([first, second], axis=1).reshape(8 * tokens, -1)
+    y, z, c, h = (lax.axis_index(n) for n in ("y", "z", "c", "h"))
+
+    pair = jnp.stack([key_cache, other_core(key_cache)])
+    fetched = jnp.concatenate(
+        [along_z(pair, s) for s in (1, 2, 3)] + [along_z(key_cache, 4)[None]], axis=0
+    )
+    keys = [pair, fetched, other_core(fetched)]
+    side = 1 - 2 * c
+    steps = np.array([0, 0, 1, 1, 2, 2, 3, 3, 4, -1, -1, -2, -2, -3, -3, -4], np.int32)
+    cores = np.array([0, 1, 0, 1, 0, 1, 0, 1, 0, 1, 0, 1, 0, 1, 0, 1], np.int32)
+    bases = ((y * 8 + (z - side * steps) % 8) * 2 + (c + cores) % 2).astype(jnp.int32) * shard
+
+    weight = lax.all_gather(output_weight.T, "z", axis=0, tiled=True)
+    weights = [weight, other_core(weight)]
+
+    payload = pack(block_order, query_content.reshape(tokens, heads * nope), query_rotary, block)
+    payload = to_all_y(payload).reshape(4 * tokens, -1)
     starts = query_start[0] + payload[::block, -1].astype(jnp.int32) * block
 
     queries = latent_queries(payload, key_up.reshape(latent, heads * nope), heads, nope, rope)
@@ -274,26 +295,38 @@
         bases,
         key_limit,
         queries,
-        shards,
+        keys,
         value_up.reshape(latent, heads * value_dim),
         scale,
     )
     partial = lax.all_to_all(
-        partial.reshape(8, tokens, -1), ("y", "c"), split_axis=0, concat_axis=0, tiled=True
+        partial.reshape(4, tokens, -1), "y", split_axis=0, concat_axis=0, tiled=True
     )
     values = merge(partial, heads)
 
-    rows = lax.all_gather(values, "y", axis=0, tiled=True)
-    product = lax.dot_general(
-        rows, weight, (((1,), (1,)), ((), ())), preferred_element_type=jnp.float32
-    ).astype(jnp.bfloat16)
+    rows = to_all_y(values).reshape(4 * tokens, -1)
+    product = jnp.concatenate(
+        [
+            lax.dot_general(
+                rows, w, (((1,), (1,)), ((), ())), preferred_element_type=jnp.float32
+            ).astype(jnp.bfloat16)
+            for w in weights
+        ],
+        axis=1,
+    )
     share = tokens // 8
     width = 16 * columns
     product = lax.all_to_all(
-        product.reshape(32, share, width), ("y", "x", "h"), split_axis=0, concat_axis=0, tiled=True
-    )
-    summed = jnp.sum(product.reshape(4, 8, share, width).astype(jnp.float32), axis=1)
-    return summed.astype(jnp.bfloat16).transpose(1, 0, 2).reshape(share, 4 * width)
+        product.reshape(16, 2 * share, width), ("y", "x"), split_axis=0, concat_axis=0, tiled=True
+    )
+    summed = jnp.sum(product.reshape(4, 4, 2, share, width).astype(jnp.float32), axis=1)
+    mine = jnp.where(h == 0, summed[:, 0], summed[:, 1])
+    theirs = jnp.where(h == 0, summed[:, 1], summed[:, 0]).astype(jnp.bfloat16)
+    got = permute(theirs, ("h",), lambda at: {"h": 1 - at["h"]})
+    total = (mine + got.astype(jnp.float32)).astype(jnp.bfloat16)
+    total = total.reshape(4, share, 2, 8, columns)
+    total = jnp.where(c == 0, total, total[:, :, ::-1])
+    return total.transpose(1, 0, 3, 2, 4).reshape(share, 4 * width)
 
 
 def solution(mesh):

time: 217 us -> 204 us (0.940)
  the two profiles are of different devices: /device:TPU:64 before, /device:TPU:2 now
where the time goes in v2:
time: 204 us; the launch traced here: 203 us
  waiting for transfers between devices  68.8 us (34%)
  starting transfers between devices  50.6 us (25%)
  Pallas kernels  28.6 us (14%)
  blocking collectives  27.1 us (13%)
  between operations  15.1 us (7%)
  local copies, waits for them, and re-layouts  7.21 us (4%)
  matrix products  2.98 us (1%)
  other arithmetic  2.43 us (1%)
    ppermute x8, starting transfers between devices, permute(): return lax.ppermute(x, names, pairs)  40.7 us
    ppermute x8, waiting for transfers between devices, permute(): return lax.ppermute(x, names, pairs)  38.7 us
    pallas_call x1, Pallas kernels, attend(): pl.pallas_call(kernel, grid_spec=pltpu.PrefetchScalarGridSpec(num_scalar_...  18.2 us
    all_gather x1, waiting for transfers between devices, per_device(): weight = lax.all_gather(output_weight.T, 'z', axis=0, tiled=True)  15.5 us
    all_to_all x1, blocking collectives, per_device(): lax.all_to_all(partial.reshape(4, tokens, -1), 'y', split_axis=0, concat_...  14.7 us
    all_to_all x1, waiting for transfers between devices, per_device(): lax.all_to_all(product.reshape(16, 2 * share, width), ('y', 'x'), split_a...  13.8 us
    all_to_all x1, blocking collectives, to_all_y(): lax.all_to_all(jnp.broadcast_to(x[None], (4,) + x.shape), 'y', split_axis...  12.4 us
    pallas_call x1, Pallas kernels, latent_queries(): pl.pallas_call(query_kernel, grid=(heads,), in_specs=[pl.BlockSpec((rows,...  6.56 us
  transfers between devices with their start and end apart: 11, of which 5 were waited for; matrix products, arithmetic and copies ran while one was open for 4% of the time, Pallas kernels for 14%

profile of v2, /device:TPU:2, one launch (start us, length us, event | category | flops | bytes accessed | tf_op | source)
XLA Modules:
  0.0 202.7 jit_solution(14208430124042322754)
XLA Ops:
  6.5 0.7 all-gather.2.cloned.1.call-update
  7.3 1.9 collective-permute-start
  9.2 1.5 collective-permute-done
  10.7 0.9 pad_maximum_fusion.2.rest_0_
  11.7 6.5 %collective-permute-start.3 = (bf16[2,576,128]{2,1,0:T(8,128)(2,1)S(1)}, bf16[2,576,128]{2,1,0:T(8,128)(2,1)S(1)}, u32[]{:S(2)}, u32[]{:S(2)}) collective-permute-start(bf16[2,576,128]{2,1,0:T(8,128)(2,1)S(1)} %pad_maximum_fusion.2.rest_0_), channel_id=1, source_target_pairs={{0,48},{1,49},{8,89},{9,88},{16,64},{17,65},{24,105},{25,104},{32,... | collective-permute-start | bytes 884744 | tf_op jit(solution)/shard_map/ppermute | solution.py:30
  18.2 6.4 %collective-permute-start.2 = (bf16[2,576,128]{2,1,0:T(8,128)(2,1)S(1)}, bf16[2,576,128]{2,1,0:T(8,128)(2,1)S(1)}, u32[]{:S(2)}, u32[]{:S(2)}) collective-permute-start(bf16[2,576,128]{2,1,0:T(8,128)(2,1)S(1)} %pad_maximum_fusion.2.rest_0_), channel_id=1, source_target_pairs={{0,32},{1,33},{8,105},{9,104},{16,48},{17,49},{24,121},{25,120},{3... | collective-permute-start | bytes 884744 | tf_op jit(solution)/shard_map/ppermute | solution.py:30
  24.6 3.8 %collective-permute-start.1 = (bf16[2,576,128]{2,1,0:T(8,128)(2,1)S(1)}, bf16[2,576,128]{2,1,0:T(8,128)(2,1)S(1)}, u32[]{:S(2)}, u32[]{:S(2)}) collective-permute-start(bf16[2,576,128]{2,1,0:T(8,128)(2,1)S(1)} %pad_maximum_fusion.2.rest_0_), channel_id=1, source_target_pairs={{0,16},{1,17},{8,121},{9,120},{16,32},{17,33},{24,8},{25,9},{32,48... | collective-permute-start | bytes 884744 | tf_op jit(solution)/shard_map/ppermute | solution.py:30
  28.4 7.3 %collective-permute-start.4 = (bf16[576,128]{1,0:T(8,128)(2,1)}, bf16[576,128]{1,0:T(8,128)(2,1)S(1)}, u32[]{:S(2)}, u32[]{:S(2)}) collective-permute-start(bf16[576,128]{1,0:T(8,128)(2,1)} %param.13), channel_id=1, source_target_pairs={{0,64},{1,65},{8,73},{9,72},{16,80},{17,81},{24,89},{25,88},{32,96... | collective-permute-start | bytes 442376 | tf_op jit(solution)/shard_map/ppermute | solution.py:30
  35.8 29.7 %collective-permute-done.4 = bf16[576,128]{1,0:T(8,128)(2,1)S(1)} collective-permute-done((bf16[576,128]{1,0:T(8,128)(2,1)}, bf16[576,128]{1,0:T(8,128)(2,1)S(1)}, u32[]{:S(2)}, u32[]{:S(2)}) %collective-permute-start.4) | collective-permute-done | bytes 147488 | tf_op jit(solution)/shard_map/ppermute | solution.py:30
  65.7 2.1 %collective-permute-start.5 = (bf16[7,576,128]{2,1,0:T(8,128)(2,1)S(1)}, bf16[7,576,128]{2,1,0:T(8,128)(2,1)S(1)}, u32[]{:S(2)}, u32[]{:S(2)}) collective-permute-start(bf16[7,576,128]{2,1,0:T(8,128)(2,1)S(1)} %pad_maximum_fusion.rest_1_), channel_id=1, source_target_pairs={{0,8},{8,0},{1,9},{9,1},{2,10},{10,2},{3,11},{11,3},{4,12},{12,4},... | collective-permute-start | bytes 3096584 | tf_op jit(solution)/shard_map/ppermute | solution.py:30
  67.7 0.7 copy.30
  68.4 1.6 shard_map.109
  70.0 1.9 broadcast_in_dim.6
  71.9 4.2 %all-to-all-start = ((bf16[4,64,1664]{2,1,0:T(8,128)(2,1)}), bf16[4,64,1664]{2,1,0:T(8,128)(2,1)}, u32[]{:S(2)}, u32[]{:S(2)}) async-start(bf16[4,64,1664]{2,1,0:T(8,128)(2,1)} %broadcast_in_dim.6), calls=%async_computation | async-start | bytes 1703936 | tf_op jit(solution)/shard_map/all_to_all | solution.py:46
  76.2 15.5 %all-gather.2.cloned.1.call-done = bf16[896,1024]{1,0:T(8,128)(2,1)} async-done(((bf16[112,1024]{1,0:T(8,128)(2,1)}), bf16[896,1024]{1,0:T(8,128)(2,1)}) %all-gather.2.cloned.1.call-update) | async-done | bytes 1835024 | tf_op jit(solution)/shard_map/all_gather | solution.py:285
  91.7 1.9 collective-permute-start.6
  95.1 1.3 copy.29
  96.7 0.9 slice.11
  97.6 6.6 %shard_map.110.query = bf16[8,256,576]{2,1,0:T(8,128)(2,1)} custom-call(bf16[256,1664]{1,0:T(8,128)(2,1)} %bitcast.1.content.rotary, bf16[256,1664]{1,0:T(8,128)(2,1)} %bitcast.1.content.rotary, bf16[512,1024]{1,0:T(8,128)(2,1)} %bitcast.56), custom_call_target="tpu_custom_call" | custom-call | tf_op jit(solution)/shard_map/pallas_call | solution.py:86
  104.3 18.2 %shard_map.111 = bf16[256,1152]{1,0:T(8,128)(2,1)S(1)} custom-call(s32[8]{0:T(128)S(1)} %add_reduce_fusion.starts, s32[16]{0:T(128)S(1)} %fusion.7.bases, s32[1]{0:T(128)S(6)} %copy.32.limit_ref, bf16[8,256,576]{2,1,0:T(8,128)(2,1)} %shard_map.110.query, bf16[2,576,128]{2,1,0:T(8,128)(2,1)S(1)} %pad_maximum_fusion.2.rest_0_, ...), custom_call_target="tpu_custom_call" | custom-call | tf_op jit(solution)/shard_map/pallas_call | solution.py:205
  122.5 14.7 %all_to_all.20.parts = bf16[4,64,1152]{2,1,0:T(8,128)(2,1)} all-to-all(bf16[4,64,1152]{2,1,0:T(8,128)(2,1)S(1)} %bitcast.55), channel_id=1, replica_groups=mesh['y'=4,'z'=8,'c'=2,'x'=4,'h'=2] {'y'}, dimensions={0} | all-to-all | bytes 1179648 | tf_op jit(solution)/shard_map/all_to_all | solution.py:302
  137.2 2.2 %shard_map.112 = bf16[64,1024]{1,0:T(8,128)(2,1)} custom-call(bf16[4,64,1152]{2,1,0:T(8,128)(2,1)} %all_to_all.20.parts), custom_call_target="tpu_custom_call" | custom-call | tf_op jit(solution)/shard_map/pallas_call | solution.py:248
  139.4 1.0 broadcast_in_dim.8
  140.4 12.4 %all_to_all.21 = bf16[4,64,1024]{2,1,0:T(8,128)(2,1)S(1)} all-to-all(bf16[4,64,1024]{2,1,0:T(8,128)(2,1)S(1)} %broadcast_in_dim.8), channel_id=1, replica_groups=mesh['y'=4,'z'=8,'c'=2,'x'=4,'h'=2] {'y'}, dimensions={0} | all-to-all | bytes 1048576 | tf_op jit(solution)/shard_map/all_to_all | solution.py:46
  152.8 0.7 convolution_convert_fusion.1
  153.6 2.2 %convolution_convert_fusion = bf16[256,896]{1,0:T(8,128)(2,1)S(1)} fusion(bf16[256,1024]{1,0:T(8,128)(2,1)S(1)} %bitcast.61, bf16[896,1024]{1,0:T(8,128)(2,1)} %collective-permute-done.6), kind=kOutput, calls=%fused_computation.1 | convolution fusion | flops 469991424 | bytes 2818048 | tf_op jit(solution)/shard_map/dot_general | solution.py:310
  155.8 1.0 pad_maximum_fusion.1
  156.8 5.7 %all-to-all-start.3 = ((bf16[16,16,1792]{2,1,0:T(8,128)(2,1)}), bf16[16,16,1792]{2,1,0:T(8,128)(2,1)S(1)}, u32[]{:S(2)}, u32[]{:S(2)}) async-start(bf16[16,16,1792]{2,1,0:T(8,128)(2,1)} %bitcast.8), calls=%async_computation.3 | async-start | bytes 1835008 | tf_op jit(solution)/shard_map/all_to_all | solution.py:319
  162.5 13.8 %all-to-all-done.3 = bf16[16,16,1792]{2,1,0:T(8,128)(2,1)S(1)} async-done(((bf16[16,16,1792]{2,1,0:T(8,128)(2,1)}), bf16[16,16,1792]{2,1,0:T(8,128)(2,1)S(1)}, u32[]{:S(2)}, u32[]{:S(2)}) %all-to-all-start.3) | async-done | bytes 917536 | tf_op jit(solution)/shard_map/all_to_all | solution.py:319
  176.5 10.7 %collective-permute-start.7 = (bf16[4,8,1792]{2,1,0:T(8,128)(2,1)S(1)}, bf16[4,8,1792]{2,1,0:T(8,128)(2,1)S(1)}, u32[]{:S(2)}, u32[]{:S(2)}) collective-permute-start(bf16[4,8,1792]{2,1,0:T(8,128)(2,1)S(1)} %fusion.4), channel_id=1, source_target_pairs={{0,1},{1,0},{2,3},{3,2},{4,5},{5,4},{6,7},{7,6},{8,9},{9,8},{10,11... | collective-permute-start | bytes 344072 | tf_op jit(solution)/shard_map/ppermute | solution.py:30
  187.2 7.4 %collective-permute-done.7 = bf16[4,8,1792]{2,1,0:T(8,128)(2,1)S(1)} collective-permute-done((bf16[4,8,1792]{2,1,0:T(8,128)(2,1)S(1)}, bf16[4,8,1792]{2,1,0:T(8,128)(2,1)S(1)}, u32[]{:S(2)}, u32[]{:S(2)}) %collective-permute-start.7) | collective-permute-done | bytes 114720 | tf_op jit(solution)/shard_map/ppermute | solution.py:30
  195.0 0.8 reshape.50
  (29 shorter events, 1.1 us)
Async XLA Ops:
  6.5 61.2 %copy-start.2 = (bf16[64,8,128]{2,1,0:T(8,128)(2,1)S(1)}, bf16[64,8,128]{2,1,0:T(8,128)(2,1)}, u32[]{:S(2)}) copy-start(bf16[64,8,128]{2,1,0:T(8,128)(2,1)} %param.11) | copy-start | bytes 393220
  6.5 85.2 %all-gather.2.cloned.1.call-start = ((), (), s32[]{:S(2)}) async-start(), calls=%async_computation.4 | async-start | bytes 2064384 | tf_op jit(solution)/shard_map/all_gather | solution.py:285
  7.3 3.5 %collective-permute-start = (bf16[576,128]{1,0:T(8,128)(2,1)}, bf16[576,128]{1,0:T(8,128)(2,1)S(1)}, u32[]{:S(2)}, u32[]{:S(2)}) collective-permute-start(bf16[576,128]{1,0:T(8,128)(2,1)} %param.13), channel_id=1, source_target_pairs={{0,8},{8,0},{1,9},{9,1},{2,10},{10,2},{3,11},{11,3},{4,12},{12,4},... | collective-permute-start | bytes 442376 | tf_op jit(solution)/shard_map/ppermute | solution.py:30
  11.7 53.8 %collective-permute-start.3 = (bf16[2,576,128]{2,1,0:T(8,128)(2,1)S(1)}, bf16[2,576,128]{2,1,0:T(8,128)(2,1)S(1)}, u32[]{:S(2)}, u32[]{:S(2)}) collective-permute-start(bf16[2,576,128]{2,1,0:T(8,128)(2,1)S(1)} %pad_maximum_fusion.2.rest_0_), channel_id=1, source_target_pairs={{0,48},{1,49},{8,89},{9,88},{16,64},{17,65},{24,105},{25,104},{32,... | collective-permute-start | bytes 884744 | tf_op jit(solution)/shard_map/ppermute | solution.py:30
  18.2 47.3 %collective-permute-start.2 = (bf16[2,576,128]{2,1,0:T(8,128)(2,1)S(1)}, bf16[2,576,128]{2,1,0:T(8,128)(2,1)S(1)}, u32[]{:S(2)}, u32[]{:S(2)}) collective-permute-start(bf16[2,576,128]{2,1,0:T(8,128)(2,1)S(1)} %pad_maximum_fusion.2.rest_0_), channel_id=1, source_target_pairs={{0,32},{1,33},{8,105},{9,104},{16,48},{17,49},{24,121},{25,120},{3... | collective-permute-start | bytes 884744 | tf_op jit(solution)/shard_map/ppermute | solution.py:30
  24.6 40.9 %collective-permute-start.1 = (bf16[2,576,128]{2,1,0:T(8,128)(2,1)S(1)}, bf16[2,576,128]{2,1,0:T(8,128)(2,1)S(1)}, u32[]{:S(2)}, u32[]{:S(2)}) collective-permute-start(bf16[2,576,128]{2,1,0:T(8,128)(2,1)S(1)} %pad_maximum_fusion.2.rest_0_), channel_id=1, source_target_pairs={{0,16},{1,17},{8,121},{9,120},{16,32},{17,33},{24,8},{25,9},{32,48... | collective-permute-start | bytes 884744 | tf_op jit(solution)/shard_map/ppermute | solution.py:30
  28.4 37.0 %collective-permute-start.4 = (bf16[576,128]{1,0:T(8,128)(2,1)}, bf16[576,128]{1,0:T(8,128)(2,1)S(1)}, u32[]{:S(2)}, u32[]{:S(2)}) collective-permute-start(bf16[576,128]{1,0:T(8,128)(2,1)} %param.13), channel_id=1, source_target_pairs={{0,64},{1,65},{8,73},{9,72},{16,80},{17,81},{24,89},{25,88},{32,96... | collective-permute-start | bytes 442376 | tf_op jit(solution)/shard_map/ppermute | solution.py:30
  65.6 29.4 %copy-start = (bf16[512,8,128]{2,1,0:T(8,128)(2,1)S(1)}, bf16[512,8,128]{2,1,0:T(8,128)(2,1)}, u32[]{:S(2)}) copy-start(bf16[512,8,128]{2,1,0:T(8,128)(2,1)} %param.14) | copy-start | bytes 3145732
  65.7 38.7 %collective-permute-start.5 = (bf16[7,576,128]{2,1,0:T(8,128)(2,1)S(1)}, bf16[7,576,128]{2,1,0:T(8,128)(2,1)S(1)}, u32[]{:S(2)}, u32[]{:S(2)}) collective-permute-start(bf16[7,576,128]{2,1,0:T(8,128)(2,1)S(1)} %pad_maximum_fusion.rest_1_), channel_id=1, source_target_pairs={{0,8},{8,0},{1,9},{9,1},{2,10},{10,2},{3,11},{11,3},{4,12},{12,4},... | collective-permute-start | bytes 3096584 | tf_op jit(solution)/shard_map/ppermute | solution.py:30
  71.9 24.8 %all-to-all-start = ((bf16[4,64,1664]{2,1,0:T(8,128)(2,1)}), bf16[4,64,1664]{2,1,0:T(8,128)(2,1)}, u32[]{:S(2)}, u32[]{:S(2)}) async-start(bf16[4,64,1664]{2,1,0:T(8,128)(2,1)} %broadcast_in_dim.6), calls=%async_computation | async-start | bytes 1703936 | tf_op jit(solution)/shard_map/all_to_all | solution.py:46
  91.7 61.8 %collective-permute-start.6 = (bf16[896,1024]{1,0:T(8,128)(2,1)}, bf16[896,1024]{1,0:T(8,128)(2,1)}, u32[]{:S(2)}, u32[]{:S(2)}) collective-permute-start(bf16[896,1024]{1,0:T(8,128)(2,1)} %all-gather.2.cloned.1.call-done), channel_id=1, source_target_pairs={{0,8},{8,0},{1,9},{9,1},{2,10},{10,2},{3,11},{11,3},{4,12},{12,4},... | collective-permute-start | bytes 5505032 | tf_op jit(solution)/shard_map/ppermute | solution.py:30
  94.3 2.1 %copy-start.1 = (bf16[512,8,128]{2,1,0:T(8,128)(2,1)S(1)}, bf16[512,8,128]{2,1,0:T(8,128)(2,1)}, u32[]{:S(2)}) copy-start(bf16[512,8,128]{2,1,0:T(8,128)(2,1)} %param.15) | copy-start | bytes 3145732
  95.1 1.6 copy-start.3
  95.1 1.6 copy-start.4
  122.5 30.3 %copy-start.5 = (bf16[896,1024]{1,0:T(8,128)(2,1)S(1)}, bf16[896,1024]{1,0:T(8,128)(2,1)}, u32[]{:S(2)}) copy-start(bf16[896,1024]{1,0:T(8,128)(2,1)} %all-gather.2.cloned.1.call-done) | copy-start | bytes 5505028
  156.8 19.5 %all-to-all-start.3 = ((bf16[16,16,1792]{2,1,0:T(8,128)(2,1)}), bf16[16,16,1792]{2,1,0:T(8,128)(2,1)S(1)}, u32[]{:S(2)}, u32[]{:S(2)}) async-start(bf16[16,16,1792]{2,1,0:T(8,128)(2,1)} %bitcast.8), calls=%async_computation.3 | async-start | bytes 1835008 | tf_op jit(solution)/shard_map/all_to_all | solution.py:319
  176.5 18.1 %collective-permute-start.7 = (bf16[4,8,1792]{2,1,0:T(8,128)(2,1)S(1)}, bf16[4,8,1792]{2,1,0:T(8,128)(2,1)S(1)}, u32[]{:S(2)}, u32[]{:S(2)}) collective-permute-start(bf16[4,8,1792]{2,1,0:T(8,128)(2,1)S(1)} %fusion.4), channel_id=1, source_target_pairs={{0,1},{1,0},{2,3},{3,2},{4,5},{5,4},{6,7},{7,6},{8,9},{9,8},{10,11... | collective-permute-start | bytes 344072 | tf_op jit(solution)/shard_map/ppermute | solution.py:30
Sparse Core Ops, SparseCore 0:
  9.4 82.2 all-gather.1

commit v3 on v2

--- a/solution.py
+++ b/solution.py
@@ -93,6 +93,9 @@
         ],
         out_specs=pl.BlockSpec((1, rows, latent + rope), lambda i: (i, 0, 0)),
         out_shape=jax.ShapeDtypeStruct((heads, rows, latent + rope), jnp.bfloat16),
+        cost_estimate=pl.CostEstimate(
+            flops=2 * heads * rows * latent * nope, bytes_accessed=8 * 1024 * 1024, transcendentals=0
+        ),
     )(payload, payload, key_up)
 
 
@@ -272,24 +275,25 @@
     shard = key_cache.shape[1]
     y, z, c, h = (lax.axis_index(n) for n in ("y", "z", "c", "h"))
 
+    weight = lax.all_gather(output_weight.T, "z", axis=0, tiled=True)
+
+    payload = pack(block_order, query_content.reshape(tokens, heads * nope), query_rotary, block)
+
     pair = jnp.stack([key_cache, other_core(key_cache)])
-    fetched = jnp.concatenate(
-        [along_z(pair, s) for s in (1, 2, 3)] + [along_z(key_cache, 4)[None]], axis=0
-    )
+    payload, pair = lax.optimization_barrier((payload, pair))
+    one, two = along_z(pair, 1), along_z(pair, 2)
+    payload = to_all_y(payload).reshape(4 * tokens, -1)
+    starts = query_start[0] + payload[::block, -1].astype(jnp.int32) * block
+    queries = latent_queries(payload, key_up.reshape(latent, heads * nope), heads, nope, rope)
+    queries, one, two = lax.optimization_barrier((queries, one, two))
+    three, four = along_z(two, 1), along_z(two[:1], 2)
+    fetched = jnp.concatenate([one, two, three, four], axis=0)
     keys = [pair, fetched, other_core(fetched)]
     side = 1 - 2 * c
     steps = np.array([0, 0, 1, 1, 2, 2, 3, 3, 4, -1, -1, -2, -2, -3, -3, -4], np.int32)
     cores = np.array([0, 1, 0, 1, 0, 1, 0, 1, 0, 1, 0, 1, 0, 1, 0, 1], np.int32)
     bases = ((y * 8 + (z - side * steps) % 8) * 2 + (c + cores) % 2).astype(jnp.int32) * shard
 
-    weight = lax.all_gather(output_weight.T, "z", axis=0, tiled=True)
-    weights = [weight, other_core(weight)]
-
-    payload = pack(block_order, query_content.reshape(tokens, heads * nope), query_rotary, block)
-    payload = to_all_y(payload).reshape(4 * tokens, -1)
-    starts = query_start[0] + payload[::block, -1].astype(jnp.int32) * block
-
-    queries = latent_queries(payload, key_up.reshape(latent, heads * nope), heads, nope, rope)
     partial = attend(
         starts,
         bases,
@@ -303,6 +307,8 @@
         partial.reshape(4, tokens, -1), "y", split_axis=0, concat_axis=0, tiled=True
     )
     values = merge(partial, heads)
+    values, weight = lax.optimization_barrier((values, weight))
+    weights = [weight, other_core(weight)]
 
     rows = to_all_y(values).reshape(4 * tokens, -1)
     product = jnp.concatenate(

time: 204 us -> 186 us (0.912)
  the two profiles are of different devices: /device:TPU:2 before, /device:TPU:32 now
where the time goes in v3:
time: 186 us; the launch traced here: 185 us
  starting transfers between devices  58.2 us (31%)
  waiting for transfers between devices  38 us (20%)
  blocking collectives  29.2 us (16%)
  Pallas kernels  28.7 us (15%)
  between operations  15 us (8%)
  local copies, waits for them, and re-layouts  10.4 us (6%)
  matrix products  2.98 us (2%)
  other arithmetic  2.28 us (1%)
    ppermute x8, starting transfers between devices, permute(): return lax.ppermute(x, names, pairs)  48.7 us
    ppermute x8, waiting for transfers between devices, permute(): return lax.ppermute(x, names, pairs)  19.7 us
    pallas_call x1, Pallas kernels, attend(): pl.pallas_call(kernel, grid_spec=pltpu.PrefetchScalarGridSpec(num_scalar_...  18.2 us
    all_to_all x1, blocking collectives, per_device(): lax.all_to_all(partial.reshape(4, tokens, -1), 'y', split_axis=0, concat_...  16.4 us
    all_to_all x1, waiting for transfers between devices, per_device(): lax.all_to_all(product.reshape(16, 2 * share, width), ('y', 'x'), split_a...  15.5 us
    all_to_all x1, blocking collectives, to_all_y(): lax.all_to_all(jnp.broadcast_to(x[None], (4,) + x.shape), 'y', split_axis...  12.8 us
    pallas_call x1, Pallas kernels, latent_queries(): pl.pallas_call(query_kernel, grid=(heads,), in_specs=[pl.BlockSpec((rows,...  6.54 us
    unnamed x14, local copies, waits for them, and re-layouts  5.39 us
  transfers between devices with their start and end apart: 11, of which 6 were waited for; matrix products, arithmetic and copies ran while one was open for 6% of the time, Pallas kernels for 16%

profile of v3, /device:TPU:32, one launch (start us, length us, event | category | flops | bytes accessed | tf_op | source)
XLA Modules:
  0.0 184.7 jit_solution(5095033898766168236)
XLA Ops:
  7.3 1.9 %collective-permute-start = (bf16[576,128]{1,0:T(8,128)(2,1)}, bf16[576,128]{1,0:T(8,128)(2,1)S(1)}, u32[]{:S(2)}, u32[]{:S(2)}) collective-permute-start(bf16[576,128]{1,0:T(8,128)(2,1)} %param.13), channel_id=1, source_target_pairs={{0,8},{8,0},{1,9},{9,1},{2,10},{10,2},{3,11},{11,3},{4,12},{12,4},... | collective-permute-start | bytes 442376 | tf_op jit(solution)/shard_map/ppermute | solution.py:30
  9.2 1.6 copy.30
  10.8 1.7 shard_map.109
  12.5 0.9 pad_maximum_fusion.1.rest_0_
  13.4 1.9 %broadcast_in_dim.4 = bf16[4,64,1664]{2,1,0:T(8,128)(2,1)} broadcast(bf16[64,1664]{1,0:T(8,128)(2,1)} %shard_map.109), dimensions={1,2} | broadcast | bytes 1064960 | tf_op jit(solution)/shard_map/broadcast_in_dim | solution.py:47
  15.3 4.5 %all-to-all-start = ((bf16[4,64,1664]{2,1,0:T(8,128)(2,1)}), bf16[4,64,1664]{2,1,0:T(8,128)(2,1)S(1)}, u32[]{:S(2)}, u32[]{:S(2)}) async-start(bf16[4,64,1664]{2,1,0:T(8,128)(2,1)} %broadcast_in_dim.4), calls=%async_computation | async-start | bytes 1703936 | tf_op jit(solution)/shard_map/all_to_all | solution.py:46
  19.8 3.8 %collective-permute-start.1 = (bf16[2,576,128]{2,1,0:T(8,128)(2,1)S(1)}, bf16[2,576,128]{2,1,0:T(8,128)(2,1)S(1)}, u32[]{:S(2)}, u32[]{:S(2)}) collective-permute-start(bf16[2,576,128]{2,1,0:T(8,128)(2,1)S(1)} %pad_maximum_fusion.1.rest_0_), channel_id=1, source_target_pairs={{0,16},{1,17},{8,121},{9,120},{16,32},{17,33},{24,8},{25,9},{32,48... | collective-permute-start | bytes 884744 | tf_op jit(solution)/shard_map/ppermute | solution.py:30
  23.6 6.4 %collective-permute-start.2 = (bf16[2,576,128]{2,1,0:T(8,128)(2,1)S(1)}, bf16[2,576,128]{2,1,0:T(8,128)(2,1)S(1)}, u32[]{:S(2)}, u32[]{:S(2)}) collective-permute-start(bf16[2,576,128]{2,1,0:T(8,128)(2,1)S(1)} %pad_maximum_fusion.1.rest_0_), channel_id=1, source_target_pairs={{0,32},{1,33},{8,105},{9,104},{16,48},{17,49},{24,121},{25,120},{3... | collective-permute-start | bytes 884744 | tf_op jit(solution)/shard_map/ppermute | solution.py:30
  30.0 1.3 copy.29
  31.3 2.1 %all-to-all-done = bf16[4,64,1664]{2,1,0:T(8,128)(2,1)S(1)} async-done(((bf16[4,64,1664]{2,1,0:T(8,128)(2,1)}), bf16[4,64,1664]{2,1,0:T(8,128)(2,1)S(1)}, u32[]{:S(2)}, u32[]{:S(2)}) %all-to-all-start) | async-done | bytes 852000 | tf_op jit(solution)/shard_map/all_to_all | solution.py:46
  33.5 0.9 copy-done
  34.4 6.5 %shard_map.110.query = bf16[8,256,576]{2,1,0:T(8,128)(2,1)} custom-call(bf16[256,1664]{1,0:T(8,128)(2,1)} %bitcast.55, bf16[256,1664]{1,0:T(8,128)(2,1)} %bitcast.56, bf16[512,1024]{1,0:T(8,128)(2,1)} %bitcast.58), custom_call_target="tpu_custom_call" | custom-call | flops 268435456 | bytes 8388608 | tf_op jit(solution)/shard_map/pallas_call | solution.py:86
  40.9 3.2 %collective-permute-done.2 = bf16[2,576,128]{2,1,0:T(8,128)(2,1)S(1)} collective-permute-done((bf16[2,576,128]{2,1,0:T(8,128)(2,1)S(1)}, bf16[2,576,128]{2,1,0:T(8,128)(2,1)S(1)}, u32[]{:S(2)}, u32[]{:S(2)}) %collective-permute-start.2) | collective-permute-done | bytes 294944 | tf_op jit(solution)/shard_map/ppermute | solution.py:30
  44.1 5.5 %collective-permute-start.3 = (bf16[2,576,128]{2,1,0:T(8,128)(2,1)S(1)}, bf16[2,576,128]{2,1,0:T(8,128)(2,1)S(1)}, u32[]{:S(2)}, u32[]{:S(2)}) collective-permute-start(bf16[2,576,128]{2,1,0:T(8,128)(2,1)S(1)} %collective-permute-done.2), channel_id=1, source_target_pairs={{0,16},{1,17},{8,121},{9,120},{16,32},{17,33},{24,8},{25,9},{32,48... | collective-permute-start | bytes 884744 | tf_op jit(solution)/shard_map/ppermute | solution.py:30
  49.6 7.4 %collective-permute-start.4 = (bf16[1,576,128]{2,1,0:T(8,128)(2,1)S(1)}, bf16[1,576,128]{2,1,0:T(8,128)(2,1)S(1)}, u32[]{:S(2)}, u32[]{:S(2)}) collective-permute-start(bf16[1,576,128]{2,1,0:T(8,128)(2,1)S(1)} %slice.15), channel_id=1, source_target_pairs={{0,32},{1,33},{8,105},{9,104},{16,48},{17,49},{24,121},{25,120},{3... | collective-permute-start | bytes 442376 | tf_op jit(solution)/shard_map/ppermute | solution.py:30
  57.2 4.0 %collective-permute-done.3 = bf16[2,576,128]{2,1,0:T(8,128)(2,1)S(1)} collective-permute-done((bf16[2,576,128]{2,1,0:T(8,128)(2,1)S(1)}, bf16[2,576,128]{2,1,0:T(8,128)(2,1)S(1)}, u32[]{:S(2)}, u32[]{:S(2)}) %collective-permute-start.3) | collective-permute-done | bytes 294944 | tf_op jit(solution)/shard_map/ppermute | solution.py:30
  61.2 5.7 %collective-permute-done.4 = bf16[1,576,128]{2,1,0:T(8,128)(2,1)S(1)} collective-permute-done((bf16[1,576,128]{2,1,0:T(8,128)(2,1)S(1)}, bf16[1,576,128]{2,1,0:T(8,128)(2,1)S(1)}, u32[]{:S(2)}, u32[]{:S(2)}) %collective-permute-start.4) | collective-permute-done | bytes 147488 | tf_op jit(solution)/shard_map/ppermute | solution.py:30
  66.9 2.3 %collective-permute-start.5 = (bf16[7,576,128]{2,1,0:T(8,128)(2,1)S(1)}, bf16[7,576,128]{2,1,0:T(8,128)(2,1)S(1)}, u32[]{:S(2)}, u32[]{:S(2)}) collective-permute-start(bf16[7,576,128]{2,1,0:T(8,128)(2,1)S(1)} %constant_dynamic-update-slice_fusion.rest_1_), channel_id=1, source_target_pairs={{0,8},{8,0},{1,9},{9,1},{2,10},{10,2},{3,11},{11,3},{4,12},{12,4},... | collective-permute-start | bytes 3096584 | tf_op jit(solution)/shard_map/ppermute | solution.py:30
  69.9 1.5 copy.28
  72.1 0.9 slice.14
  73.2 18.2 %shard_map.111 = bf16[256,1152]{1,0:T(8,128)(2,1)S(1)} custom-call(s32[8]{0:T(128)S(1)} %add_reduce_fusion.starts, s32[16]{0:T(128)S(1)} %fusion.7.bases, s32[1]{0:T(128)S(6)} %copy.35.limit_ref, bf16[8,256,576]{2,1,0:T(8,128)(2,1)} %shard_map.110.query, bf16[2,576,128]{2,1,0:T(8,128)(2,1)S(1)} %pad_maximum_fusion.1.rest_0_, ...), custom_call_target="tpu_custom_call" | custom-call | tf_op jit(solution)/shard_map/pallas_call | solution.py:208
  91.4 16.4 %all_to_all.20.parts = bf16[4,64,1152]{2,1,0:T(8,128)(2,1)} all-to-all(bf16[4,64,1152]{2,1,0:T(8,128)(2,1)S(1)} %bitcast.54), channel_id=1, replica_groups=mesh['y'=4,'z'=8,'c'=2,'x'=4,'h'=2] {'y'}, dimensions={0} | all-to-all | bytes 1179648 | tf_op jit(solution)/shard_map/all_to_all | solution.py:306
  107.8 2.2 %shard_map.112 = bf16[64,1024]{1,0:T(8,128)(2,1)} custom-call(bf16[4,64,1152]{2,1,0:T(8,128)(2,1)} %all_to_all.20.parts), custom_call_target="tpu_custom_call" | custom-call | tf_op jit(solution)/shard_map/pallas_call | solution.py:251
  110.0 1.9 %collective-permute-start.6 = (bf16[896,1024]{1,0:T(8,128)(2,1)}, bf16[896,1024]{1,0:T(8,128)(2,1)S(1)}, u32[]{:S(2)}, u32[]{:S(2)}) collective-permute-start(bf16[896,1024]{1,0:T(8,128)(2,1)} %all-gather.2.cloned.1.call-done), channel_id=1, source_target_pairs={{0,8},{8,0},{1,9},{9,1},{2,10},{10,2},{3,11},{11,3},{4,12},{12,4},... | collective-permute-start | bytes 5505032 | tf_op jit(solution)/shard_map/ppermute | solution.py:30
  111.9 1.0 broadcast_in_dim.5
  112.9 12.8 %all_to_all.21 = bf16[4,64,1024]{2,1,0:T(8,128)(2,1)S(1)} all-to-all(bf16[4,64,1024]{2,1,0:T(8,128)(2,1)S(1)} %broadcast_in_dim.5), channel_id=1, replica_groups=mesh['y'=4,'z'=8,'c'=2,'x'=4,'h'=2] {'y'}, dimensions={0} | all-to-all | bytes 1048576 | tf_op jit(solution)/shard_map/all_to_all | solution.py:46
  125.7 2.2 %convolution_convert_fusion.1 = bf16[256,896]{1,0:T(8,128)(2,1)S(1)} fusion(bf16[256,1024]{1,0:T(8,128)(2,1)S(1)} %bitcast.62, bf16[896,1024]{1,0:T(8,128)(2,1)} %all-gather.2.cloned.1.call-done), kind=kOutput, calls=%fused_computation.2 | convolution fusion | flops 469991424 | bytes 2818048 | tf_op jit(solution)/shard_map/dot_general | solution.py:316
  128.7 1.0 pad_maximum_fusion
  129.7 5.0 %all-to-all-start.3 = ((bf16[16,16,1792]{2,1,0:T(8,128)(2,1)}), bf16[16,16,1792]{2,1,0:T(8,128)(2,1)S(1)}, u32[]{:S(2)}, u32[]{:S(2)}) async-start(bf16[16,16,1792]{2,1,0:T(8,128)(2,1)} %bitcast.7), calls=%async_computation.3 | async-start | bytes 1835008 | tf_op jit(solution)/shard_map/all_to_all | solution.py:325
  134.7 15.5 %all-to-all-done.3 = bf16[16,16,1792]{2,1,0:T(8,128)(2,1)S(1)} async-done(((bf16[16,16,1792]{2,1,0:T(8,128)(2,1)}), bf16[16,16,1792]{2,1,0:T(8,128)(2,1)S(1)}, u32[]{:S(2)}, u32[]{:S(2)}) %all-to-all-start.3) | async-done | bytes 917536 | tf_op jit(solution)/shard_map/all_to_all | solution.py:325
  150.3 19.4 %collective-permute-start.7 = (bf16[4,8,1792]{2,1,0:T(8,128)(2,1)S(1)}, bf16[4,8,1792]{2,1,0:T(8,128)(2,1)S(1)}, u32[]{:S(2)}, u32[]{:S(2)}) collective-permute-start(bf16[4,8,1792]{2,1,0:T(8,128)(2,1)S(1)} %fusion.4), channel_id=1, source_target_pairs={{0,1},{1,0},{2,3},{3,2},{4,5},{5,4},{6,7},{7,6},{8,9},{9,8},{10,11... | collective-permute-start | bytes 344072 | tf_op jit(solution)/shard_map/ppermute | solution.py:30
  169.8 6.8 %collective-permute-done.7 = bf16[4,8,1792]{2,1,0:T(8,128)(2,1)S(1)} collective-permute-done((bf16[4,8,1792]{2,1,0:T(8,128)(2,1)S(1)}, bf16[4,8,1792]{2,1,0:T(8,128)(2,1)S(1)}, u32[]{:S(2)}, u32[]{:S(2)}) %collective-permute-start.7) | collective-permute-done | bytes 114720 | tf_op jit(solution)/shard_map/ppermute | solution.py:30
  (29 shorter events, 3.1 us)
Async XLA Ops:
  6.5 103.5 %all-gather.2.cloned.1.call-start = ((), (), s32[]{:S(2)}) async-start(), calls=%async_computation.4 | async-start | bytes 2064384 | tf_op jit(solution)/shard_map/all_gather | solution.py:278
  7.3 5.2 %collective-permute-start = (bf16[576,128]{1,0:T(8,128)(2,1)}, bf16[576,128]{1,0:T(8,128)(2,1)S(1)}, u32[]{:S(2)}, u32[]{:S(2)}) collective-permute-start(bf16[576,128]{1,0:T(8,128)(2,1)} %param.13), channel_id=1, source_target_pairs={{0,8},{8,0},{1,9},{9,1},{2,10},{10,2},{3,11},{11,3},{4,12},{12,4},... | collective-permute-start | bytes 442376 | tf_op jit(solution)/shard_map/ppermute | solution.py:30
  10.8 19.3 %copy-start.1 = (bf16[512,8,128]{2,1,0:T(8,128)(2,1)S(1)}, bf16[512,8,128]{2,1,0:T(8,128)(2,1)}, u32[]{:S(2)}) copy-start(bf16[512,8,128]{2,1,0:T(8,128)(2,1)} %param.14) | copy-start | bytes 3145732
  15.3 18.1 %all-to-all-start = ((bf16[4,64,1664]{2,1,0:T(8,128)(2,1)}), bf16[4,64,1664]{2,1,0:T(8,128)(2,1)S(1)}, u32[]{:S(2)}, u32[]{:S(2)}) async-start(bf16[4,64,1664]{2,1,0:T(8,128)(2,1)} %broadcast_in_dim.4), calls=%async_computation | async-start | bytes 1703936 | tf_op jit(solution)/shard_map/all_to_all | solution.py:46
  19.8 21.1 %collective-permute-start.1 = (bf16[2,576,128]{2,1,0:T(8,128)(2,1)S(1)}, bf16[2,576,128]{2,1,0:T(8,128)(2,1)S(1)}, u32[]{:S(2)}, u32[]{:S(2)}) collective-permute-start(bf16[2,576,128]{2,1,0:T(8,128)(2,1)S(1)} %pad_maximum_fusion.1.rest_0_), channel_id=1, source_target_pairs={{0,16},{1,17},{8,121},{9,120},{16,32},{17,33},{24,8},{25,9},{32,48... | collective-permute-start | bytes 884744 | tf_op jit(solution)/shard_map/ppermute | solution.py:30
  23.6 20.5 %collective-permute-start.2 = (bf16[2,576,128]{2,1,0:T(8,128)(2,1)S(1)}, bf16[2,576,128]{2,1,0:T(8,128)(2,1)S(1)}, u32[]{:S(2)}, u32[]{:S(2)}) collective-permute-start(bf16[2,576,128]{2,1,0:T(8,128)(2,1)S(1)} %pad_maximum_fusion.1.rest_0_), channel_id=1, source_target_pairs={{0,32},{1,33},{8,105},{9,104},{16,48},{17,49},{24,121},{25,120},{3... | collective-permute-start | bytes 884744 | tf_op jit(solution)/shard_map/ppermute | solution.py:30
  33.5 0.9 copy-start
  44.1 17.0 %collective-permute-start.3 = (bf16[2,576,128]{2,1,0:T(8,128)(2,1)S(1)}, bf16[2,576,128]{2,1,0:T(8,128)(2,1)S(1)}, u32[]{:S(2)}, u32[]{:S(2)}) collective-permute-start(bf16[2,576,128]{2,1,0:T(8,128)(2,1)S(1)} %collective-permute-done.2), channel_id=1, source_target_pairs={{0,16},{1,17},{8,121},{9,120},{16,32},{17,33},{24,8},{25,9},{32,48... | collective-permute-start | bytes 884744 | tf_op jit(solution)/shard_map/ppermute | solution.py:30
  49.6 17.2 %collective-permute-start.4 = (bf16[1,576,128]{2,1,0:T(8,128)(2,1)S(1)}, bf16[1,576,128]{2,1,0:T(8,128)(2,1)S(1)}, u32[]{:S(2)}, u32[]{:S(2)}) collective-permute-start(bf16[1,576,128]{2,1,0:T(8,128)(2,1)S(1)} %slice.15), channel_id=1, source_target_pairs={{0,32},{1,33},{8,105},{9,104},{16,48},{17,49},{24,121},{25,120},{3... | collective-permute-start | bytes 442376 | tf_op jit(solution)/shard_map/ppermute | solution.py:30
  57.1 15.0 %copy-start.2 = (s32[16]{0:T(128)S(1)}, s32[16]{0:T(128)}, u32[]{:S(2)}) copy-start(s32[16]{0:T(128)} %constant.56.clone) | copy-start | bytes 196
  57.1 15.0 %copy-start.3 = (s32[16]{0:T(128)S(1)}, s32[16]{0:T(128)}, u32[]{:S(2)}) copy-start(s32[16]{0:T(128)} %constant.57.clone) | copy-start | bytes 196
  66.9 6.3 %collective-permute-start.5 = (bf16[7,576,128]{2,1,0:T(8,128)(2,1)S(1)}, bf16[7,576,128]{2,1,0:T(8,128)(2,1)S(1)}, u32[]{:S(2)}, u32[]{:S(2)}) collective-permute-start(bf16[7,576,128]{2,1,0:T(8,128)(2,1)S(1)} %constant_dynamic-update-slice_fusion.rest_1_), channel_id=1, source_target_pairs={{0,8},{8,0},{1,9},{9,1},{2,10},{10,2},{3,11},{11,3},{4,12},{12,4},... | collective-permute-start | bytes 3096584 | tf_op jit(solution)/shard_map/ppermute | solution.py:30
  110.0 17.9 %collective-permute-start.6 = (bf16[896,1024]{1,0:T(8,128)(2,1)}, bf16[896,1024]{1,0:T(8,128)(2,1)S(1)}, u32[]{:S(2)}, u32[]{:S(2)}) collective-permute-start(bf16[896,1024]{1,0:T(8,128)(2,1)} %all-gather.2.cloned.1.call-done), channel_id=1, source_target_pairs={{0,8},{8,0},{1,9},{9,1},{2,10},{10,2},{3,11},{11,3},{4,12},{12,4},... | collective-permute-start | bytes 5505032 | tf_op jit(solution)/shard_map/ppermute | solution.py:30
  129.7 20.5 %all-to-all-start.3 = ((bf16[16,16,1792]{2,1,0:T(8,128)(2,1)}), bf16[16,16,1792]{2,1,0:T(8,128)(2,1)S(1)}, u32[]{:S(2)}, u32[]{:S(2)}) async-start(bf16[16,16,1792]{2,1,0:T(8,128)(2,1)} %bitcast.7), calls=%async_computation.3 | async-start | bytes 1835008 | tf_op jit(solution)/shard_map/all_to_all | solution.py:325
  150.3 26.3 %collective-permute-start.7 = (bf16[4,8,1792]{2,1,0:T(8,128)(2,1)S(1)}, bf16[4,8,1792]{2,1,0:T(8,128)(2,1)S(1)}, u32[]{:S(2)}, u32[]{:S(2)}) collective-permute-start(bf16[4,8,1792]{2,1,0:T(8,128)(2,1)S(1)} %fusion.4), channel_id=1, source_target_pairs={{0,1},{1,0},{2,3},{3,2},{4,5},{5,4},{6,7},{7,6},{8,9},{9,8},{10,11... | collective-permute-start | bytes 344072 | tf_op jit(solution)/shard_map/ppermute | solution.py:30
Sparse Core Ops, SparseCore 0:
  9.4 77.2 all-gather.1

commit v4 on v3

--- a/solution.py
+++ b/solution.py
@@ -42,30 +42,32 @@
     return permute(x, ("c",), lambda at: {"c": 1 - at["c"]})
 
 
-def to_all_y(x):
-    return lax.all_to_all(
-        jnp.broadcast_to(x[None], (4,) + x.shape), "y", split_axis=0, concat_axis=0, tiled=True
-    )
+def swap_y(x):
+    return lax.all_to_all(x, "y", split_axis=0, concat_axis=0, tiled=True)
 
 
 def pack_kernel(order, content, rotary, out, *, block):
-    left = content.shape[1]
-    out[:, :left] = content[...]
-    out[:, left : left + rotary.shape[1]] = rotary[...]
-    row = lax.broadcasted_iota(jnp.int32, (out.shape[0], STATS), 0)
-    number = jnp.where(row < block, order[0], order[1])
-    out[:, left + rotary.shape[1] :] = number.astype(jnp.float32).astype(out.dtype)
-
-
-def pack(order, content, rotary, block):
-    rows = content.shape[0]
-    width = content.shape[1] + rotary.shape[1] + STATS
+    heads, nope = content.shape[1:]
+    left = heads * nope
+    width = left + rotary.shape[1]
+    row = lax.broadcasted_iota(jnp.int32, (out.shape[1], STATS), 0)
+    number = jnp.where(row < block, order[0], order[1]).astype(jnp.float32).astype(out.dtype)
+    for i in range(out.shape[0]):
+        for h in range(heads):
+            out[i, :, h * nope : (h + 1) * nope] = content[:, h, :]
+        out[i, :, left:width] = rotary[...]
+        out[i, :, width:] = number
+
+
+def pack(order, content, rotary, block, copies):
+    rows, heads, nope = content.shape
+    width = heads * nope + rotary.shape[1] + STATS
     vmem = pl.BlockSpec(memory_space=pltpu.VMEM)
     return pl.pallas_call(
         functools.partial(pack_kernel, block=block),
         in_specs=[pl.BlockSpec(memory_space=pltpu.SMEM), vmem, vmem],
         out_specs=vmem,
-        out_shape=jax.ShapeDtypeStruct((rows, width), jnp.bfloat16),
+        out_shape=jax.ShapeDtypeStruct((copies, rows, width), jnp.bfloat16),
     )(order, content, rotary)
 
 
@@ -99,10 +101,32 @@
     )(payload, payload, key_up)
 
 
+def three_parts(x):
+    parts = []
+    for _ in range(3):
+        part = x.astype(jnp.bfloat16).astype(jnp.float32)
+        parts.append(part)
+        x = x - part
+    return parts
+
+
+def read_stats(rows, heads):
+    stats = rows[:, rows.shape[1] - STATS :].astype(jnp.float32)
+    return stats[:, :heads] + stats[:, heads : 2 * heads] + stats[:, 2 * heads : 3 * heads]
+
+
+def write_stats(rows, lse):
+    heads = lse.shape[1]
+    empty = jnp.zeros((lse.shape[0], STATS - 3 * heads), jnp.float32)
+    rows[:, rows.shape[1] - STATS :] = jnp.concatenate(three_parts(lse) + [empty], axis=1).astype(
+        rows.dtype
+    )
+
+
 def attend_kernel(
-    starts, bases, limit_ref, query, *rest, shards, coef, latent, block, heads, groups
+    starts, bases, limit_ref, query, *rest, shards, coef, latent, block, heads, groups, with_before
 ):
-    *keys, value_up, out, mixed = rest
+    *keys, value_up, before, out, mixed = rest
     group = pl.program_id(0)
     rows = heads * block
     width = keys[0].shape[2]
@@ -116,12 +140,7 @@
         at = pl.ds(group * 2 * block + half * block, block)
         mixed[:, at, :] = normal.astype(mixed.dtype).reshape(heads, block, latent)
         lane = lax.broadcasted_iota(jnp.int32, (block, STATS), 1)
-        parts = []
-        left = lse
-        for _ in range(3):
-            part = left.astype(jnp.bfloat16).astype(jnp.float32)
-            parts.append(part)
-            left = left - part
+        parts = three_parts(lse)
         stats = jnp.zeros((block, STATS), jnp.float32)
         for k, part in enumerate(parts):
             for h in range(heads):
@@ -182,14 +201,23 @@
 
     @pl.when(group == groups - 1)
     def _():
+        if with_before:
+            old, new = read_stats(before, heads), read_stats(out, heads)
+            top = jnp.maximum(old, new)
+            old, new = jnp.exp2(old - top), jnp.exp2(new - top)
+            total = old + new
+            old, new = old / total, new / total
+            write_stats(out, top + jnp.log2(total))
         for h in range(heads):
             cols = slice(h * 128, (h + 1) * 128)
-            out[:, cols] = jnp.dot(
-                mixed[h], value_up[:, cols], preferred_element_type=jnp.float32
-            ).astype(out.dtype)
-
-
-def attend(starts, bases, limit, query, keys, value_up, scale):
+            value = jnp.dot(mixed[h], value_up[:, cols], preferred_element_type=jnp.float32)
+            if with_before:
+                value = value * new[:, h : h + 1]
+                value = value + before[:, cols].astype(jnp.float32) * old[:, h : h + 1]
+            out[:, cols] = value.astype(out.dtype)
+
+
+def attend(starts, bases, limit, query, keys, value_up, scale, before=None):
     heads, tokens, depth = query.shape
     latent, value_width = value_up.shape
     shards = sum(k.shape[0] for k in keys)
@@ -204,7 +232,10 @@
         block=per_group // 2,
         heads=heads,
         groups=groups,
-    )
+        with_before=before is not None,
+    )
+    if before is None:
+        before = jnp.zeros((16, STATS), jnp.bfloat16)
     return pl.pallas_call(
         kernel,
         grid_spec=pltpu.PrefetchScalarGridSpec(
@@ -212,24 +243,19 @@
             grid=(groups,),
             in_specs=[pl.BlockSpec((heads, per_group, depth), lambda i, *_: (0, i, 0))]
             + [whole(k.shape) for k in keys]
-            + [whole(value_up.shape)],
+            + [whole(value_up.shape), whole(before.shape)],
             out_specs=whole((tokens, value_width + STATS)),
             scratch_shapes=[pltpu.VMEM((heads, tokens, latent), jnp.bfloat16)],
         ),
         out_shape=jax.ShapeDtypeStruct((tokens, value_width + STATS), jnp.bfloat16),
         compiler_params=pltpu.CompilerParams(vmem_limit_bytes=48 * 1024 * 1024),
-    )(starts, bases, limit, query, *keys, value_up)
+    )(starts, bases, limit, query, *keys, value_up, before)
 
 
 def merge_kernel(parts, out, *, heads, sources):
-    width = out.shape[1]
+    width = out.shape[2]
     each = width // heads
-    lses = []
-    for s in range(sources):
-        stats = parts[s, :, width:].astype(jnp.float32)
-        lses.append(
-            stats[:, :heads] + stats[:, heads : 2 * heads] + stats[:, 2 * heads : 3 * heads]
-        )
+    lses = [read_stats(parts.at[s], heads) for s in range(sources)]
     top = functools.reduce(jnp.maximum, lses)
     weights = [jnp.exp2(v - top) for v in lses]
     total = functools.reduce(jnp.add, weights)
@@ -242,15 +268,16 @@
                 weights[s][:, h : h + 1] * parts[s, :, cols].astype(jnp.float32)
                 for s in range(sources)
             ],
-        )
-        out[:, cols] = value.astype(out.dtype)
-
-
-def merge(parts, heads):
+        ).astype(out.dtype)
+        for i in range(out.shape[0]):
+            out[i, :, cols] = value
+
+
+def merge(parts, heads, copies):
     sources, tokens, width = parts.shape
     return pl.pallas_call(
         functools.partial(merge_kernel, heads=heads, sources=sources),
-        out_shape=jax.ShapeDtypeStruct((tokens, width - STATS), jnp.bfloat16),
+        out_shape=jax.ShapeDtypeStruct((copies, tokens, width - STATS), jnp.bfloat16),
     )(parts)
 
 
@@ -277,40 +304,46 @@
 
     weight = lax.all_gather(output_weight.T, "z", axis=0, tiled=True)
 
-    payload = pack(block_order, query_content.reshape(tokens, heads * nope), query_rotary, block)
+    packed = pack(block_order, query_content, query_rotary, block, 4)
 
     pair = jnp.stack([key_cache, other_core(key_cache)])
-    payload, pair = lax.optimization_barrier((payload, pair))
     one, two = along_z(pair, 1), along_z(pair, 2)
-    payload = to_all_y(payload).reshape(4 * tokens, -1)
+    two, _ = lax.optimization_barrier((two, packed))
+    near = jnp.concatenate([one, two], axis=0)
+    near_swapped = other_core(near)
+    three, four = along_z(two, 1), along_z(two[:1], 2)
+
+    payload = swap_y(packed).reshape(4 * tokens, -1)
     starts = query_start[0] + payload[::block, -1].astype(jnp.int32) * block
     queries = latent_queries(payload, key_up.reshape(latent, heads * nope), heads, nope, rope)
-    queries, one, two = lax.optimization_barrier((queries, one, two))
-    three, four = along_z(two, 1), along_z(two[:1], 2)
-    fetched = jnp.concatenate([one, two, three, four], axis=0)
-    keys = [pair, fetched, other_core(fetched)]
+
     side = 1 - 2 * c
-    steps = np.array([0, 0, 1, 1, 2, 2, 3, 3, 4, -1, -1, -2, -2, -3, -3, -4], np.int32)
-    cores = np.array([0, 1, 0, 1, 0, 1, 0, 1, 0, 1, 0, 1, 0, 1, 0, 1], np.int32)
-    bases = ((y * 8 + (z - side * steps) % 8) * 2 + (c + cores) % 2).astype(jnp.int32) * shard
-
-    partial = attend(
-        starts,
-        bases,
-        key_limit,
-        queries,
-        keys,
-        value_up.reshape(latent, heads * value_dim),
-        scale,
-    )
-    partial = lax.all_to_all(
-        partial.reshape(4, tokens, -1), "y", split_axis=0, concat_axis=0, tiled=True
-    )
-    values = merge(partial, heads)
+
+    def bases_of(steps, cores):
+        steps, cores = np.array(steps, np.int32), np.array(cores, np.int32)
+        place = (y * 8 + (z - side * steps) % 8) * 2 + (c + cores) % 2
+        return place.astype(jnp.int32) * shard
+
+    attend_part = functools.partial(
+        attend, starts, limit=key_limit, query=queries, scale=scale,
+        value_up=value_up.reshape(latent, heads * value_dim),
+    )
+    partial = attend_part(
+        bases_of([0, 0, 1, 1, 2, 2, -1, -1, -2, -2], [0, 1, 0, 1, 0, 1, 1, 0, 1, 0]),
+        keys=[pair, near, near_swapped],
+    )
+    three, four, partial = lax.optimization_barrier((three, four, partial))
+    far = jnp.concatenate([three, four], axis=0)
+    partial = attend_part(
+        bases_of([3, 3, 4, -3, -3, -4], [0, 1, 0, 1, 0, 1]),
+        keys=[far, other_core(far)],
+        before=partial,
+    )
+    values = merge(swap_y(partial.reshape(4, tokens, -1)), heads, 4)
     values, weight = lax.optimization_barrier((values, weight))
     weights = [weight, other_core(weight)]
 
-    rows = to_all_y(values).reshape(4 * tokens, -1)
+    rows = swap_y(values).reshape(4 * tokens, -1)
     product = jnp.concatenate(
         [
             lax.dot_general(

time: 186 us -> 172 us (0.925)
  starting transfers between devices: 58.2 us -> 47 us
  waiting for transfers between devices: 38 us -> 32.3 us
  Pallas kernels: 28.7 us -> 33.2 us
    ppermute x8 -> x9, starting transfers between devices: 48.7 us -> 37.3 us  [permute(): return lax.ppermute(x, names, pairs)]
    ppermute x8 -> x9, waiting for transfers between devices: 19.7 us -> 16.2 us  [permute(): return lax.ppermute(x, names, pairs)]
    pallas_call x1 -> x2, Pallas kernels: 18.2 us -> 21.7 us  [attend(): pl.pallas_call(kernel, grid_spec=pltpu.PrefetchScalarGridSpec(num_scalar_...]
    broadcast_in_dim x2 -> x1, local copies, waits for them, and re-layouts: 2.86 us -> 0.01 us  [attend(): before = jnp.zeros((16, STATS), jnp.bfloat16)]
    all_to_all x1, waiting for transfers between devices: 2.13 us -> 0.01 us  [swap_y(): return lax.all_to_all(x, 'y', split_axis=0, concat_axis=0, tiled=True)]
    unnamed x14 -> x22, local copies, waits for them, and re-layouts: 5.39 us -> 5.84 us
  transfers between devices with their start and end apart: 11 -> 12, of which waited for: 6 -> 5; matrix products, arithmetic and copies ran while one was open for 6% -> 4% of each run, Pallas kernels for 16% -> 19%
where the time goes in v4:
time: 172 us; the launch traced here: 171 us
  starting transfers between devices  47 us (27%)
  Pallas kernels  33.2 us (19%)
  waiting for transfers between devices  32.3 us (19%)
  blocking collectives  29.3 us (17%)
  between operations  15 us (9%)
  local copies, waits for them, and re-layouts  8.76 us (5%)
  matrix products  2.98 us (2%)
  other arithmetic  2.31 us (1%)
    ppermute x9, starting transfers between devices, permute(): return lax.ppermute(x, names, pairs)  37.3 us
    all_to_all x2, blocking collectives, swap_y(): return lax.all_to_all(x, 'y', split_axis=0, concat_axis=0, tiled=True)  29.3 us
    pallas_call x2, Pallas kernels, attend(): pl.pallas_call(kernel, grid_spec=pltpu.PrefetchScalarGridSpec(num_scalar_...  21.7 us
    ppermute x9, waiting for transfers between devices, permute(): return lax.ppermute(x, names, pairs)  16.2 us
    all_to_all x1, waiting for transfers between devices, per_device(): lax.all_to_all(product.reshape(16, 2 * share, width), ('y', 'x'), split_a...  15.4 us
    pallas_call x1, Pallas kernels, latent_queries(): pl.pallas_call(query_kernel, grid=(heads,), in_specs=[pl.BlockSpec((rows,...  6.55 us
    unnamed x22, local copies, waits for them, and re-layouts  5.84 us
    all_to_all x1, starting transfers between devices, per_device(): lax.all_to_all(product.reshape(16, 2 * share, width), ('y', 'x'), split_a...  5.08 us
  transfers between devices with their start and end apart: 12, of which 5 were waited for; matrix products, arithmetic and copies ran while one was open for 4% of the time, Pallas kernels for 19%

profile of v4, /device:TPU:32, one launch (start us, length us, event | category | flops | bytes accessed | tf_op | source)
XLA Modules:
  0.0 170.9 jit_solution(5005004432518904137)
XLA Ops:
  7.3 1.9 %collective-permute-start = (bf16[576,128]{1,0:T(8,128)(2,1)}, bf16[576,128]{1,0:T(8,128)(2,1)S(1)}, u32[]{:S(2)}, u32[]{:S(2)}) collective-permute-start(bf16[576,128]{1,0:T(8,128)(2,1)} %param.15), channel_id=1, source_target_pairs={{0,8},{8,0},{1,9},{9,1},{2,10},{10,2},{3,11},{11,3},{4,12},{12,4},... | collective-permute-start | bytes 442376 | tf_op jit(solution)/shard_map/ppermute | solution.py:30
  9.2 1.5 collective-permute-done
  10.7 0.9 pad_maximum_fusion.1.rest_0_
  11.7 5.2 %collective-permute-start.1 = (bf16[2,576,128]{2,1,0:T(8,128)(2,1)S(1)}, bf16[2,576,128]{2,1,0:T(8,128)(2,1)S(1)}, u32[]{:S(2)}, u32[]{:S(2)}) collective-permute-start(bf16[2,576,128]{2,1,0:T(8,128)(2,1)S(1)} %pad_maximum_fusion.1.rest_0_), channel_id=1, source_target_pairs={{0,32},{1,33},{8,105},{9,104},{16,48},{17,49},{24,121},{25,120},{3... | collective-permute-start | bytes 884744 | tf_op jit(solution)/shard_map/ppermute | solution.py:30
  16.9 5.0 %collective-permute-start.4 = (bf16[2,576,128]{2,1,0:T(8,128)(2,1)S(1)}, bf16[2,576,128]{2,1,0:T(8,128)(2,1)S(1)}, u32[]{:S(2)}, u32[]{:S(2)}) collective-permute-start(bf16[2,576,128]{2,1,0:T(8,128)(2,1)S(1)} %pad_maximum_fusion.1.rest_0_), channel_id=1, source_target_pairs={{0,16},{1,17},{8,121},{9,120},{16,32},{17,33},{24,8},{25,9},{32,48... | collective-permute-start | bytes 884744 | tf_op jit(solution)/shard_map/ppermute | solution.py:30
  21.9 2.6 %shard_map.127 = bf16[4,64,1664]{2,1,0:T(8,128)(2,1)} custom-call(s32[2]{0:T(128)} %order.1, bf16[64,8,128]{2,1,0:T(8,128)(2,1)} %content.1, bf16[64,512]{1,0:T(8,128)(2,1)} %rotary.1), custom_call_target="tpu_custom_call" | custom-call | tf_op jit(solution)/shard_map/pallas_call | solution.py:66
  24.5 4.6 %all-to-all-start = ((bf16[4,64,1664]{2,1,0:T(8,128)(2,1)}), bf16[4,64,1664]{2,1,0:T(8,128)(2,1)S(1)}, u32[]{:S(2)}, u32[]{:S(2)}) async-start(bf16[4,64,1664]{2,1,0:T(8,128)(2,1)} %shard_map.127), calls=%async_computation | async-start | bytes 1703936 | tf_op jit(solution)/shard_map/all_to_all | solution.py:46
  29.1 1.3 collective-permute-done.1
  31.2 3.5 %collective-permute-start.5 = (bf16[4,576,128]{2,1,0:T(8,128)(2,1)S(1)}, bf16[4,576,128]{2,1,0:T(8,128)(2,1)S(1)}, u32[]{:S(2)}, u32[]{:S(2)}) collective-permute-start(bf16[4,576,128]{2,1,0:T(8,128)(2,1)S(1)} %constant_dynamic-update-slice_fusion.rest_1_), channel_id=1, source_target_pairs={{0,8},{8,0},{1,9},{9,1},{2,10},{10,2},{3,11},{11,3},{4,12},{12,4},... | collective-permute-start | bytes 1769480 | tf_op jit(solution)/shard_map/ppermute | solution.py:30
  34.8 3.1 %collective-permute-start.2 = (bf16[2,576,128]{2,1,0:T(8,128)(2,1)}, bf16[2,576,128]{2,1,0:T(8,128)(2,1)}, u32[]{:S(2)}, u32[]{:S(2)}) collective-permute-start(bf16[2,576,128]{2,1,0:T(8,128)(2,1)} %copy-done.4), channel_id=1, source_target_pairs={{0,16},{1,17},{8,121},{9,120},{16,32},{17,33},{24,8},{25,9},{32,48... | collective-permute-start | bytes 884744 | tf_op jit(solution)/shard_map/ppermute | solution.py:30
  37.9 1.6 slice.15
  39.5 3.4 %collective-permute-start.3 = (bf16[1,576,128]{2,1,0:T(8,128)(2,1)}, bf16[1,576,128]{2,1,0:T(8,128)(2,1)S(1)}, u32[]{:S(2)}, u32[]{:S(2)}) collective-permute-start(bf16[1,576,128]{2,1,0:T(8,128)(2,1)} %slice.15), channel_id=1, source_target_pairs={{0,32},{1,33},{8,105},{9,104},{16,48},{17,49},{24,121},{25,120},{3... | collective-permute-start | bytes 442376 | tf_op jit(solution)/shard_map/ppermute | solution.py:30
  44.2 1.3 copy.29
  45.9 0.8 copy-done.1
  46.7 6.6 %shard_map.128.query = bf16[8,256,576]{2,1,0:T(8,128)(2,1)} custom-call(bf16[256,1664]{1,0:T(8,128)(2,1)} %bitcast.53, bf16[256,1664]{1,0:T(8,128)(2,1)} %bitcast.54, bf16[512,1024]{1,0:T(8,128)(2,1)} %bitcast.55), custom_call_target="tpu_custom_call" | custom-call | flops 268435456 | bytes 8388608 | tf_op jit(solution)/shard_map/pallas_call | solution.py:88
  53.4 1.7 %copy-done = bf16[8,256,576]{2,1,0:T(8,128)(2,1)S(1)} copy-done((bf16[8,256,576]{2,1,0:T(8,128)(2,1)S(1)}, bf16[8,256,576]{2,1,0:T(8,128)(2,1)}, u32[]{:S(2)}) %copy-start) | copy-done | bytes 2359320
  55.1 12.5 %shard_map.129.rest_3_ = bf16[256,1152]{1,0:T(8,128)(2,1)S(1)} custom-call(s32[8]{0:T(128)S(1)} %add_reduce_fusion.starts, s32[10]{0:T(128)S(1)} %fusion.9.bases, s32[1]{0:T(128)S(6)} %copy.33.limit_ref, bf16[8,256,576]{2,1,0:T(8,128)(2,1)S(1)} %copy-done, bf16[2,576,128]{2,1,0:T(8,128)(2,1)S(1)} %pad_maximum_fusion.1.rest_0_, ...), custom_call_target="tpu_custom_call" | custom-call | tf_op jit(solution)/shard_map/pallas_call | solution.py:239
  67.7 1.0 constant_dynamic-update-slice_fusion.3
  68.7 3.9 %collective-permute-start.6 = (bf16[3,576,128]{2,1,0:T(8,128)(2,1)S(1)}, bf16[3,576,128]{2,1,0:T(8,128)(2,1)S(1)}, u32[]{:S(2)}, u32[]{:S(2)}) collective-permute-start(bf16[3,576,128]{2,1,0:T(8,128)(2,1)S(1)} %constant_dynamic-update-slice_fusion.2.rest_0_), channel_id=1, source_target_pairs={{0,8},{8,0},{1,9},{9,1},{2,10},{10,2},{3,11},{11,3},{4,12},{12,4},... | collective-permute-start | bytes 1327112 | tf_op jit(solution)/shard_map/ppermute | solution.py:30
  72.7 1.4 collective-permute-done.6.rest_1_
  74.0 9.2 %shard_map.130 = bf16[256,1152]{1,0:T(8,128)(2,1)S(1)} custom-call(s32[8]{0:T(128)S(1)} %add_reduce_fusion.starts, s32[6]{0:T(128)S(1)} %fusion.10.bases, s32[1]{0:T(128)S(6)} %copy.33.limit_ref, bf16[8,256,576]{2,1,0:T(8,128)(2,1)S(1)} %copy-done, bf16[3,576,128]{2,1,0:T(8,128)(2,1)S(1)} %constant_dynamic-update-slice_fusion.2.rest_0_, ...), custom_call_target="tpu_custom_call" | custom-call | tf_op jit(solution)/shard_map/pallas_call | solution.py:239
  83.2 15.5 %all_to_all.20.parts = bf16[4,64,1152]{2,1,0:T(8,128)(2,1)} all-to-all(bf16[4,64,1152]{2,1,0:T(8,128)(2,1)S(1)} %bitcast.51), channel_id=1, replica_groups=mesh['y'=4,'z'=8,'c'=2,'x'=4,'h'=2] {'y'}, dimensions={0} | all-to-all | bytes 1179648 | tf_op jit(solution)/shard_map/all_to_all | solution.py:46
  98.7 2.4 %shard_map.131 = bf16[4,64,1024]{2,1,0:T(8,128)(2,1)} custom-call(bf16[4,64,1152]{2,1,0:T(8,128)(2,1)} %all_to_all.20.parts), custom_call_target="tpu_custom_call" | custom-call | tf_op jit(solution)/shard_map/pallas_call | solution.py:278
  101.1 2.0 %collective-permute-start.7 = (bf16[896,1024]{1,0:T(8,128)(2,1)}, bf16[896,1024]{1,0:T(8,128)(2,1)S(1)}, u32[]{:S(2)}, u32[]{:S(2)}) collective-permute-start(bf16[896,1024]{1,0:T(8,128)(2,1)} %all-gather.2.cloned.1.call-done), channel_id=1, source_target_pairs={{0,8},{8,0},{1,9},{9,1},{2,10},{10,2},{3,11},{11,3},{4,12},{12,4},... | collective-permute-start | bytes 5505032 | tf_op jit(solution)/shard_map/ppermute | solution.py:30
  103.1 13.8 %all_to_all.21 = bf16[4,64,1024]{2,1,0:T(8,128)(2,1)S(1)} all-to-all(bf16[4,64,1024]{2,1,0:T(8,128)(2,1)} %shard_map.131), channel_id=1, replica_groups=mesh['y'=4,'z'=8,'c'=2,'x'=4,'h'=2] {'y'}, dimensions={0} | all-to-all | bytes 1048576 | tf_op jit(solution)/shard_map/all_to_all | solution.py:46
  116.9 2.2 %convolution_convert_fusion.1 = bf16[256,896]{1,0:T(8,128)(2,1)S(1)} fusion(bf16[256,1024]{1,0:T(8,128)(2,1)S(1)} %bitcast.59, bf16[896,1024]{1,0:T(8,128)(2,1)} %all-gather.2.cloned.1.call-done), kind=kOutput, calls=%fused_computation.2 | convolution fusion | flops 469991424 | bytes 2818048 | tf_op jit(solution)/shard_map/dot_general | solution.py:349
  119.9 1.0 pad_maximum_fusion
  120.9 5.1 %all-to-all-start.3 = ((bf16[16,16,1792]{2,1,0:T(8,128)(2,1)}), bf16[16,16,1792]{2,1,0:T(8,128)(2,1)S(1)}, u32[]{:S(2)}, u32[]{:S(2)}) async-start(bf16[16,16,1792]{2,1,0:T(8,128)(2,1)} %bitcast.7), calls=%async_computation.3 | async-start | bytes 1835008 | tf_op jit(solution)/shard_map/all_to_all | solution.py:358
  126.0 15.4 %all-to-all-done.3 = bf16[16,16,1792]{2,1,0:T(8,128)(2,1)S(1)} async-done(((bf16[16,16,1792]{2,1,0:T(8,128)(2,1)}), bf16[16,16,1792]{2,1,0:T(8,128)(2,1)S(1)}, u32[]{:S(2)}, u32[]{:S(2)}) %all-to-all-start.3) | async-done | bytes 917536 | tf_op jit(solution)/shard_map/all_to_all | solution.py:358
  141.5 9.3 %collective-permute-start.8 = (bf16[4,8,1792]{2,1,0:T(8,128)(2,1)S(1)}, bf16[4,8,1792]{2,1,0:T(8,128)(2,1)S(1)}, u32[]{:S(2)}, u32[]{:S(2)}) collective-permute-start(bf16[4,8,1792]{2,1,0:T(8,128)(2,1)S(1)} %fusion.4), channel_id=1, source_target_pairs={{0,1},{1,0},{2,3},{3,2},{4,5},{5,4},{6,7},{7,6},{8,9},{9,8},{10,11... | collective-permute-start | bytes 344072 | tf_op jit(solution)/shard_map/ppermute | solution.py:30
  150.9 12.0 %collective-permute-done.8 = bf16[4,8,1792]{2,1,0:T(8,128)(2,1)S(1)} collective-permute-done((bf16[4,8,1792]{2,1,0:T(8,128)(2,1)S(1)}, bf16[4,8,1792]{2,1,0:T(8,128)(2,1)S(1)}, u32[]{:S(2)}, u32[]{:S(2)}) %collective-permute-start.8) | collective-permute-done | bytes 114720 | tf_op jit(solution)/shard_map/ppermute | solution.py:30
  163.2 0.8 reshape.44
  (41 shorter events, 3.3 us)
Async XLA Ops:
  6.5 94.6 %all-gather.2.cloned.1.call-start = ((), (), s32[]{:S(2)}) async-start(), calls=%async_computation.4 | async-start | bytes 2064384 | tf_op jit(solution)/shard_map/all_gather | solution.py:305
  7.3 3.5 %collective-permute-start = (bf16[576,128]{1,0:T(8,128)(2,1)}, bf16[576,128]{1,0:T(8,128)(2,1)S(1)}, u32[]{:S(2)}, u32[]{:S(2)}) collective-permute-start(bf16[576,128]{1,0:T(8,128)(2,1)} %param.15), channel_id=1, source_target_pairs={{0,8},{8,0},{1,9},{9,1},{2,10},{10,2},{3,11},{11,3},{4,12},{12,4},... | collective-permute-start | bytes 442376 | tf_op jit(solution)/shard_map/ppermute | solution.py:30
  11.7 18.8 %collective-permute-start.1 = (bf16[2,576,128]{2,1,0:T(8,128)(2,1)S(1)}, bf16[2,576,128]{2,1,0:T(8,128)(2,1)S(1)}, u32[]{:S(2)}, u32[]{:S(2)}) collective-permute-start(bf16[2,576,128]{2,1,0:T(8,128)(2,1)S(1)} %pad_maximum_fusion.1.rest_0_), channel_id=1, source_target_pairs={{0,32},{1,33},{8,105},{9,104},{16,48},{17,49},{24,121},{25,120},{3... | collective-permute-start | bytes 884744 | tf_op jit(solution)/shard_map/ppermute | solution.py:30
  16.9 13.6 %collective-permute-start.4 = (bf16[2,576,128]{2,1,0:T(8,128)(2,1)S(1)}, bf16[2,576,128]{2,1,0:T(8,128)(2,1)S(1)}, u32[]{:S(2)}, u32[]{:S(2)}) collective-permute-start(bf16[2,576,128]{2,1,0:T(8,128)(2,1)S(1)} %pad_maximum_fusion.1.rest_0_), channel_id=1, source_target_pairs={{0,16},{1,17},{8,121},{9,120},{16,32},{17,33},{24,8},{25,9},{32,48... | collective-permute-start | bytes 884744 | tf_op jit(solution)/shard_map/ppermute | solution.py:30
  24.5 18.3 %copy-start.7 = (s32[10]{0:T(128)S(1)}, s32[10]{0:T(128)}, u32[]{:S(2)}) copy-start(s32[10]{0:T(128)} %constant.78.clone) | copy-start | bytes 124
  24.5 18.3 %copy-start.8 = (s32[10]{0:T(128)S(1)}, s32[10]{0:T(128)}, u32[]{:S(2)}) copy-start(s32[10]{0:T(128)} %constant.77.clone) | copy-start | bytes 124
  24.5 19.6 %copy-start.2 = (bf16[512,8,128]{2,1,0:T(8,128)(2,1)S(1)}, bf16[512,8,128]{2,1,0:T(8,128)(2,1)}, u32[]{:S(2)}) copy-start(bf16[512,8,128]{2,1,0:T(8,128)(2,1)} %param.16) | copy-start | bytes 3145732
  24.5 21.2 %all-to-all-start = ((bf16[4,64,1664]{2,1,0:T(8,128)(2,1)}), bf16[4,64,1664]{2,1,0:T(8,128)(2,1)S(1)}, u32[]{:S(2)}, u32[]{:S(2)}) async-start(bf16[4,64,1664]{2,1,0:T(8,128)(2,1)} %shard_map.127), calls=%async_computation | async-start | bytes 1703936 | tf_op jit(solution)/shard_map/all_to_all | solution.py:46
  30.5 0.7 copy-start.4
  31.2 22.1 %collective-permute-start.5 = (bf16[4,576,128]{2,1,0:T(8,128)(2,1)S(1)}, bf16[4,576,128]{2,1,0:T(8,128)(2,1)S(1)}, u32[]{:S(2)}, u32[]{:S(2)}) collective-permute-start(bf16[4,576,128]{2,1,0:T(8,128)(2,1)S(1)} %constant_dynamic-update-slice_fusion.rest_1_), channel_id=1, source_target_pairs={{0,8},{8,0},{1,9},{9,1},{2,10},{10,2},{3,11},{11,3},{4,12},{12,4},... | collective-permute-start | bytes 1769480 | tf_op jit(solution)/shard_map/ppermute | solution.py:30
  34.8 10.7 %copy-start.3 = (bf16[512,8,128]{2,1,0:T(8,128)(2,1)S(1)}, bf16[512,8,128]{2,1,0:T(8,128)(2,1)}, u32[]{:S(2)}) copy-start(bf16[512,8,128]{2,1,0:T(8,128)(2,1)} %param.17) | copy-start | bytes 3145732
  34.8 32.9 %collective-permute-start.2 = (bf16[2,576,128]{2,1,0:T(8,128)(2,1)}, bf16[2,576,128]{2,1,0:T(8,128)(2,1)}, u32[]{:S(2)}, u32[]{:S(2)}) collective-permute-start(bf16[2,576,128]{2,1,0:T(8,128)(2,1)} %copy-done.4), channel_id=1, source_target_pairs={{0,16},{1,17},{8,121},{9,120},{16,32},{17,33},{24,8},{25,9},{32,48... | collective-permute-start | bytes 884744 | tf_op jit(solution)/shard_map/ppermute | solution.py:30
  39.5 28.2 %collective-permute-start.3 = (bf16[1,576,128]{2,1,0:T(8,128)(2,1)}, bf16[1,576,128]{2,1,0:T(8,128)(2,1)S(1)}, u32[]{:S(2)}, u32[]{:S(2)}) collective-permute-start(bf16[1,576,128]{2,1,0:T(8,128)(2,1)} %slice.15), channel_id=1, source_target_pairs={{0,32},{1,33},{8,105},{9,104},{16,48},{17,49},{24,121},{25,120},{3... | collective-permute-start | bytes 442376 | tf_op jit(solution)/shard_map/ppermute | solution.py:30
  45.8 0.9 copy-start.1
  53.4 1.7 %copy-start = (bf16[8,256,576]{2,1,0:T(8,128)(2,1)S(1)}, bf16[8,256,576]{2,1,0:T(8,128)(2,1)}, u32[]{:S(2)}) copy-start(bf16[8,256,576]{2,1,0:T(8,128)(2,1)} %shard_map.128.query) | copy-start | bytes 7077892
  55.1 17.5 %copy-start.5 = (s32[6]{0:T(128)S(1)}, s32[6]{0:T(128)}, u32[]{:S(2)}) copy-start(s32[6]{0:T(128)} %constant.80.clone) | copy-start | bytes 76
  55.1 17.5 %copy-start.6 = (s32[6]{0:T(128)S(1)}, s32[6]{0:T(128)}, u32[]{:S(2)}) copy-start(s32[6]{0:T(128)} %constant.79.clone) | copy-start | bytes 76
  68.7 5.3 %collective-permute-start.6 = (bf16[3,576,128]{2,1,0:T(8,128)(2,1)S(1)}, bf16[3,576,128]{2,1,0:T(8,128)(2,1)S(1)}, u32[]{:S(2)}, u32[]{:S(2)}) collective-permute-start(bf16[3,576,128]{2,1,0:T(8,128)(2,1)S(1)} %constant_dynamic-update-slice_fusion.2.rest_0_), channel_id=1, source_target_pairs={{0,8},{8,0},{1,9},{9,1},{2,10},{10,2},{3,11},{11,3},{4,12},{12,4},... | collective-permute-start | bytes 1327112 | tf_op jit(solution)/shard_map/ppermute | solution.py:30
  101.1 18.1 %collective-permute-start.7 = (bf16[896,1024]{1,0:T(8,128)(2,1)}, bf16[896,1024]{1,0:T(8,128)(2,1)S(1)}, u32[]{:S(2)}, u32[]{:S(2)}) collective-permute-start(bf16[896,1024]{1,0:T(8,128)(2,1)} %all-gather.2.cloned.1.call-done), channel_id=1, source_target_pairs={{0,8},{8,0},{1,9},{9,1},{2,10},{10,2},{3,11},{11,3},{4,12},{12,4},... | collective-permute-start | bytes 5505032 | tf_op jit(solution)/shard_map/ppermute | solution.py:30
  120.9 20.5 %all-to-all-start.3 = ((bf16[16,16,1792]{2,1,0:T(8,128)(2,1)}), bf16[16,16,1792]{2,1,0:T(8,128)(2,1)S(1)}, u32[]{:S(2)}, u32[]{:S(2)}) async-start(bf16[16,16,1792]{2,1,0:T(8,128)(2,1)} %bitcast.7), calls=%async_computation.3 | async-start | bytes 1835008 | tf_op jit(solution)/shard_map/all_to_all | solution.py:358
  141.5 21.3 %collective-permute-start.8 = (bf16[4,8,1792]{2,1,0:T(8,128)(2,1)S(1)}, bf16[4,8,1792]{2,1,0:T(8,128)(2,1)S(1)}, u32[]{:S(2)}, u32[]{:S(2)}) collective-permute-start(bf16[4,8,1792]{2,1,0:T(8,128)(2,1)S(1)} %fusion.4), channel_id=1, source_target_pairs={{0,1},{1,0},{2,3},{3,2},{4,5},{5,4},{6,7},{7,6},{8,9},{9,8},{10,11... | collective-permute-start | bytes 344072 | tf_op jit(solution)/shard_map/ppermute | solution.py:30
Sparse Core Ops, SparseCore 0:
  9.4 74.0 all-gather.1

commit v5 on v4

--- a/solution.py
+++ b/solution.py
@@ -71,34 +71,34 @@
     )(order, content, rotary)
 
 
-def query_kernel(content, rotary, key_up, out):
-    head = pl.program_id(0)
-    latent = lax.dot_general(
-        content[...], key_up[...], (((1,), (1,)), ((), ())), preferred_element_type=jnp.float32
-    )
-    out[0, :, : latent.shape[1]] = latent.astype(out.dtype)
-    pair = rotary[...]
-    half = pair.shape[1] // 2
-    out[0, :, latent.shape[1] :] = jnp.where(head % 2 == 0, pair[:, :half], pair[:, half:])
+def query_kernel(payload, key_up, out, *, heads, nope, rope):
+    latent = key_up.shape[0]
+    for h in range(heads):
+        cols = slice(h * nope, (h + 1) * nope)
+        out[h, :latent, :] = lax.dot_general(
+            key_up[:, cols],
+            payload[:, cols],
+            (((1,), (1,)), ((), ())),
+            preferred_element_type=jnp.float32,
+        ).astype(out.dtype)
+    for p in range(heads // 2):
+        cols = slice(heads * nope + 2 * p * rope, heads * nope + 2 * (p + 1) * rope)
+        both = payload[:, cols].astype(jnp.float32).T.astype(out.dtype)
+        out[2 * p, latent:, :] = both[:rope]
+        out[2 * p + 1, latent:, :] = both[rope:]
 
 
 def latent_queries(payload, key_up, heads, nope, rope):
     rows = payload.shape[0]
     latent = key_up.shape[0]
     return pl.pallas_call(
-        query_kernel,
-        grid=(heads,),
-        in_specs=[
-            pl.BlockSpec((rows, nope), lambda i: (0, i)),
-            pl.BlockSpec((rows, 2 * rope), lambda i: (0, heads * nope // (2 * rope) + i // 2)),
-            pl.BlockSpec((latent, nope), lambda i: (0, i)),
-        ],
-        out_specs=pl.BlockSpec((1, rows, latent + rope), lambda i: (i, 0, 0)),
-        out_shape=jax.ShapeDtypeStruct((heads, rows, latent + rope), jnp.bfloat16),
+        functools.partial(query_kernel, heads=heads, nope=nope, rope=rope),
+        out_shape=jax.ShapeDtypeStruct((heads, latent + rope, rows), jnp.bfloat16),
+        compiler_params=pltpu.CompilerParams(vmem_limit_bytes=48 * 1024 * 1024),
         cost_estimate=pl.CostEstimate(
             flops=2 * heads * rows * latent * nope, bytes_accessed=8 * 1024 * 1024, transcendentals=0
         ),
-    )(payload, payload, key_up)
+    )(payload, key_up)
 
 
 def three_parts(x):
@@ -115,123 +115,117 @@
     return stats[:, :heads] + stats[:, heads : 2 * heads] + stats[:, 2 * heads : 3 * heads]
 
 
-def write_stats(rows, lse):
-    heads = lse.shape[1]
-    empty = jnp.zeros((lse.shape[0], STATS - 3 * heads), jnp.float32)
-    rows[:, rows.shape[1] - STATS :] = jnp.concatenate(three_parts(lse) + [empty], axis=1).astype(
-        rows.dtype
-    )
-
-
 def attend_kernel(
-    starts, bases, limit_ref, query, *rest, shards, coef, latent, block, heads, groups, with_before
+    starts, bases, limit_ref, query, *rest, shards, coef, block, some, with_before
 ):
-    *keys, value_up, before, out, mixed = rest
-    group = pl.program_id(0)
-    rows = heads * block
+    *keys, value_up, before, out, turned, lses, olds = rest
+    first = pl.program_id(0) * some
+    heads, tokens = lses.shape
+    value_dim, latent = value_up.shape[1:]
     width = keys[0].shape[2]
+    tiles = [(r, i) for r in keys for i in range(r.shape[0])]
+    columns = some * tokens
     limit = limit_ref[0]
-    lowest, highest = bases[0], bases[0]
+    left = out.shape[1] - STATS
+
+    @pl.when(first == 0)
+    def _():
+        for n, (r, i) in enumerate(tiles):
+            turned[n * width : (n + 1) * width, :] = r[i].T
+        if with_before:
+            stats = before[:, left:].astype(jnp.float32).T
+            olds[...] = stats[:heads] + stats[heads : 2 * heads] + stats[2 * heads : 3 * heads]
+
+    highest, nearest = bases[0], starts[0]
     for i in range(1, shards):
-        lowest = jnp.minimum(lowest, bases[i])
         highest = jnp.maximum(highest, bases[i])
-
-    def write(half, normal, lse):
-        at = pl.ds(group * 2 * block + half * block, block)
-        mixed[:, at, :] = normal.astype(mixed.dtype).reshape(heads, block, latent)
-        lane = lax.broadcasted_iota(jnp.int32, (block, STATS), 1)
-        parts = three_parts(lse)
-        stats = jnp.zeros((block, STATS), jnp.float32)
-        for k, part in enumerate(parts):
-            for h in range(heads):
-                stats = jnp.where(
-                    lane == k * heads + h, part[h * block : (h + 1) * block, :], stats
-                )
-        out[at, out.shape[1] - STATS :] = stats.astype(out.dtype)
-
-    def run(half, masked):
-        rows_q = query[:, half * block : (half + 1) * block, :].reshape(rows, -1)
-        k = jnp.concatenate([r[i] for r in keys for i in range(r.shape[0])], axis=1)
-        s = jnp.dot(rows_q, k, preferred_element_type=jnp.float32)
+    for i in range(1, tokens // block):
+        nearest = jnp.minimum(nearest, starts[i])
+    sure = highest + width - 1 <= jnp.minimum(nearest, limit - 1)
+
+    def run(masked):
+        q = jnp.concatenate([query[i] for i in range(some)], axis=1)
+        s = jnp.dot(turned[...], q, preferred_element_type=jnp.float32)
         if masked:
-            token = lax.broadcasted_iota(jnp.int32, (rows, width), 0) % block
-            last = jnp.minimum(starts[group * 2 + half] + token, limit - 1)
-            lane = lax.broadcasted_iota(jnp.int32, (rows, width), 1)
+            token = lax.broadcasted_iota(jnp.int32, (1, columns), 1) % tokens
+            last = token % block
+            for i in range(tokens // block):
+                last = last + jnp.where(token // block == i, starts[i], 0)
+            last = jnp.minimum(last, limit - 1)
+            row = lax.broadcasted_iota(jnp.int32, (width, columns), 0)
             s = jnp.concatenate(
                 [
-                    jnp.where(lane + bases[i] <= last, s[:, i * width : (i + 1) * width], NEG)
-                    for i in range(shards)
+                    jnp.where(row + bases[n] <= last, s[n * width : (n + 1) * width], NEG)
+                    for n in range(shards)
                 ],
-                axis=1,
+                axis=0,
             )
-        top = jnp.max(s, axis=1, keepdims=True)
+        top = jnp.max(s, axis=0, keepdims=True)
         if masked:
             top = jnp.maximum(top, NEG / 10)
         weights = jnp.exp2(s * coef - top * coef)
-        total = jnp.sum(weights, axis=1, keepdims=True)
-        values = lax.dot_general(
-            weights.astype(jnp.bfloat16),
-            k[:latent],
-            (((1,), (1,)), ((), ())),
-            preferred_element_type=jnp.float32,
-        )
+        total = jnp.sum(weights, axis=0, keepdims=True)
+        k = jnp.concatenate([r[i, :latent] for r, i in tiles], axis=1)
+        values = jnp.dot(k, weights.astype(jnp.bfloat16), preferred_element_type=jnp.float32)
         if masked:
-            some = total > 0
-            safe = jnp.where(some, total, 1.0)
-            write(half, values / safe, jnp.where(some, top * coef + jnp.log2(safe), NEG))
+            seen = total > 0
+            total = jnp.where(seen, total, 1.0)
+            lse = jnp.where(seen, top * coef + jnp.log2(total), NEG)
         else:
-            write(half, values / total, top * coef + jnp.log2(total))
-
-    for half in range(2):
-        start = starts[group * 2 + half]
-        sure = highest + width - 1 <= jnp.minimum(start, limit - 1)
-        some = lowest <= jnp.minimum(start + block - 1, limit - 1)
-
-        @pl.when(sure)
-        def _():
-            run(half, False)
-
-        @pl.when(jnp.logical_and(some, jnp.logical_not(sure)))
-        def _():
-            run(half, True)
-
-        @pl.when(jnp.logical_not(some))
-        def _():
-            write(half, jnp.zeros((rows, latent), jnp.float32), jnp.full((rows, 1), NEG))
-
-    @pl.when(group == groups - 1)
+            lse = top * coef + jnp.log2(total)
+        mixed = (values * (1.0 / total)).astype(jnp.bfloat16)
+        mine = [lse[:, i * tokens : (i + 1) * tokens] for i in range(some)]
+        new = [None] * some
+        if with_before:
+            old = []
+            for i in range(some):
+                past = olds[pl.ds(first + i, 1), :]
+                peak = jnp.maximum(past, mine[i])
+                a, b = jnp.exp2(past - peak), jnp.exp2(mine[i] - peak)
+                old.append(a / (a + b))
+                new[i] = b / (a + b)
+                mine[i] = peak + jnp.log2(a + b)
+            old = jnp.concatenate(old + [jnp.zeros((8 - some, tokens), jnp.float32)], axis=0).T
+        for i in range(some):
+            lses[pl.ds(first + i, 1), :] = mine[i]
+            value = jnp.dot(
+                value_up[i], mixed[:, i * tokens : (i + 1) * tokens], preferred_element_type=jnp.float32
+            )
+            if with_before:
+                value = value * new[i]
+            value = value.T
+            cols = pl.ds(pl.multiple_of((first + i) * value_dim, value_dim), value_dim)
+            if with_before:
+                value = value + before[:, cols].astype(jnp.float32) * old[:, i : i + 1]
+            out[:, cols] = value.astype(out.dtype)
+
+    @pl.when(sure)
     def _():
-        if with_before:
-            old, new = read_stats(before, heads), read_stats(out, heads)
-            top = jnp.maximum(old, new)
-            old, new = jnp.exp2(old - top), jnp.exp2(new - top)
-            total = old + new
-            old, new = old / total, new / total
-            write_stats(out, top + jnp.log2(total))
-        for h in range(heads):
-            cols = slice(h * 128, (h + 1) * 128)
-            value = jnp.dot(mixed[h], value_up[:, cols], preferred_element_type=jnp.float32)
-            if with_before:
-                value = value * new[:, h : h + 1]
-                value = value + before[:, cols].astype(jnp.float32) * old[:, h : h + 1]
-            out[:, cols] = value.astype(out.dtype)
-
-
-def attend(starts, bases, limit, query, keys, value_up, scale, before=None):
-    heads, tokens, depth = query.shape
-    latent, value_width = value_up.shape
+        run(False)
+
+    @pl.when(jnp.logical_not(sure))
+    def _():
+        run(True)
+
+    @pl.when(first + some == heads)
+    def _():
+        empty = jnp.zeros((STATS - 3 * heads, tokens), jnp.float32)
+        stats = jnp.concatenate(three_parts(lses[...]) + [empty], axis=0)
+        out[:, left:] = stats.T.astype(out.dtype)
+
+
+def attend(starts, bases, limit, query, keys, value_up, scale, before=None, some=4):
+    heads, depth, tokens = query.shape
+    value_dim, latent = value_up.shape[1:]
     shards = sum(k.shape[0] for k in keys)
-    groups = starts.shape[0] // 2
-    per_group = tokens // groups
+    width = keys[0].shape[2]
     whole = lambda shape: pl.BlockSpec(shape, lambda i, *_: (0,) * len(shape))
     kernel = functools.partial(
         attend_kernel,
         shards=shards,
         coef=scale * LOG2E,
-        latent=latent,
-        block=per_group // 2,
-        heads=heads,
-        groups=groups,
+        block=tokens // starts.shape[0],
+        some=some,
         with_before=before is not None,
     )
     if before is None:
@@ -240,14 +234,19 @@
         kernel,
         grid_spec=pltpu.PrefetchScalarGridSpec(
             num_scalar_prefetch=3,
-            grid=(groups,),
-            in_specs=[pl.BlockSpec((heads, per_group, depth), lambda i, *_: (0, i, 0))]
+            grid=(heads // some,),
+            in_specs=[pl.BlockSpec((some, depth, tokens), lambda i, *_: (i, 0, 0))]
             + [whole(k.shape) for k in keys]
-            + [whole(value_up.shape), whole(before.shape)],
-            out_specs=whole((tokens, value_width + STATS)),
-            scratch_shapes=[pltpu.VMEM((heads, tokens, latent), jnp.bfloat16)],
+            + [pl.BlockSpec((some, value_dim, latent), lambda i, *_: (i, 0, 0))]
+            + [whole(before.shape)],
+            out_specs=whole((tokens, heads * value_dim + STATS)),
+            scratch_shapes=[
+                pltpu.VMEM((shards * width, depth), jnp.bfloat16),
+                pltpu.VMEM((heads, tokens), jnp.float32),
+                pltpu.VMEM((heads, tokens), jnp.float32),
+            ],
         ),
-        out_shape=jax.ShapeDtypeStruct((tokens, value_width + STATS), jnp.bfloat16),
+        out_shape=jax.ShapeDtypeStruct((tokens, heads * value_dim + STATS), jnp.bfloat16),
         compiler_params=pltpu.CompilerParams(vmem_limit_bytes=48 * 1024 * 1024),
     )(starts, bases, limit, query, *keys, value_up, before)
 
@@ -295,7 +294,6 @@
     tokens, heads, nope = query_content.shape
     latent = key_up.shape[0]
     rope = query_rotary.shape[1] // heads
-    value_dim = value_up.shape[2]
     columns = output_weight.shape[1]
     block = tokens // 2
     scale = 1.0 / math.sqrt(nope + rope)
@@ -308,14 +306,16 @@
 
     pair = jnp.stack([key_cache, other_core(key_cache)])
     one, two = along_z(pair, 1), along_z(pair, 2)
-    two, _ = lax.optimization_barrier((two, packed))
+    key_up = key_up.reshape(latent, heads * nope)
+    value_up = value_up.transpose(1, 2, 0)
+    two, _, key_up, value_up = lax.optimization_barrier((two, packed, key_up, value_up))
     near = jnp.concatenate([one, two], axis=0)
     near_swapped = other_core(near)
     three, four = along_z(two, 1), along_z(two[:1], 2)
 
     payload = swap_y(packed).reshape(4 * tokens, -1)
     starts = query_start[0] + payload[::block, -1].astype(jnp.int32) * block
-    queries = latent_queries(payload, key_up.reshape(latent, heads * nope), heads, nope, rope)
+    queries = latent_queries(payload, key_up, heads, nope, rope)
 
     side = 1 - 2 * c
 
@@ -326,7 +326,7 @@
 
     attend_part = functools.partial(
         attend, starts, limit=key_limit, query=queries, scale=scale,
-        value_up=value_up.reshape(latent, heads * value_dim),
+        value_up=value_up,
     )
     partial = attend_part(
         bases_of([0, 0, 1, 1, 2, 2, -1, -1, -2, -2], [0, 1, 0, 1, 0, 1, 1, 0, 1, 0]),

time: 172 us -> 161 us (0.936)
  the two profiles are of different devices: /device:TPU:32 before, /device:TPU:64 now
where the time goes in v5:
time: 161 us
  starting transfers between devices  49.1 us (30%)
  blocking collectives  29.8 us (19%)
  waiting for transfers between devices  28.3 us (18%)
  Pallas kernels  23.5 us (15%)
  between operations  15 us (9%)
  local copies, waits for them, and re-layouts  9.52 us (6%)
  matrix products  2.98 us (2%)
  other arithmetic  2.32 us (1%)
    ppermute x9, starting transfers between devices, permute(): return lax.ppermute(x, names, pairs)  39.7 us
    all_to_all x2, blocking collectives, swap_y(): return lax.all_to_all(x, 'y', split_axis=0, concat_axis=0, tiled=True)  29.8 us
    pallas_call x2, Pallas kernels, attend(): pl.pallas_call(kernel, grid_spec=pltpu.PrefetchScalarGridSpec(num_scalar_...  17.8 us
    all_to_all x1, waiting for transfers between devices, per_device(): lax.all_to_all(product.reshape(16, 2 * share, width), ('y', 'x'), split_a...  15.5 us
    ppermute x9, waiting for transfers between devices, permute(): return lax.ppermute(x, names, pairs)  12.1 us
    all_to_all x1, starting transfers between devices, per_device(): lax.all_to_all(product.reshape(16, 2 * share, width), ('y', 'x'), split_a...  4.92 us
    unnamed x20, local copies, waits for them, and re-layouts  4.73 us
    all_to_all x1, starting transfers between devices, swap_y(): return lax.all_to_all(x, 'y', split_axis=0, concat_axis=0, tiled=True)  4.46 us
  transfers between devices with their start and end apart: 12, of which 4 were waited for; matrix products, arithmetic and copies ran while one was open for 7% of the time, Pallas kernels for 15%

profile of v5, /device:TPU:64, one launch (start us, length us, event | category | flops | bytes accessed | tf_op | source)
XLA Modules:
  0.0 160.5 jit_solution(435715087632290331)
XLA Ops:
  7.3 1.9 %collective-permute-start = (bf16[576,128]{1,0:T(8,128)(2,1)}, bf16[576,128]{1,0:T(8,128)(2,1)S(1)}, u32[]{:S(2)}, u32[]{:S(2)}) collective-permute-start(bf16[576,128]{1,0:T(8,128)(2,1)} %param.15), channel_id=1, source_target_pairs={{0,8},{8,0},{1,9},{9,1},{2,10},{10,2},{3,11},{11,3},{4,12},{12,4},... | collective-permute-start | bytes 442376 | tf_op jit(solution)/shard_map/ppermute | solution.py:30
  9.2 1.5 collective-permute-done
  10.7 0.9 pad_maximum_fusion.1.rest_0_
  11.7 6.4 %collective-permute-start.1 = (bf16[2,576,128]{2,1,0:T(8,128)(2,1)S(1)}, bf16[2,576,128]{2,1,0:T(8,128)(2,1)S(1)}, u32[]{:S(2)}, u32[]{:S(2)}) collective-permute-start(bf16[2,576,128]{2,1,0:T(8,128)(2,1)S(1)} %pad_maximum_fusion.1.rest_0_), channel_id=1, source_target_pairs={{0,32},{1,33},{8,105},{9,104},{16,48},{17,49},{24,121},{25,120},{3... | collective-permute-start | bytes 884744 | tf_op jit(solution)/shard_map/ppermute | solution.py:30
  18.1 3.8 %collective-permute-start.4 = (bf16[2,576,128]{2,1,0:T(8,128)(2,1)S(1)}, bf16[2,576,128]{2,1,0:T(8,128)(2,1)}, u32[]{:S(2)}, u32[]{:S(2)}) collective-permute-start(bf16[2,576,128]{2,1,0:T(8,128)(2,1)S(1)} %pad_maximum_fusion.1.rest_0_), channel_id=1, source_target_pairs={{0,16},{1,17},{8,121},{9,120},{16,32},{17,33},{24,8},{25,9},{32,48... | collective-permute-start | bytes 884744 | tf_op jit(solution)/shard_map/ppermute | solution.py:30
  21.9 2.6 %shard_map.127 = bf16[4,64,1664]{2,1,0:T(8,128)(2,1)} custom-call(s32[2]{0:T(128)} %order.1, bf16[64,8,128]{2,1,0:T(8,128)(2,1)} %content.1, bf16[64,512]{1,0:T(8,128)(2,1)} %rotary.1), custom_call_target="tpu_custom_call" | custom-call | tf_op jit(solution)/shard_map/pallas_call | solution.py:66
  24.5 4.5 %all-to-all-start = ((bf16[4,64,1664]{2,1,0:T(8,128)(2,1)}), bf16[4,64,1664]{2,1,0:T(8,128)(2,1)S(1)}, u32[]{:S(2)}, u32[]{:S(2)}) async-start(bf16[4,64,1664]{2,1,0:T(8,128)(2,1)} %shard_map.127), calls=%async_computation | async-start | bytes 1703936 | tf_op jit(solution)/shard_map/all_to_all | solution.py:46
  29.3 1.6 %copy.21 = bf16[512,8,128]{0,2,1:T(8,128)(2,1)S(1)} copy(bf16[512,8,128]{2,1,0:T(8,128)(2,1)} %param.17) | data formatting | bytes 2097152 | tf_op args[4]
  31.7 1.0 constant_dynamic-update-slice_fusion.1
  32.7 1.0 constant_dynamic-update-slice_fusion.rest_1_
  33.7 4.0 %collective-permute-start.5 = (bf16[4,576,128]{2,1,0:T(8,128)(2,1)S(1)}, bf16[4,576,128]{2,1,0:T(8,128)(2,1)}, u32[]{:S(2)}, u32[]{:S(2)}) collective-permute-start(bf16[4,576,128]{2,1,0:T(8,128)(2,1)S(1)} %constant_dynamic-update-slice_fusion.rest_1_), channel_id=1, source_target_pairs={{0,8},{8,0},{1,9},{9,1},{2,10},{10,2},{3,11},{11,3},{4,12},{12,4},... | collective-permute-start | bytes 1769480 | tf_op jit(solution)/shard_map/ppermute | solution.py:30
  37.7 1.9 %collective-permute-start.2 = (bf16[2,576,128]{2,1,0:T(8,128)(2,1)}, bf16[2,576,128]{2,1,0:T(8,128)(2,1)}, u32[]{:S(2)}, u32[]{:S(2)}) collective-permute-start(bf16[2,576,128]{2,1,0:T(8,128)(2,1)} %copy-done.3), channel_id=1, source_target_pairs={{0,16},{1,17},{8,121},{9,120},{16,32},{17,33},{24,8},{25,9},{32,48... | collective-permute-start | bytes 884744 | tf_op jit(solution)/shard_map/ppermute | solution.py:30
  39.6 1.6 slice.15
  41.2 6.2 %collective-permute-start.3 = (bf16[1,576,128]{2,1,0:T(8,128)(2,1)}, bf16[1,576,128]{2,1,0:T(8,128)(2,1)}, u32[]{:S(2)}, u32[]{:S(2)}) collective-permute-start(bf16[1,576,128]{2,1,0:T(8,128)(2,1)} %slice.15), channel_id=1, source_target_pairs={{0,32},{1,33},{8,105},{9,104},{16,48},{17,49},{24,121},{25,120},{3... | collective-permute-start | bytes 442376 | tf_op jit(solution)/shard_map/ppermute | solution.py:30
  49.9 11.0 %shard_map.129.rest_3_ = bf16[256,1152]{1,0:T(8,128)(2,1)S(1)} custom-call(s32[8]{0:T(128)S(1)} %add_reduce_fusion.starts, s32[10]{0:T(128)S(1)} %fusion.9.bases, s32[1]{0:T(128)S(6)} %copy.34.limit_ref, bf16[8,576,256]{2,1,0:T(8,128)(2,1)S(1)} %shard_map.128.query, bf16[2,576,128]{2,1,0:T(8,128)(2,1)S(1)} %copy-done.1, ...), custom_call_target="tpu_custom_call" | custom-call | tf_op jit(solution)/shard_map/pallas_call | solution.py:233
  60.9 1.0 constant_dynamic-update-slice_fusion.3
  61.8 0.9 constant_dynamic-update-slice_fusion.2.rest_0_
  62.8 4.6 %collective-permute-start.6 = (bf16[3,576,128]{2,1,0:T(8,128)(2,1)S(1)}, bf16[3,576,128]{2,1,0:T(8,128)(2,1)S(1)}, u32[]{:S(2)}, u32[]{:S(2)}) collective-permute-start(bf16[3,576,128]{2,1,0:T(8,128)(2,1)S(1)} %constant_dynamic-update-slice_fusion.2.rest_0_), channel_id=1, source_target_pairs={{0,8},{8,0},{1,9},{9,1},{2,10},{10,2},{3,11},{11,3},{4,12},{12,4},... | collective-permute-start | bytes 1327112 | tf_op jit(solution)/shard_map/ppermute | solution.py:30
  67.4 1.2 collective-permute-done.6.rest_1_
  68.6 6.9 %shard_map.130 = bf16[256,1152]{1,0:T(8,128)(2,1)S(1)} custom-call(s32[8]{0:T(128)S(1)} %add_reduce_fusion.starts, s32[6]{0:T(128)S(1)} %fusion.10.bases, s32[1]{0:T(128)S(6)} %copy.34.limit_ref, bf16[8,576,256]{2,1,0:T(8,128)(2,1)S(1)} %shard_map.128.query, bf16[3,576,128]{2,1,0:T(8,128)(2,1)S(1)} %constant_dynamic-update-slice_fusion.2.rest_0_, ...), custom_call_target="tpu_custom_call" | custom-call | tf_op jit(solution)/shard_map/pallas_call | solution.py:233
  75.5 15.9 %all_to_all.20.parts = bf16[4,64,1152]{2,1,0:T(8,128)(2,1)} all-to-all(bf16[4,64,1152]{2,1,0:T(8,128)(2,1)S(1)} %bitcast.51), channel_id=1, replica_groups=mesh['y'=4,'z'=8,'c'=2,'x'=4,'h'=2] {'y'}, dimensions={0} | all-to-all | bytes 1179648 | tf_op jit(solution)/shard_map/all_to_all | solution.py:46
  91.4 2.4 %shard_map.131 = bf16[4,64,1024]{2,1,0:T(8,128)(2,1)} custom-call(bf16[4,64,1152]{2,1,0:T(8,128)(2,1)} %all_to_all.20.parts), custom_call_target="tpu_custom_call" | custom-call | tf_op jit(solution)/shard_map/pallas_call | solution.py:277
  93.8 1.9 %collective-permute-start.7 = (bf16[896,1024]{1,0:T(8,128)(2,1)}, bf16[896,1024]{1,0:T(8,128)(2,1)S(1)}, u32[]{:S(2)}, u32[]{:S(2)}) collective-permute-start(bf16[896,1024]{1,0:T(8,128)(2,1)} %all-gather.2.cloned.1.call-done), channel_id=1, source_target_pairs={{0,8},{8,0},{1,9},{9,1},{2,10},{10,2},{3,11},{11,3},{4,12},{12,4},... | collective-permute-start | bytes 5505032 | tf_op jit(solution)/shard_map/ppermute | solution.py:30
  95.7 13.9 %all_to_all.21 = bf16[4,64,1024]{2,1,0:T(8,128)(2,1)S(1)} all-to-all(bf16[4,64,1024]{2,1,0:T(8,128)(2,1)} %shard_map.131), channel_id=1, replica_groups=mesh['y'=4,'z'=8,'c'=2,'x'=4,'h'=2] {'y'}, dimensions={0} | all-to-all | bytes 1048576 | tf_op jit(solution)/shard_map/all_to_all | solution.py:46
  109.5 2.2 %convolution_convert_fusion.1 = bf16[256,896]{1,0:T(8,128)(2,1)S(1)} fusion(bf16[256,1024]{1,0:T(8,128)(2,1)S(1)} %bitcast.54, bf16[896,1024]{1,0:T(8,128)(2,1)} %all-gather.2.cloned.1.call-done), kind=kOutput, calls=%fused_computation.2 | convolution fusion | flops 469991424 | bytes 2818048 | tf_op jit(solution)/shard_map/dot_general | solution.py:349
  111.8 0.7 convolution_convert_fusion
  112.6 1.0 pad_maximum_fusion
  113.6 4.9 %all-to-all-start.3 = ((bf16[16,16,1792]{2,1,0:T(8,128)(2,1)}), bf16[16,16,1792]{2,1,0:T(8,128)(2,1)S(1)}, u32[]{:S(2)}, u32[]{:S(2)}) async-start(bf16[16,16,1792]{2,1,0:T(8,128)(2,1)} %bitcast.8), calls=%async_computation.3 | async-start | bytes 1835008 | tf_op jit(solution)/shard_map/all_to_all | solution.py:358
  118.5 15.5 %all-to-all-done.3 = bf16[16,16,1792]{2,1,0:T(8,128)(2,1)S(1)} async-done(((bf16[16,16,1792]{2,1,0:T(8,128)(2,1)}), bf16[16,16,1792]{2,1,0:T(8,128)(2,1)S(1)}, u32[]{:S(2)}, u32[]{:S(2)}) %all-to-all-start.3) | async-done | bytes 917536 | tf_op jit(solution)/shard_map/all_to_all | solution.py:358
  134.2 8.9 %collective-permute-start.8 = (bf16[4,8,1792]{2,1,0:T(8,128)(2,1)S(1)}, bf16[4,8,1792]{2,1,0:T(8,128)(2,1)S(1)}, u32[]{:S(2)}, u32[]{:S(2)}) collective-permute-start(bf16[4,8,1792]{2,1,0:T(8,128)(2,1)S(1)} %fusion.4), channel_id=1, source_target_pairs={{0,1},{1,0},{2,3},{3,2},{4,5},{5,4},{6,7},{7,6},{8,9},{9,8},{10,11... | collective-permute-start | bytes 344072 | tf_op jit(solution)/shard_map/ppermute | solution.py:30
  143.1 9.4 %collective-permute-done.8 = bf16[4,8,1792]{2,1,0:T(8,128)(2,1)S(1)} collective-permute-done((bf16[4,8,1792]{2,1,0:T(8,128)(2,1)S(1)}, bf16[4,8,1792]{2,1,0:T(8,128)(2,1)S(1)}, u32[]{:S(2)}, u32[]{:S(2)}) %collective-permute-start.8) | collective-permute-done | bytes 114720 | tf_op jit(solution)/shard_map/ppermute | solution.py:30
  152.8 0.8 reshape.40
  (39 shorter events, 3.4 us)
Async XLA Ops:
  6.5 22.5 %copy-start.2 = (bf16[512,8,128]{2,1,0:T(8,128)(2,1)S(1)}, bf16[512,8,128]{2,1,0:T(8,128)(2,1)}, u32[]{:S(2)}) copy-start(bf16[512,8,128]{2,1,0:T(8,128)(2,1)} %param.16) | copy-start | bytes 3145732
  6.5 87.2 %all-gather.2.cloned.1.call-start = ((), (), s32[]{:S(2)}) async-start(), calls=%async_computation.4 | async-start | bytes 2064384 | tf_op jit(solution)/shard_map/all_gather | solution.py:303
  7.3 3.5 %collective-permute-start = (bf16[576,128]{1,0:T(8,128)(2,1)}, bf16[576,128]{1,0:T(8,128)(2,1)S(1)}, u32[]{:S(2)}, u32[]{:S(2)}) collective-permute-start(bf16[576,128]{1,0:T(8,128)(2,1)} %param.15), channel_id=1, source_target_pairs={{0,8},{8,0},{1,9},{9,1},{2,10},{10,2},{3,11},{11,3},{4,12},{12,4},... | collective-permute-start | bytes 442376 | tf_op jit(solution)/shard_map/ppermute | solution.py:30
  11.7 17.6 %copy-start = (bf16[2,576,128]{2,1,0:T(8,128)(2,1)}, bf16[2,576,128]{2,1,0:T(8,128)(2,1)S(1)}, u32[]{:S(2)}) copy-start(bf16[2,576,128]{2,1,0:T(8,128)(2,1)S(1)} %pad_maximum_fusion.1.rest_0_) | copy-start | bytes 884740
  11.7 19.3 %collective-permute-start.1 = (bf16[2,576,128]{2,1,0:T(8,128)(2,1)S(1)}, bf16[2,576,128]{2,1,0:T(8,128)(2,1)S(1)}, u32[]{:S(2)}, u32[]{:S(2)}) collective-permute-start(bf16[2,576,128]{2,1,0:T(8,128)(2,1)S(1)} %pad_maximum_fusion.1.rest_0_), channel_id=1, source_target_pairs={{0,32},{1,33},{8,105},{9,104},{16,48},{17,49},{24,121},{25,120},{3... | collective-permute-start | bytes 884744 | tf_op jit(solution)/shard_map/ppermute | solution.py:30
  18.1 13.6 %collective-permute-start.4 = (bf16[2,576,128]{2,1,0:T(8,128)(2,1)S(1)}, bf16[2,576,128]{2,1,0:T(8,128)(2,1)}, u32[]{:S(2)}, u32[]{:S(2)}) collective-permute-start(bf16[2,576,128]{2,1,0:T(8,128)(2,1)S(1)} %pad_maximum_fusion.1.rest_0_), channel_id=1, source_target_pairs={{0,16},{1,17},{8,121},{9,120},{16,32},{17,33},{24,8},{25,9},{32,48... | collective-permute-start | bytes 884744 | tf_op jit(solution)/shard_map/ppermute | solution.py:30
  24.5 24.2 %all-to-all-start = ((bf16[4,64,1664]{2,1,0:T(8,128)(2,1)}), bf16[4,64,1664]{2,1,0:T(8,128)(2,1)S(1)}, u32[]{:S(2)}, u32[]{:S(2)}) async-start(bf16[4,64,1664]{2,1,0:T(8,128)(2,1)} %shard_map.127), calls=%async_computation | async-start | bytes 1703936 | tf_op jit(solution)/shard_map/all_to_all | solution.py:46
  29.3 18.2 %copy-start.6 = (s32[10]{0:T(128)S(1)}, s32[10]{0:T(128)}, u32[]{:S(2)}) copy-start(s32[10]{0:T(128)} %constant.78.clone) | copy-start | bytes 124
  29.3 18.2 %copy-start.7 = (s32[10]{0:T(128)S(1)}, s32[10]{0:T(128)}, u32[]{:S(2)}) copy-start(s32[10]{0:T(128)} %constant.77.clone) | copy-start | bytes 124
  31.0 0.7 copy-start.3
  33.7 16.0 %collective-permute-start.5 = (bf16[4,576,128]{2,1,0:T(8,128)(2,1)S(1)}, bf16[4,576,128]{2,1,0:T(8,128)(2,1)}, u32[]{:S(2)}, u32[]{:S(2)}) collective-permute-start(bf16[4,576,128]{2,1,0:T(8,128)(2,1)S(1)} %constant_dynamic-update-slice_fusion.rest_1_), channel_id=1, source_target_pairs={{0,8},{8,0},{1,9},{9,1},{2,10},{10,2},{3,11},{11,3},{4,12},{12,4},... | collective-permute-start | bytes 1769480 | tf_op jit(solution)/shard_map/ppermute | solution.py:30
  37.7 23.2 %collective-permute-start.2 = (bf16[2,576,128]{2,1,0:T(8,128)(2,1)}, bf16[2,576,128]{2,1,0:T(8,128)(2,1)}, u32[]{:S(2)}, u32[]{:S(2)}) collective-permute-start(bf16[2,576,128]{2,1,0:T(8,128)(2,1)} %copy-done.3), channel_id=1, source_target_pairs={{0,16},{1,17},{8,121},{9,120},{16,32},{17,33},{24,8},{25,9},{32,48... | collective-permute-start | bytes 884744 | tf_op jit(solution)/shard_map/ppermute | solution.py:30
  41.2 19.6 %collective-permute-start.3 = (bf16[1,576,128]{2,1,0:T(8,128)(2,1)}, bf16[1,576,128]{2,1,0:T(8,128)(2,1)}, u32[]{:S(2)}, u32[]{:S(2)}) collective-permute-start(bf16[1,576,128]{2,1,0:T(8,128)(2,1)} %slice.15), channel_id=1, source_target_pairs={{0,32},{1,33},{8,105},{9,104},{16,48},{17,49},{24,121},{25,120},{3... | collective-permute-start | bytes 442376 | tf_op jit(solution)/shard_map/ppermute | solution.py:30
  48.9 1.0 copy-start.1
  49.9 17.5 %copy-start.4 = (s32[6]{0:T(128)S(1)}, s32[6]{0:T(128)}, u32[]{:S(2)}) copy-start(s32[6]{0:T(128)} %constant.80.clone) | copy-start | bytes 76
  49.9 17.5 %copy-start.5 = (s32[6]{0:T(128)S(1)}, s32[6]{0:T(128)}, u32[]{:S(2)}) copy-start(s32[6]{0:T(128)} %constant.79.clone) | copy-start | bytes 76
  62.8 5.8 %collective-permute-start.6 = (bf16[3,576,128]{2,1,0:T(8,128)(2,1)S(1)}, bf16[3,576,128]{2,1,0:T(8,128)(2,1)S(1)}, u32[]{:S(2)}, u32[]{:S(2)}) collective-permute-start(bf16[3,576,128]{2,1,0:T(8,128)(2,1)S(1)} %constant_dynamic-update-slice_fusion.2.rest_0_), channel_id=1, source_target_pairs={{0,8},{8,0},{1,9},{9,1},{2,10},{10,2},{3,11},{11,3},{4,12},{12,4},... | collective-permute-start | bytes 1327112 | tf_op jit(solution)/shard_map/ppermute | solution.py:30
  93.8 18.0 %collective-permute-start.7 = (bf16[896,1024]{1,0:T(8,128)(2,1)}, bf16[896,1024]{1,0:T(8,128)(2,1)S(1)}, u32[]{:S(2)}, u32[]{:S(2)}) collective-permute-start(bf16[896,1024]{1,0:T(8,128)(2,1)} %all-gather.2.cloned.1.call-done), channel_id=1, source_target_pairs={{0,8},{8,0},{1,9},{9,1},{2,10},{10,2},{3,11},{11,3},{4,12},{12,4},... | collective-permute-start | bytes 5505032 | tf_op jit(solution)/shard_map/ppermute | solution.py:30
  113.6 20.4 %all-to-all-start.3 = ((bf16[16,16,1792]{2,1,0:T(8,128)(2,1)}), bf16[16,16,1792]{2,1,0:T(8,128)(2,1)S(1)}, u32[]{:S(2)}, u32[]{:S(2)}) async-start(bf16[16,16,1792]{2,1,0:T(8,128)(2,1)} %bitcast.8), calls=%async_computation.3 | async-start | bytes 1835008 | tf_op jit(solution)/shard_map/all_to_all | solution.py:358
  134.2 18.3 %collective-permute-start.8 = (bf16[4,8,1792]{2,1,0:T(8,128)(2,1)S(1)}, bf16[4,8,1792]{2,1,0:T(8,128)(2,1)S(1)}, u32[]{:S(2)}, u32[]{:S(2)}) collective-permute-start(bf16[4,8,1792]{2,1,0:T(8,128)(2,1)S(1)} %fusion.4), channel_id=1, source_target_pairs={{0,1},{1,0},{2,3},{3,2},{4,5},{5,4},{6,7},{7,6},{8,9},{9,8},{10,11... | collective-permute-start | bytes 344072 | tf_op jit(solution)/shard_map/ppermute | solution.py:30
Sparse Core Ops, SparseCore 0:
  9.4 69.4 all-gather.1

commit v6 on v5

--- a/solution.py
+++ b/solution.py
@@ -71,8 +71,12 @@
     )(order, content, rotary)
 
 
-def query_kernel(payload, key_up, out, *, heads, nope, rope):
+def query_kernel(start, payload, key_up, out, starts, *, heads, nope, rope):
     latent = key_up.shape[0]
+    block = payload.shape[0] // starts.shape[0]
+    for i in range(starts.shape[0]):
+        number = payload[i * block : (i + 1) * block, payload.shape[1] - STATS :]
+        starts[i] = start[0] + jnp.max(number.astype(jnp.float32)).astype(jnp.int32) * block
     for h in range(heads):
         cols = slice(h * nope, (h + 1) * nope)
         out[h, :latent, :] = lax.dot_general(
@@ -88,17 +92,23 @@
         out[2 * p + 1, latent:, :] = both[rope:]
 
 
-def latent_queries(payload, key_up, heads, nope, rope):
+def latent_queries(start, payload, key_up, heads, nope, rope, blocks):
     rows = payload.shape[0]
     latent = key_up.shape[0]
+    smem, vmem = pl.BlockSpec(memory_space=pltpu.SMEM), pl.BlockSpec(memory_space=pltpu.VMEM)
     return pl.pallas_call(
         functools.partial(query_kernel, heads=heads, nope=nope, rope=rope),
-        out_shape=jax.ShapeDtypeStruct((heads, latent + rope, rows), jnp.bfloat16),
+        in_specs=[smem, vmem, vmem],
+        out_specs=[vmem, smem],
+        out_shape=[
+            jax.ShapeDtypeStruct((heads, latent + rope, rows), jnp.bfloat16),
+            jax.ShapeDtypeStruct((blocks,), jnp.int32),
+        ],
         compiler_params=pltpu.CompilerParams(vmem_limit_bytes=48 * 1024 * 1024),
         cost_estimate=pl.CostEstimate(
             flops=2 * heads * rows * latent * nope, bytes_accessed=8 * 1024 * 1024, transcendentals=0
         ),
-    )(payload, key_up)
+    )(start, payload, key_up)
 
 
 def three_parts(x):
@@ -116,7 +126,7 @@
 
 
 def attend_kernel(
-    starts, bases, limit_ref, query, *rest, shards, coef, block, some, with_before
+    starts, place, query, *rest, shards, coef, block, some, with_before
 ):
     *keys, value_up, before, out, turned, lses, olds = rest
     first = pl.program_id(0) * some
@@ -125,7 +135,11 @@
     width = keys[0].shape[2]
     tiles = [(r, i) for r in keys for i in range(r.shape[0])]
     columns = some * tokens
-    limit = limit_ref[0]
+    limit = place[3]
+    side = 1 - 2 * place[2]
+    bases = [
+        ((place[0] * 8 + (place[1] + 8 - side * step) % 8) * 2 + core) * width for step, core in shards
+    ]
     left = out.shape[1] - STATS
 
     @pl.when(first == 0)
@@ -137,7 +151,7 @@
             olds[...] = stats[:heads] + stats[heads : 2 * heads] + stats[2 * heads : 3 * heads]
 
     highest, nearest = bases[0], starts[0]
-    for i in range(1, shards):
+    for i in range(1, len(shards)):
         highest = jnp.maximum(highest, bases[i])
     for i in range(1, tokens // block):
         nearest = jnp.minimum(nearest, starts[i])
@@ -156,7 +170,7 @@
             s = jnp.concatenate(
                 [
                     jnp.where(row + bases[n] <= last, s[n * width : (n + 1) * width], NEG)
-                    for n in range(shards)
+                    for n in range(len(shards))
                 ],
                 axis=0,
             )
@@ -214,10 +228,9 @@
         out[:, left:] = stats.T.astype(out.dtype)
 
 
-def attend(starts, bases, limit, query, keys, value_up, scale, before=None, some=4):
+def attend(starts, place, query, keys, shards, value_up, scale, before=None, some=4):
     heads, depth, tokens = query.shape
     value_dim, latent = value_up.shape[1:]
-    shards = sum(k.shape[0] for k in keys)
     width = keys[0].shape[2]
     whole = lambda shape: pl.BlockSpec(shape, lambda i, *_: (0,) * len(shape))
     kernel = functools.partial(
@@ -233,7 +246,7 @@
     return pl.pallas_call(
         kernel,
         grid_spec=pltpu.PrefetchScalarGridSpec(
-            num_scalar_prefetch=3,
+            num_scalar_prefetch=2,
             grid=(heads // some,),
             in_specs=[pl.BlockSpec((some, depth, tokens), lambda i, *_: (i, 0, 0))]
             + [whole(k.shape) for k in keys]
@@ -241,14 +254,14 @@
             + [whole(before.shape)],
             out_specs=whole((tokens, heads * value_dim + STATS)),
             scratch_shapes=[
-                pltpu.VMEM((shards * width, depth), jnp.bfloat16),
+                pltpu.VMEM((len(shards) * width, depth), jnp.bfloat16),
                 pltpu.VMEM((heads, tokens), jnp.float32),
                 pltpu.VMEM((heads, tokens), jnp.float32),
             ],
         ),
         out_shape=jax.ShapeDtypeStruct((tokens, heads * value_dim + STATS), jnp.bfloat16),
         compiler_params=pltpu.CompilerParams(vmem_limit_bytes=48 * 1024 * 1024),
-    )(starts, bases, limit, query, *keys, value_up, before)
+    )(starts, place, query, *keys, value_up, before)
 
 
 def merge_kernel(parts, out, *, heads, sources):
@@ -280,6 +293,32 @@
     )(parts)
 
 
+def product_kernel(rows, mine, other, out):
+    step = pl.program_id(0)
+    width = mine.shape[0]
+    for n, weight in enumerate((mine, other)):
+        cols = pl.ds(pl.multiple_of(step * width + n * out.shape[1] // 2, width), width)
+        out[:, cols] = lax.dot_general(
+            rows[...], weight[...], (((1,), (1,)), ((), ())), preferred_element_type=jnp.float32
+        ).astype(out.dtype)
+
+
+def project(rows, mine, other, width=128):
+    tokens, depth = rows.shape
+    columns = mine.shape[0]
+    return pl.pallas_call(
+        product_kernel,
+        grid=(columns // width,),
+        in_specs=[
+            pl.BlockSpec((tokens, depth), lambda i: (0, 0)),
+            pl.BlockSpec((width, depth), lambda i: (i, 0)),
+            pl.BlockSpec((width, depth), lambda i: (i, 0)),
+        ],
+        out_specs=pl.BlockSpec((tokens, 2 * columns), lambda i: (0, 0)),
+        out_shape=jax.ShapeDtypeStruct((tokens, 2 * columns), jnp.bfloat16),
+    )(rows, mine, other)
+
+
 def per_device(
     query_content,
     query_rotary,
@@ -297,62 +336,42 @@
     columns = output_weight.shape[1]
     block = tokens // 2
     scale = 1.0 / math.sqrt(nope + rope)
-    shard = key_cache.shape[1]
     y, z, c, h = (lax.axis_index(n) for n in ("y", "z", "c", "h"))
 
     weight = lax.all_gather(output_weight.T, "z", axis=0, tiled=True)
 
     packed = pack(block_order, query_content, query_rotary, block, 4)
 
-    pair = jnp.stack([key_cache, other_core(key_cache)])
+    pair = lax.all_gather(key_cache, "c", axis=0, tiled=True).reshape(2, *key_cache.shape)
     one, two = along_z(pair, 1), along_z(pair, 2)
     key_up = key_up.reshape(latent, heads * nope)
     value_up = value_up.transpose(1, 2, 0)
-    two, _, key_up, value_up = lax.optimization_barrier((two, packed, key_up, value_up))
+    place = jnp.concatenate([jnp.stack([y, z, c]).astype(jnp.int32), key_limit])
+    two, _, key_up, value_up, place = lax.optimization_barrier(
+        (two, packed, key_up, value_up, place)
+    )
     near = jnp.concatenate([one, two], axis=0)
     near_swapped = other_core(near)
-    three, four = along_z(two, 1), along_z(two[:1], 2)
+    three, four = along_z(two, 1), along_z(two, 2)
 
     payload = swap_y(packed).reshape(4 * tokens, -1)
-    starts = query_start[0] + payload[::block, -1].astype(jnp.int32) * block
-    queries = latent_queries(payload, key_up, heads, nope, rope)
-
-    side = 1 - 2 * c
-
-    def bases_of(steps, cores):
-        steps, cores = np.array(steps, np.int32), np.array(cores, np.int32)
-        place = (y * 8 + (z - side * steps) % 8) * 2 + (c + cores) % 2
-        return place.astype(jnp.int32) * shard
+    queries, starts = latent_queries(query_start, payload, key_up, heads, nope, rope, 8)
 
     attend_part = functools.partial(
-        attend, starts, limit=key_limit, query=queries, scale=scale,
-        value_up=value_up,
-    )
+        attend, starts, place, queries, scale=scale, value_up=value_up
+    )
+    pairs = lambda steps: [(step, core) for step in steps for core in (0, 1)]
+    partial = attend_part(keys=[pair, near, near_swapped], shards=pairs((0, 1, 2, -1, -2)))
+    three, four, partial = lax.optimization_barrier((three, four, partial))
     partial = attend_part(
-        bases_of([0, 0, 1, 1, 2, 2, -1, -1, -2, -2], [0, 1, 0, 1, 0, 1, 1, 0, 1, 0]),
-        keys=[pair, near, near_swapped],
-    )
-    three, four, partial = lax.optimization_barrier((three, four, partial))
-    far = jnp.concatenate([three, four], axis=0)
-    partial = attend_part(
-        bases_of([3, 3, 4, -3, -3, -4], [0, 1, 0, 1, 0, 1]),
-        keys=[far, other_core(far)],
-        before=partial,
+        keys=[four, three, other_core(three)], shards=pairs((4, 3, -3)), before=partial
     )
     values = merge(swap_y(partial.reshape(4, tokens, -1)), heads, 4)
     values, weight = lax.optimization_barrier((values, weight))
     weights = [weight, other_core(weight)]
 
     rows = swap_y(values).reshape(4 * tokens, -1)
-    product = jnp.concatenate(
-        [
-            lax.dot_general(
-                rows, w, (((1,), (1,)), ((), ())), preferred_element_type=jnp.float32
-            ).astype(jnp.bfloat16)
-            for w in weights
-        ],
-        axis=1,
-    )
+    product = project(rows, *weights)
     share = tokens // 8
     width = 16 * columns
     product = lax.all_to_all(

time: 161 us -> 169 us (1.050)
  the two profiles are of different devices: /device:TPU:64 before, /device:TPU:32 now
where the time goes in v6:
time: 169 us; the launch traced here: 168 us
  starting transfers between devices  52 us (31%)
  Pallas kernels  32.2 us (19%)
  waiting for transfers between devices  31 us (18%)
  blocking collectives  31 us (18%)
  between operations  14.9 us (9%)
  local copies, waits for them, and re-layouts  7.02 us (4%)
    ppermute x8, starting transfers between devices, permute(): return lax.ppermute(x, names, pairs)  42.4 us
    all_to_all x2, blocking collectives, swap_y(): return lax.all_to_all(x, 'y', split_axis=0, concat_axis=0, tiled=True)  28.7 us
    pallas_call x2, Pallas kernels, attend(): pl.pallas_call(kernel, grid_spec=pltpu.PrefetchScalarGridSpec(num_scalar_...  18.9 us
    all_to_all x1, waiting for transfers between devices, per_device(): lax.all_to_all(product.reshape(16, 2 * share, width), ('y', 'x'), split_a...  15.5 us
    ppermute x8, waiting for transfers between devices, permute(): return lax.ppermute(x, names, pairs)  14.8 us
    pallas_call x1, Pallas kernels, project(): pl.pallas_call(product_kernel, grid=(columns // width,), in_specs=[pl.Blo...  7.06 us
    all_to_all x1, starting transfers between devices, per_device(): lax.all_to_all(product.reshape(16, 2 * share, width), ('y', 'x'), split_a...  5.17 us
    unnamed x13, local copies, waits for them, and re-layouts  4.86 us
  transfers between devices with their start and end apart: 11, of which 3 were waited for; matrix products, arithmetic and copies ran while one was open for 2% of the time, Pallas kernels for 15%

profile of v6, /device:TPU:32, one launch (start us, length us, event | category | flops | bytes accessed | tf_op | source)
XLA Modules:
  0.0 168.5 jit_solution(14665561893739615479)
XLA Ops:
  6.5 0.7 all-gather.2.cloned.1.call-update
  7.3 2.2 %all_gather.6 = bf16[1152,128]{1,0:T(8,128)(2,1)S(1)} all-gather(bf16[576,128]{1,0:T(8,128)(2,1)} %param.11), channel_id=1, replica_groups=mesh['y'=4,'z'=8,'c'=2,'x'=4,'h'=2] {'c'}, dimensions={0}, use_global_device_ids=true | all-gather | bytes 442368 | tf_op jit(solution)/shard_map/all_gather | solution.py:345
  9.5 5.2 %collective-permute-start = (bf16[2,576,128]{2,1,0:T(8,128)(2,1)S(1)}, bf16[2,576,128]{2,1,0:T(8,128)(2,1)S(1)}, u32[]{:S(2)}, u32[]{:S(2)}) collective-permute-start(bf16[2,576,128]{2,1,0:T(8,128)(2,1)S(1)} %bitcast.47), channel_id=1, source_target_pairs={{0,32},{1,33},{8,105},{9,104},{16,48},{17,49},{24,121},{25,120},{3... | collective-permute-start | bytes 884744 | tf_op jit(solution)/shard_map/ppermute | solution.py:30
  14.7 5.0 %collective-permute-start.3 = (bf16[2,576,128]{2,1,0:T(8,128)(2,1)S(1)}, bf16[2,576,128]{2,1,0:T(8,128)(2,1)}, u32[]{:S(2)}, u32[]{:S(2)}) collective-permute-start(bf16[2,576,128]{2,1,0:T(8,128)(2,1)S(1)} %bitcast.48), channel_id=1, source_target_pairs={{0,16},{1,17},{8,121},{9,120},{16,32},{17,33},{24,8},{25,9},{32,48... | collective-permute-start | bytes 884744 | tf_op jit(solution)/shard_map/ppermute | solution.py:30
  19.7 2.6 %shard_map.91 = bf16[4,64,1664]{2,1,0:T(8,128)(2,1)} custom-call(s32[2]{0:T(128)} %order.1, bf16[64,8,128]{2,1,0:T(8,128)(2,1)} %content.1, bf16[64,512]{1,0:T(8,128)(2,1)} %rotary.1), custom_call_target="tpu_custom_call" | custom-call | tf_op jit(solution)/shard_map/pallas_call | solution.py:66
  22.3 4.5 %all-to-all-start = ((bf16[4,64,1664]{2,1,0:T(8,128)(2,1)}), bf16[4,64,1664]{2,1,0:T(8,128)(2,1)S(1)}, u32[]{:S(2)}, u32[]{:S(2)}) async-start(bf16[4,64,1664]{2,1,0:T(8,128)(2,1)} %shard_map.91), calls=%async_computation | async-start | bytes 1703936 | tf_op jit(solution)/shard_map/all_to_all | solution.py:46
  26.8 0.3 copy.26
  27.1 1.6 copy.17
  29.5 0.7 copy-done.4
  30.2 1.0 constant_dynamic-update-slice_fusion.1
  31.2 1.0 constant_dynamic-update-slice_fusion.rest_1_
  32.2 4.9 %collective-permute-start.4 = (bf16[4,576,128]{2,1,0:T(8,128)(2,1)S(1)}, bf16[4,576,128]{2,1,0:T(8,128)(2,1)}, u32[]{:S(2)}, u32[]{:S(2)}) collective-permute-start(bf16[4,576,128]{2,1,0:T(8,128)(2,1)S(1)} %constant_dynamic-update-slice_fusion.rest_1_), channel_id=1, source_target_pairs={{0,8},{8,0},{1,9},{9,1},{2,10},{10,2},{3,11},{11,3},{4,12},{12,4},... | collective-permute-start | bytes 1769480 | tf_op jit(solution)/shard_map/ppermute | solution.py:30
  37.1 3.0 %collective-permute-start.1 = (bf16[2,576,128]{2,1,0:T(8,128)(2,1)}, bf16[2,576,128]{2,1,0:T(8,128)(2,1)}, u32[]{:S(2)}, u32[]{:S(2)}) collective-permute-start(bf16[2,576,128]{2,1,0:T(8,128)(2,1)} %copy-done.4), channel_id=1, source_target_pairs={{0,16},{1,17},{8,121},{9,120},{16,32},{17,33},{24,8},{25,9},{32,48... | collective-permute-start | bytes 884744 | tf_op jit(solution)/shard_map/ppermute | solution.py:30
  40.1 3.1 %collective-permute-start.2 = (bf16[2,576,128]{2,1,0:T(8,128)(2,1)}, bf16[2,576,128]{2,1,0:T(8,128)(2,1)}, u32[]{:S(2)}, u32[]{:S(2)}) collective-permute-start(bf16[2,576,128]{2,1,0:T(8,128)(2,1)} %copy-done.4), channel_id=1, source_target_pairs={{0,32},{1,33},{8,105},{9,104},{16,48},{17,49},{24,121},{25,120},{3... | collective-permute-start | bytes 884744 | tf_op jit(solution)/shard_map/ppermute | solution.py:30
  43.8 1.2 shard_map.92
  45.0 11.0 %shard_map.93.rest_4_ = bf16[256,1152]{1,0:T(8,128)(2,1)S(1)} custom-call(s32[8]{0:T(128)S(1)} %get-tuple-element.17.starts, s32[4]{0:T(128)S(1)} %pad_add_fusion.place, bf16[8,576,256]{2,1,0:T(8,128)(2,1)S(1)} %get-tuple-element.19.query, bf16[2,576,128]{2,1,0:T(8,128)(2,1)S(1)} %bitcast.49, ...), custom_call_target="tpu_custom_call" | custom-call | tf_op jit(solution)/shard_map/pallas_call | solution.py:246
  56.1 14.8 %collective-permute-start.5 = (bf16[2,576,128]{2,1,0:T(8,128)(2,1)}, bf16[2,576,128]{2,1,0:T(8,128)(2,1)S(1)}, u32[]{:S(2)}, u32[]{:S(2)}) collective-permute-start(bf16[2,576,128]{2,1,0:T(8,128)(2,1)} %collective-permute-done.1.rest_1_), channel_id=1, source_target_pairs={{0,8},{8,0},{1,9},{9,1},{2,10},{10,2},{3,11},{11,3},{4,12},{12,4},... | collective-permute-start | bytes 884744 | tf_op jit(solution)/shard_map/ppermute | solution.py:30
  70.9 1.2 collective-permute-done.5.rest_2_
  72.1 7.9 %shard_map.94 = bf16[256,1152]{1,0:T(8,128)(2,1)S(1)} custom-call(s32[8]{0:T(128)S(1)} %get-tuple-element.17.starts, s32[4]{0:T(128)S(1)} %pad_add_fusion.place, bf16[8,576,256]{2,1,0:T(8,128)(2,1)S(1)} %get-tuple-element.19.query, bf16[2,576,128]{2,1,0:T(8,128)(2,1)} %collective-permute-done.2.rest_0_, bf16[2,576,128]{2,1,0:T(8,128)(2,1)} %collective-permute-done.1.rest_1_, ...), custom_call_target="tpu_custom_call" | custom-call | tf_op jit(solution)/shard_map/pallas_call | solution.py:246
  80.1 14.1 %all_to_all.20.parts = bf16[4,64,1152]{2,1,0:T(8,128)(2,1)} all-to-all(bf16[4,64,1152]{2,1,0:T(8,128)(2,1)S(1)} %bitcast.46), channel_id=1, replica_groups=mesh['y'=4,'z'=8,'c'=2,'x'=4,'h'=2] {'y'}, dimensions={0} | all-to-all | bytes 1179648 | tf_op jit(solution)/shard_map/all_to_all | solution.py:46
  94.2 2.4 %shard_map.95 = bf16[4,64,1024]{2,1,0:T(8,128)(2,1)} custom-call(bf16[4,64,1152]{2,1,0:T(8,128)(2,1)} %all_to_all.20.parts), custom_call_target="tpu_custom_call" | custom-call | tf_op jit(solution)/shard_map/pallas_call | solution.py:290
  96.6 1.9 %collective-permute-start.6 = (bf16[896,1024]{1,0:T(8,128)(2,1)}, bf16[896,1024]{1,0:T(8,128)(2,1)S(1)}, u32[]{:S(2)}, u32[]{:S(2)}) collective-permute-start(bf16[896,1024]{1,0:T(8,128)(2,1)} %all-gather.2.cloned.1.call-done.mine), channel_id=1, source_target_pairs={{0,8},{8,0},{1,9},{9,1},{2,10},{10,2},{3,11},{11,3},{4,12},{12,4},... | collective-permute-start | bytes 5505032 | tf_op jit(solution)/shard_map/ppermute | solution.py:30
  98.5 14.6 %all_to_all.21 = bf16[4,64,1024]{2,1,0:T(8,128)(2,1)} all-to-all(bf16[4,64,1024]{2,1,0:T(8,128)(2,1)} %shard_map.95), channel_id=1, replica_groups=mesh['y'=4,'z'=8,'c'=2,'x'=4,'h'=2] {'y'}, dimensions={0} | all-to-all | bytes 1048576 | tf_op jit(solution)/shard_map/all_to_all | solution.py:46
  113.1 1.2 copy-done.2
  114.4 7.1 %shard_map.96 = bf16[256,1792]{1,0:T(8,128)(2,1)} custom-call(bf16[256,1024]{1,0:T(8,128)(2,1)} %bitcast.52, bf16[896,1024]{1,0:T(8,128)(2,1)} %all-gather.2.cloned.1.call-done.mine, bf16[896,1024]{1,0:T(8,128)(2,1)} %copy-done.2), custom_call_target="tpu_custom_call" | custom-call | tf_op jit(solution)/shard_map/pallas_call | solution.py:309
  121.4 5.2 %all-to-all-start.3 = ((bf16[16,16,1792]{2,1,0:T(8,128)(2,1)}), bf16[16,16,1792]{2,1,0:T(8,128)(2,1)S(1)}, u32[]{:S(2)}, u32[]{:S(2)}) async-start(bf16[16,16,1792]{2,1,0:T(8,128)(2,1)} %bitcast.50), calls=%async_computation.3 | async-start | bytes 1835008 | tf_op jit(solution)/shard_map/all_to_all | solution.py:377
  126.6 15.5 %all-to-all-done.3 = bf16[16,16,1792]{2,1,0:T(8,128)(2,1)S(1)} async-done(((bf16[16,16,1792]{2,1,0:T(8,128)(2,1)}), bf16[16,16,1792]{2,1,0:T(8,128)(2,1)S(1)}, u32[]{:S(2)}, u32[]{:S(2)}) %all-to-all-start.3) | async-done | bytes 917536 | tf_op jit(solution)/shard_map/all_to_all | solution.py:377
  142.1 0.1 convert_reduce_fusion
  142.3 4.5 %collective-permute-start.7 = (bf16[4,8,1792]{2,1,0:T(8,128)(2,1)S(1)}, bf16[4,8,1792]{2,1,0:T(8,128)(2,1)S(1)}, u32[]{:S(2)}, u32[]{:S(2)}) collective-permute-start(bf16[4,8,1792]{2,1,0:T(8,128)(2,1)S(1)} %fusion.4), channel_id=1, source_target_pairs={{0,1},{1,0},{2,3},{3,2},{4,5},{5,4},{6,7},{7,6},{8,9},{9,8},{10,11... | collective-permute-start | bytes 344072 | tf_op jit(solution)/shard_map/ppermute | solution.py:30
  146.8 13.6 %collective-permute-done.7 = bf16[4,8,1792]{2,1,0:T(8,128)(2,1)S(1)} collective-permute-done((bf16[4,8,1792]{2,1,0:T(8,128)(2,1)S(1)}, bf16[4,8,1792]{2,1,0:T(8,128)(2,1)S(1)}, u32[]{:S(2)}, u32[]{:S(2)}) %collective-permute-start.7) | collective-permute-done | bytes 114720 | tf_op jit(solution)/shard_map/ppermute | solution.py:30
  160.4 0.2 reshape.38
  160.8 0.8 reshape.39
  (23 shorter events, 0.3 us)
Async XLA Ops:
  6.5 20.3 %copy-start.3 = (bf16[512,8,128]{2,1,0:T(8,128)(2,1)S(1)}, bf16[512,8,128]{2,1,0:T(8,128)(2,1)}, u32[]{:S(2)}) copy-start(bf16[512,8,128]{2,1,0:T(8,128)(2,1)} %param.12) | copy-start | bytes 3145732
  6.5 90.0 %all-gather.2.cloned.1.call-start = ((), (), s32[]{:S(2)}) async-start(), calls=%async_computation.4 | async-start | bytes 2064384 | tf_op jit(solution)/shard_map/all_gather | solution.py:341
  9.5 17.6 %copy-start = (bf16[1152,128]{1,0:T(8,128)(2,1)}, bf16[1152,128]{1,0:T(8,128)(2,1)S(1)}, u32[]{:S(2)}) copy-start(bf16[1152,128]{1,0:T(8,128)(2,1)S(1)} %all_gather.6) | copy-start | bytes 884740
  9.5 20.0 %collective-permute-start = (bf16[2,576,128]{2,1,0:T(8,128)(2,1)S(1)}, bf16[2,576,128]{2,1,0:T(8,128)(2,1)S(1)}, u32[]{:S(2)}, u32[]{:S(2)}) collective-permute-start(bf16[2,576,128]{2,1,0:T(8,128)(2,1)S(1)} %bitcast.47), channel_id=1, source_target_pairs={{0,32},{1,33},{8,105},{9,104},{16,48},{17,49},{24,121},{25,120},{3... | collective-permute-start | bytes 884744 | tf_op jit(solution)/shard_map/ppermute | solution.py:30
  14.7 15.5 %collective-permute-start.3 = (bf16[2,576,128]{2,1,0:T(8,128)(2,1)S(1)}, bf16[2,576,128]{2,1,0:T(8,128)(2,1)}, u32[]{:S(2)}, u32[]{:S(2)}) collective-permute-start(bf16[2,576,128]{2,1,0:T(8,128)(2,1)S(1)} %bitcast.48), channel_id=1, source_target_pairs={{0,16},{1,17},{8,121},{9,120},{16,32},{17,33},{24,8},{25,9},{32,48... | collective-permute-start | bytes 884744 | tf_op jit(solution)/shard_map/ppermute | solution.py:30
  22.3 21.5 %all-to-all-start = ((bf16[4,64,1664]{2,1,0:T(8,128)(2,1)}), bf16[4,64,1664]{2,1,0:T(8,128)(2,1)S(1)}, u32[]{:S(2)}, u32[]{:S(2)}) async-start(bf16[4,64,1664]{2,1,0:T(8,128)(2,1)} %shard_map.91), calls=%async_computation | async-start | bytes 1703936 | tf_op jit(solution)/shard_map/all_to_all | solution.py:46
  29.4 0.7 copy-start.4
  32.2 12.8 %collective-permute-start.4 = (bf16[4,576,128]{2,1,0:T(8,128)(2,1)S(1)}, bf16[4,576,128]{2,1,0:T(8,128)(2,1)}, u32[]{:S(2)}, u32[]{:S(2)}) collective-permute-start(bf16[4,576,128]{2,1,0:T(8,128)(2,1)S(1)} %constant_dynamic-update-slice_fusion.rest_1_), channel_id=1, source_target_pairs={{0,8},{8,0},{1,9},{9,1},{2,10},{10,2},{3,11},{11,3},{4,12},{12,4},... | collective-permute-start | bytes 1769480 | tf_op jit(solution)/shard_map/ppermute | solution.py:30
  37.1 19.0 %collective-permute-start.1 = (bf16[2,576,128]{2,1,0:T(8,128)(2,1)}, bf16[2,576,128]{2,1,0:T(8,128)(2,1)}, u32[]{:S(2)}, u32[]{:S(2)}) collective-permute-start(bf16[2,576,128]{2,1,0:T(8,128)(2,1)} %copy-done.4), channel_id=1, source_target_pairs={{0,16},{1,17},{8,121},{9,120},{16,32},{17,33},{24,8},{25,9},{32,48... | collective-permute-start | bytes 884744 | tf_op jit(solution)/shard_map/ppermute | solution.py:30
  40.1 16.0 %collective-permute-start.2 = (bf16[2,576,128]{2,1,0:T(8,128)(2,1)}, bf16[2,576,128]{2,1,0:T(8,128)(2,1)}, u32[]{:S(2)}, u32[]{:S(2)}) collective-permute-start(bf16[2,576,128]{2,1,0:T(8,128)(2,1)} %copy-done.4), channel_id=1, source_target_pairs={{0,32},{1,33},{8,105},{9,104},{16,48},{17,49},{24,121},{25,120},{3... | collective-permute-start | bytes 884744 | tf_op jit(solution)/shard_map/ppermute | solution.py:30
  43.8 1.2 copy-start.1
  56.1 16.1 %collective-permute-start.5 = (bf16[2,576,128]{2,1,0:T(8,128)(2,1)}, bf16[2,576,128]{2,1,0:T(8,128)(2,1)S(1)}, u32[]{:S(2)}, u32[]{:S(2)}) collective-permute-start(bf16[2,576,128]{2,1,0:T(8,128)(2,1)} %collective-permute-done.1.rest_1_), channel_id=1, source_target_pairs={{0,8},{8,0},{1,9},{9,1},{2,10},{10,2},{3,11},{11,3},{4,12},{12,4},... | collective-permute-start | bytes 884744 | tf_op jit(solution)/shard_map/ppermute | solution.py:30
  96.6 16.6 %collective-permute-start.6 = (bf16[896,1024]{1,0:T(8,128)(2,1)}, bf16[896,1024]{1,0:T(8,128)(2,1)S(1)}, u32[]{:S(2)}, u32[]{:S(2)}) collective-permute-start(bf16[896,1024]{1,0:T(8,128)(2,1)} %all-gather.2.cloned.1.call-done.mine), channel_id=1, source_target_pairs={{0,8},{8,0},{1,9},{9,1},{2,10},{10,2},{3,11},{11,3},{4,12},{12,4},... | collective-permute-start | bytes 5505032 | tf_op jit(solution)/shard_map/ppermute | solution.py:30
  113.1 1.2 copy-start.2
  121.4 20.7 %all-to-all-start.3 = ((bf16[16,16,1792]{2,1,0:T(8,128)(2,1)}), bf16[16,16,1792]{2,1,0:T(8,128)(2,1)S(1)}, u32[]{:S(2)}, u32[]{:S(2)}) async-start(bf16[16,16,1792]{2,1,0:T(8,128)(2,1)} %bitcast.50), calls=%async_computation.3 | async-start | bytes 1835008 | tf_op jit(solution)/shard_map/all_to_all | solution.py:377
  142.3 18.1 %collective-permute-start.7 = (bf16[4,8,1792]{2,1,0:T(8,128)(2,1)S(1)}, bf16[4,8,1792]{2,1,0:T(8,128)(2,1)S(1)}, u32[]{:S(2)}, u32[]{:S(2)}) collective-permute-start(bf16[4,8,1792]{2,1,0:T(8,128)(2,1)S(1)} %fusion.4), channel_id=1, source_target_pairs={{0,1},{1,0},{2,3},{3,2},{4,5},{5,4},{6,7},{7,6},{8,9},{9,8},{10,11... | collective-permute-start | bytes 344072 | tf_op jit(solution)/shard_map/ppermute | solution.py:30
Sparse Core Ops, SparseCore 0:
  9.4 75.3 all-gather.1

commit v7 on v6

--- a/solution.py
+++ b/solution.py
@@ -14,6 +14,7 @@
 SIZES = {"y": 4, "z": 8, "c": 2, "x": 4, "h": 2}
 NAMES = tuple(SIZES)
 STATS = 128
+MINE, OTHER = 2, 3
 
 
 def permute(x, names, move):
@@ -137,8 +138,10 @@
     columns = some * tokens
     limit = place[3]
     side = 1 - 2 * place[2]
+    cores = {0: 0, 1: 1, MINE: place[2], OTHER: 1 - place[2]}
     bases = [
-        ((place[0] * 8 + (place[1] + 8 - side * step) % 8) * 2 + core) * width for step, core in shards
+        ((place[0] * 8 + (place[1] + 8 - side * step) % 8) * 2 + cores[core]) * width
+        for step, core in shards
     ]
     left = out.shape[1] - STATS
 
@@ -264,8 +267,12 @@
     )(starts, place, query, *keys, value_up, before)
 
 
-def merge_kernel(parts, out, *, heads, sources):
+def merge_kernel(half, parts, out, *, heads, sources):
     width = out.shape[2]
+    share = out.shape[1] // 8
+    first = lambda value, which: [
+        value[i * share : (i + 1) * share] for i in range(8) if i % 2 == which
+    ]
     each = width // heads
     lses = [read_stats(parts.at[s], heads) for s in range(sources)]
     top = functools.reduce(jnp.maximum, lses)
@@ -280,43 +287,25 @@
                 weights[s][:, h : h + 1] * parts[s, :, cols].astype(jnp.float32)
                 for s in range(sources)
             ],
+        )
+        even, odd = first(value, 0), first(value, 1)
+        value = jnp.where(
+            half[0] == 0, jnp.concatenate(odd + even, axis=0), jnp.concatenate(even + odd, axis=0)
         ).astype(out.dtype)
         for i in range(out.shape[0]):
             out[i, :, cols] = value
 
 
-def merge(parts, heads, copies):
+def merge(half, parts, heads, copies):
     sources, tokens, width = parts.shape
     return pl.pallas_call(
         functools.partial(merge_kernel, heads=heads, sources=sources),
+        in_specs=[
+            pl.BlockSpec(memory_space=pltpu.SMEM),
+            pl.BlockSpec(memory_space=pltpu.VMEM),
+        ],
         out_shape=jax.ShapeDtypeStruct((copies, tokens, width - STATS), jnp.bfloat16),
-    )(parts)
-
-
-def product_kernel(rows, mine, other, out):
-    step = pl.program_id(0)
-    width = mine.shape[0]
-    for n, weight in enumerate((mine, other)):
-        cols = pl.ds(pl.multiple_of(step * width + n * out.shape[1] // 2, width), width)
-        out[:, cols] = lax.dot_general(
-            rows[...], weight[...], (((1,), (1,)), ((), ())), preferred_element_type=jnp.float32
-        ).astype(out.dtype)
-
-
-def project(rows, mine, other, width=128):
-    tokens, depth = rows.shape
-    columns = mine.shape[0]
-    return pl.pallas_call(
-        product_kernel,
-        grid=(columns // width,),
-        in_specs=[
-            pl.BlockSpec((tokens, depth), lambda i: (0, 0)),
-            pl.BlockSpec((width, depth), lambda i: (i, 0)),
-            pl.BlockSpec((width, depth), lambda i: (i, 0)),
-        ],
-        out_specs=pl.BlockSpec((tokens, 2 * columns), lambda i: (0, 0)),
-        out_shape=jax.ShapeDtypeStruct((tokens, 2 * columns), jnp.bfloat16),
-    )(rows, mine, other)
+    )(half, parts)
 
 
 def per_device(
@@ -347,12 +336,13 @@
     key_up = key_up.reshape(latent, heads * nope)
     value_up = value_up.transpose(1, 2, 0)
     place = jnp.concatenate([jnp.stack([y, z, c]).astype(jnp.int32), key_limit])
-    two, _, key_up, value_up, place = lax.optimization_barrier(
-        (two, packed, key_up, value_up, place)
+    half = h.astype(jnp.int32)[None]
+    two, _, key_up, value_up, place, half = lax.optimization_barrier(
+        (two, packed, key_up, value_up, place, half)
     )
     near = jnp.concatenate([one, two], axis=0)
     near_swapped = other_core(near)
-    three, four = along_z(two, 1), along_z(two, 2)
+    three, four = along_z(two, 1), along_z(lax.dynamic_slice_in_dim(two, c, 1), 2)
 
     payload = swap_y(packed).reshape(4 * tokens, -1)
     queries, starts = latent_queries(query_start, payload, key_up, heads, nope, rope, 8)
@@ -364,27 +354,40 @@
     partial = attend_part(keys=[pair, near, near_swapped], shards=pairs((0, 1, 2, -1, -2)))
     three, four, partial = lax.optimization_barrier((three, four, partial))
     partial = attend_part(
-        keys=[four, three, other_core(three)], shards=pairs((4, 3, -3)), before=partial
-    )
-    values = merge(swap_y(partial.reshape(4, tokens, -1)), heads, 4)
+        keys=[three, other_core(three), four, other_core(four)],
+        shards=pairs((3, -3)) + [(4, MINE), (4, OTHER)],
+        before=partial,
+    )
+    values = merge(half, swap_y(partial.reshape(4, tokens, -1)), heads, 4)
     values, weight = lax.optimization_barrier((values, weight))
     weights = [weight, other_core(weight)]
 
-    rows = swap_y(values).reshape(4 * tokens, -1)
-    product = project(rows, *weights)
+    rows = swap_y(values)
     share = tokens // 8
-    width = 16 * columns
-    product = lax.all_to_all(
-        product.reshape(16, 2 * share, width), ("y", "x"), split_axis=0, concat_axis=0, tiled=True
-    )
-    summed = jnp.sum(product.reshape(4, 4, 2, share, width).astype(jnp.float32), axis=1)
-    mine = jnp.where(h == 0, summed[:, 0], summed[:, 1])
-    theirs = jnp.where(h == 0, summed[:, 1], summed[:, 0]).astype(jnp.bfloat16)
+
+    def summed(part):
+        part = part.reshape(4 * tokens // 2, -1)
+        product = jnp.concatenate(
+            [
+                lax.dot_general(
+                    part, w, (((1,), (1,)), ((), ())), preferred_element_type=jnp.float32
+                ).astype(jnp.bfloat16)
+                for w in weights
+            ],
+            axis=1,
+        )
+        product = lax.all_to_all(
+            product.reshape(16, share, -1), ("y", "x"), split_axis=0, concat_axis=0, tiled=True
+        )
+        return jnp.sum(product.reshape(4, 4, share, -1).astype(jnp.float32), axis=1)
+
+    theirs = summed(rows[:, : tokens // 2]).astype(jnp.bfloat16)
     got = permute(theirs, ("h",), lambda at: {"h": 1 - at["h"]})
+    mine = summed(rows[:, tokens // 2 :])
     total = (mine + got.astype(jnp.float32)).astype(jnp.bfloat16)
     total = total.reshape(4, share, 2, 8, columns)
     total = jnp.where(c == 0, total, total[:, :, ::-1])
-    return total.transpose(1, 0, 3, 2, 4).reshape(share, 4 * width)
+    return total.transpose(1, 0, 3, 2, 4).reshape(share, 16 * 4 * columns)
 
 
 def solution(mesh):

time: 169 us -> 159 us (0.941)
  waiting for transfers between devices: 31 us -> 22.1 us
  Pallas kernels: 32.2 us -> 25.1 us
  matrix products: 0 us -> 2.85 us
  starting transfers between devices: 52 us -> 54.3 us
    pallas_call x1 -> x0, Pallas kernels: 7.06 us -> none  [project(): pl.pallas_call(product_kernel, grid=(columns // width,), in_specs=[pl.Blo...]
    all_to_all x1 -> x2, waiting for transfers between devices: 15.5 us -> 8.85 us  [summed(): lax.all_to_all(product.reshape(16, share, -1), ('y', 'x'), split_axis=0,...]
    all_to_all x1 -> x2, starting transfers between devices: 5.17 us -> 8.53 us  [summed(): lax.all_to_all(product.reshape(16, share, -1), ('y', 'x'), split_axis=0,...]
    dot_general x0 -> x4, matrix products: none -> 2.85 us  [summed(): lax.dot_general(part, w, (((1,), (1,)), ((), ())), preferred_element_type...]
    ppermute x8 -> x9, waiting for transfers between devices: 14.8 us -> 12.5 us  [permute(): return lax.ppermute(x, names, pairs)]
    unnamed x13 -> x11, local copies, waits for them, and re-layouts: 4.86 us -> 2.92 us
    ppermute x8 -> x9, starting transfers between devices: 42.4 us -> 41.3 us  [permute(): return lax.ppermute(x, names, pairs)]
  transfers between devices with their start and end apart: 11 -> 13, of which waited for: 3 -> 3; matrix products, arithmetic and copies ran while one was open for 2% -> 6% of each run, Pallas kernels for 15% -> 16%
where the time goes in v7:
time: 159 us; the launch traced here: 158 us
  starting transfers between devices  54.3 us (34%)
  blocking collectives  30 us (19%)
  Pallas kernels  25.1 us (16%)
  waiting for transfers between devices  22.1 us (14%)
  between operations  15 us (9%)
  local copies, waits for them, and re-layouts  6.71 us (4%)
  matrix products  2.85 us (2%)
  other arithmetic  1.87 us (1%)
    ppermute x9, starting transfers between devices, permute(): return lax.ppermute(x, names, pairs)  41.3 us
    all_to_all x2, blocking collectives, swap_y(): return lax.all_to_all(x, 'y', split_axis=0, concat_axis=0, tiled=True)  27.7 us
    pallas_call x2, Pallas kernels, attend(): pl.pallas_call(kernel, grid_spec=pltpu.PrefetchScalarGridSpec(num_scalar_...  18.9 us
    ppermute x9, waiting for transfers between devices, permute(): return lax.ppermute(x, names, pairs)  12.5 us
    all_to_all x2, waiting for transfers between devices, summed(): lax.all_to_all(product.reshape(16, share, -1), ('y', 'x'), split_axis=0,...  8.85 us
    all_to_all x2, starting transfers between devices, summed(): lax.all_to_all(product.reshape(16, share, -1), ('y', 'x'), split_axis=0,...  8.53 us
    all_to_all x1, starting transfers between devices, swap_y(): return lax.all_to_all(x, 'y', split_axis=0, concat_axis=0, tiled=True)  4.46 us
  transfers between devices with their start and end apart: 13, of which 3 were waited for; matrix products, arithmetic and copies ran while one was open for 6% of the time, Pallas kernels for 16%

profile of v7, /device:TPU:32, one launch (start us, length us, event | category | flops | bytes accessed | tf_op | source)
XLA Modules:
  0.0 157.9 jit_solution(11530252210798730553)
XLA Ops:
  7.3 2.2 %all_gather.6 = bf16[1152,128]{1,0:T(8,128)(2,1)S(1)} all-gather(bf16[576,128]{1,0:T(8,128)(2,1)} %param.11), channel_id=1, replica_groups=mesh['y'=4,'z'=8,'c'=2,'x'=4,'h'=2] {'c'}, dimensions={0}, use_global_device_ids=true | all-gather | bytes 442368 | tf_op jit(solution)/shard_map/all_gather | solution.py:334
  9.5 5.2 %collective-permute-start = (bf16[2,576,128]{2,1,0:T(8,128)(2,1)S(1)}, bf16[2,576,128]{2,1,0:T(8,128)(2,1)}, u32[]{:S(2)}, u32[]{:S(2)}) collective-permute-start(bf16[2,576,128]{2,1,0:T(8,128)(2,1)S(1)} %bitcast.39), channel_id=1, source_target_pairs={{0,32},{1,33},{8,105},{9,104},{16,48},{17,49},{24,121},{25,120},{3... | collective-permute-start | bytes 884744 | tf_op jit(solution)/shard_map/ppermute | solution.py:31
  14.7 5.0 %collective-permute-start.3 = (bf16[2,576,128]{2,1,0:T(8,128)(2,1)S(1)}, bf16[2,576,128]{2,1,0:T(8,128)(2,1)}, u32[]{:S(2)}, u32[]{:S(2)}) collective-permute-start(bf16[2,576,128]{2,1,0:T(8,128)(2,1)S(1)} %bitcast.40), channel_id=1, source_target_pairs={{0,16},{1,17},{8,121},{9,120},{16,32},{17,33},{24,8},{25,9},{32,48... | collective-permute-start | bytes 884744 | tf_op jit(solution)/shard_map/ppermute | solution.py:31
  19.7 2.6 %shard_map.91 = bf16[4,64,1664]{2,1,0:T(8,128)(2,1)} custom-call(s32[2]{0:T(128)} %order.1, bf16[64,8,128]{2,1,0:T(8,128)(2,1)} %content.1, bf16[64,512]{1,0:T(8,128)(2,1)} %rotary.1), custom_call_target="tpu_custom_call" | custom-call | tf_op jit(solution)/shard_map/pallas_call | solution.py:67
  22.3 4.5 %all-to-all-start = ((bf16[4,64,1664]{2,1,0:T(8,128)(2,1)}), bf16[4,64,1664]{2,1,0:T(8,128)(2,1)S(1)}, u32[]{:S(2)}, u32[]{:S(2)}) async-start(bf16[4,64,1664]{2,1,0:T(8,128)(2,1)} %shard_map.91), calls=%async_computation | async-start | bytes 1703936 | tf_op jit(solution)/shard_map/all_to_all | solution.py:47
  27.1 1.6 %copy.12 = bf16[512,8,128]{0,2,1:T(8,128)(2,1)S(1)} copy(bf16[512,8,128]{2,1,0:T(8,128)(2,1)} %param.13) | data formatting | bytes 2097152 | tf_op args[4]
  29.5 1.0 constant_dynamic-update-slice_fusion.1
  30.5 1.0 constant_dynamic-update-slice_fusion.rest_1_
  31.5 4.8 %collective-permute-start.4 = (bf16[4,576,128]{2,1,0:T(8,128)(2,1)S(1)}, bf16[4,576,128]{2,1,0:T(8,128)(2,1)}, u32[]{:S(2)}, u32[]{:S(2)}) collective-permute-start(bf16[4,576,128]{2,1,0:T(8,128)(2,1)S(1)} %constant_dynamic-update-slice_fusion.rest_1_), channel_id=1, source_target_pairs={{0,8},{8,0},{1,9},{9,1},{2,10},{10,2},{3,11},{11,3},{4,12},{12,4},... | collective-permute-start | bytes 1769480 | tf_op jit(solution)/shard_map/ppermute | solution.py:31
  36.3 3.0 %collective-permute-start.1 = (bf16[2,576,128]{2,1,0:T(8,128)(2,1)}, bf16[2,576,128]{2,1,0:T(8,128)(2,1)}, u32[]{:S(2)}, u32[]{:S(2)}) collective-permute-start(bf16[2,576,128]{2,1,0:T(8,128)(2,1)} %collective-permute-done), channel_id=1, source_target_pairs={{0,16},{1,17},{8,121},{9,120},{16,32},{17,33},{24,8},{25,9},{32,48... | collective-permute-start | bytes 884744 | tf_op jit(solution)/shard_map/ppermute | solution.py:31
  39.3 1.6 %constant_dynamic-slice_fusion = bf16[1,576,128]{2,1,0:T(8,128)(2,1)} fusion(bf16[2,576,128]{2,1,0:T(8,128)(2,1)} %collective-permute-done, s32[]{:T(128)S(6)} %select_n.12), kind=kLoop, calls=%fused_computation.15 | loop fusion | bytes 294916 | tf_op jit(solution)/shard_map/dynamic_slice | solution.py:345
  40.9 3.1 %collective-permute-start.2 = (bf16[1,576,128]{2,1,0:T(8,128)(2,1)}, bf16[1,576,128]{2,1,0:T(8,128)(2,1)}, u32[]{:S(2)}, u32[]{:S(2)}) collective-permute-start(bf16[1,576,128]{2,1,0:T(8,128)(2,1)} %constant_dynamic-slice_fusion), channel_id=1, source_target_pairs={{0,32},{1,33},{8,105},{9,104},{16,48},{17,49},{24,121},{25,120},{3... | collective-permute-start | bytes 442376 | tf_op jit(solution)/shard_map/ppermute | solution.py:31
  44.7 1.2 shard_map.92
  45.9 11.0 %shard_map.93.rest_5_ = bf16[256,1152]{1,0:T(8,128)(2,1)S(1)} custom-call(s32[8]{0:T(128)S(1)} %get-tuple-element.19.starts, s32[4]{0:T(128)S(1)} %pad_add_fusion.place, bf16[8,576,256]{2,1,0:T(8,128)(2,1)S(1)} %get-tuple-element.21.query, bf16[2,576,128]{2,1,0:T(8,128)(2,1)S(1)} %bitcast.41, ...), custom_call_target="tpu_custom_call" | custom-call | tf_op jit(solution)/shard_map/pallas_call | solution.py:249
  56.9 5.8 %collective-permute-start.5 = (bf16[2,576,128]{2,1,0:T(8,128)(2,1)}, bf16[2,576,128]{2,1,0:T(8,128)(2,1)S(1)}, u32[]{:S(2)}, u32[]{:S(2)}) collective-permute-start(bf16[2,576,128]{2,1,0:T(8,128)(2,1)} %collective-permute-done.1.rest_0_), channel_id=1, source_target_pairs={{0,8},{8,0},{1,9},{9,1},{2,10},{10,2},{3,11},{11,3},{4,12},{12,4},... | collective-permute-start | bytes 884744 | tf_op jit(solution)/shard_map/ppermute | solution.py:31
  62.8 2.1 %collective-permute-start.6 = (bf16[1,576,128]{2,1,0:T(8,128)(2,1)}, bf16[1,576,128]{2,1,0:T(8,128)(2,1)S(1)}, u32[]{:S(2)}, u32[]{:S(2)}) collective-permute-start(bf16[1,576,128]{2,1,0:T(8,128)(2,1)} %collective-permute-done.2.rest_2_), channel_id=1, source_target_pairs={{0,8},{8,0},{1,9},{9,1},{2,10},{10,2},{3,11},{11,3},{4,12},{12,4},... | collective-permute-start | bytes 442376 | tf_op jit(solution)/shard_map/ppermute | solution.py:31
  64.9 1.4 collective-permute-done.6.rest_3_
  66.3 7.9 %shard_map.94 = bf16[256,1152]{1,0:T(8,128)(2,1)S(1)} custom-call(s32[8]{0:T(128)S(1)} %get-tuple-element.19.starts, s32[4]{0:T(128)S(1)} %pad_add_fusion.place, bf16[8,576,256]{2,1,0:T(8,128)(2,1)S(1)} %get-tuple-element.21.query, bf16[2,576,128]{2,1,0:T(8,128)(2,1)} %collective-permute-done.1.rest_0_, ...), custom_call_target="tpu_custom_call" | custom-call | tf_op jit(solution)/shard_map/pallas_call | solution.py:249
  74.2 13.9 %all_to_all.25.parts = bf16[4,64,1152]{2,1,0:T(8,128)(2,1)} all-to-all(bf16[4,64,1152]{2,1,0:T(8,128)(2,1)S(1)} %bitcast.38), channel_id=1, replica_groups=mesh['y'=4,'z'=8,'c'=2,'x'=4,'h'=2] {'y'}, dimensions={0} | all-to-all | bytes 1179648 | tf_op jit(solution)/shard_map/all_to_all | solution.py:47
  88.0 2.4 %shard_map.95 = bf16[4,64,1024]{2,1,0:T(8,128)(2,1)} custom-call(s32[1]{0:T(128)} %bitcast.5.half, bf16[4,64,1152]{2,1,0:T(8,128)(2,1)} %all_to_all.25.parts), custom_call_target="tpu_custom_call" | custom-call | tf_op jit(solution)/shard_map/pallas_call | solution.py:301
  90.5 2.0 %collective-permute-start.7 = (bf16[896,1024]{1,0:T(8,128)(2,1)}, bf16[896,1024]{1,0:T(8,128)(2,1)S(1)}, u32[]{:S(2)}, u32[]{:S(2)}) collective-permute-start(bf16[896,1024]{1,0:T(8,128)(2,1)} %all-gather.2.cloned.1.call-done), channel_id=1, source_target_pairs={{0,8},{8,0},{1,9},{9,1},{2,10},{10,2},{3,11},{11,3},{4,12},{12,4},... | collective-permute-start | bytes 5505032 | tf_op jit(solution)/shard_map/ppermute | solution.py:31
  92.5 13.9 %all_to_all.26 = bf16[4,64,1024]{2,1,0:T(8,128)(2,1)S(1)} all-to-all(bf16[4,64,1024]{2,1,0:T(8,128)(2,1)} %shard_map.95), channel_id=1, replica_groups=mesh['y'=4,'z'=8,'c'=2,'x'=4,'h'=2] {'y'}, dimensions={0} | all-to-all | bytes 1048576 | tf_op jit(solution)/shard_map/all_to_all | solution.py:47
  106.4 0.7 convolution_convert_fusion.3
  107.2 0.7 convolution_convert_fusion.1
  108.6 0.8 maximum_bitcast_fusion.1
  109.4 5.0 %all-to-all-start.4 = ((bf16[16,8,1792]{2,1,0:T(8,128)(2,1)}), bf16[16,8,1792]{2,1,0:T(8,128)(2,1)S(1)}, u32[]{:S(2)}, u32[]{:S(2)}) async-start(bf16[16,8,1792]{2,1,0:T(8,128)(2,1)} %maximum_bitcast_fusion.1), calls=%async_computation.4 | async-start | bytes 917504 | tf_op jit(solution)/shard_map/all_to_all | solution.py:379
  115.1 0.8 maximum_bitcast_fusion
  115.9 8.9 %all-to-all-done.4 = bf16[16,8,1792]{2,1,0:T(8,128)(2,1)S(1)} async-done(((bf16[16,8,1792]{2,1,0:T(8,128)(2,1)}), bf16[16,8,1792]{2,1,0:T(8,128)(2,1)S(1)}, u32[]{:S(2)}, u32[]{:S(2)}) %all-to-all-start.4) | async-done | bytes 458784 | tf_op jit(solution)/shard_map/all_to_all | solution.py:379
  124.8 3.6 %all-to-all-start.3 = ((bf16[16,8,1792]{2,1,0:T(8,128)(2,1)}), bf16[16,8,1792]{2,1,0:T(8,128)(2,1)S(1)}, u32[]{:S(2)}, u32[]{:S(2)}) async-start(bf16[16,8,1792]{2,1,0:T(8,128)(2,1)} %maximum_bitcast_fusion), calls=%async_computation.3 | async-start | bytes 917504 | tf_op jit(solution)/shard_map/all_to_all | solution.py:379
  128.4 10.2 %collective-permute-start.8 = (bf16[4,8,1792]{2,1,0:T(8,128)(2,1)S(1)}, bf16[4,8,1792]{2,1,0:T(8,128)(2,1)S(1)}, u32[]{:S(2)}, u32[]{:S(2)}) collective-permute-start(bf16[4,8,1792]{2,1,0:T(8,128)(2,1)S(1)} %bitcast_reduce_fusion), channel_id=1, source_target_pairs={{0,1},{1,0},{2,3},{3,2},{4,5},{5,4},{6,7},{7,6},{8,9},{9,8},{10,11... | collective-permute-start | bytes 344072 | tf_op jit(solution)/shard_map/ppermute | solution.py:31
  138.7 11.1 %collective-permute-done.8 = bf16[4,8,1792]{2,1,0:T(8,128)(2,1)S(1)} collective-permute-done((bf16[4,8,1792]{2,1,0:T(8,128)(2,1)S(1)}, bf16[4,8,1792]{2,1,0:T(8,128)(2,1)S(1)}, u32[]{:S(2)}, u32[]{:S(2)}) %collective-permute-start.8) | collective-permute-done | bytes 114720 | tf_op jit(solution)/shard_map/ppermute | solution.py:31
  150.2 0.8 reshape.46
  (32 shorter events, 3.1 us)
Async XLA Ops:
  6.5 20.3 %copy-start.3 = (bf16[512,8,128]{2,1,0:T(8,128)(2,1)S(1)}, bf16[512,8,128]{2,1,0:T(8,128)(2,1)}, u32[]{:S(2)}) copy-start(bf16[512,8,128]{2,1,0:T(8,128)(2,1)} %param.12) | copy-start | bytes 3145732
  6.5 83.9 %all-gather.2.cloned.1.call-start = ((), (), s32[]{:S(2)}) async-start(), calls=%async_computation.5 | async-start | bytes 2064384 | tf_op jit(solution)/shard_map/all_gather | solution.py:330
  9.5 17.6 %copy-start = (bf16[1152,128]{1,0:T(8,128)(2,1)}, bf16[1152,128]{1,0:T(8,128)(2,1)S(1)}, u32[]{:S(2)}) copy-start(bf16[1152,128]{1,0:T(8,128)(2,1)S(1)} %all_gather.6) | copy-start | bytes 884740
  9.5 20.0 %collective-permute-start = (bf16[2,576,128]{2,1,0:T(8,128)(2,1)S(1)}, bf16[2,576,128]{2,1,0:T(8,128)(2,1)}, u32[]{:S(2)}, u32[]{:S(2)}) collective-permute-start(bf16[2,576,128]{2,1,0:T(8,128)(2,1)S(1)} %bitcast.39), channel_id=1, source_target_pairs={{0,32},{1,33},{8,105},{9,104},{16,48},{17,49},{24,121},{25,120},{3... | collective-permute-start | bytes 884744 | tf_op jit(solution)/shard_map/ppermute | solution.py:31
  14.7 14.8 %collective-permute-start.3 = (bf16[2,576,128]{2,1,0:T(8,128)(2,1)S(1)}, bf16[2,576,128]{2,1,0:T(8,128)(2,1)}, u32[]{:S(2)}, u32[]{:S(2)}) collective-permute-start(bf16[2,576,128]{2,1,0:T(8,128)(2,1)S(1)} %bitcast.40), channel_id=1, source_target_pairs={{0,16},{1,17},{8,121},{9,120},{16,32},{17,33},{24,8},{25,9},{32,48... | collective-permute-start | bytes 884744 | tf_op jit(solution)/shard_map/ppermute | solution.py:31
  22.3 22.3 %all-to-all-start = ((bf16[4,64,1664]{2,1,0:T(8,128)(2,1)}), bf16[4,64,1664]{2,1,0:T(8,128)(2,1)S(1)}, u32[]{:S(2)}, u32[]{:S(2)}) async-start(bf16[4,64,1664]{2,1,0:T(8,128)(2,1)} %shard_map.91), calls=%async_computation | async-start | bytes 1703936 | tf_op jit(solution)/shard_map/all_to_all | solution.py:47
  31.5 14.4 %collective-permute-start.4 = (bf16[4,576,128]{2,1,0:T(8,128)(2,1)S(1)}, bf16[4,576,128]{2,1,0:T(8,128)(2,1)}, u32[]{:S(2)}, u32[]{:S(2)}) collective-permute-start(bf16[4,576,128]{2,1,0:T(8,128)(2,1)S(1)} %constant_dynamic-update-slice_fusion.rest_1_), channel_id=1, source_target_pairs={{0,8},{8,0},{1,9},{9,1},{2,10},{10,2},{3,11},{11,3},{4,12},{12,4},... | collective-permute-start | bytes 1769480 | tf_op jit(solution)/shard_map/ppermute | solution.py:31
  36.3 20.6 %collective-permute-start.1 = (bf16[2,576,128]{2,1,0:T(8,128)(2,1)}, bf16[2,576,128]{2,1,0:T(8,128)(2,1)}, u32[]{:S(2)}, u32[]{:S(2)}) collective-permute-start(bf16[2,576,128]{2,1,0:T(8,128)(2,1)} %collective-permute-done), channel_id=1, source_target_pairs={{0,16},{1,17},{8,121},{9,120},{16,32},{17,33},{24,8},{25,9},{32,48... | collective-permute-start | bytes 884744 | tf_op jit(solution)/shard_map/ppermute | solution.py:31
  40.9 16.0 %collective-permute-start.2 = (bf16[1,576,128]{2,1,0:T(8,128)(2,1)}, bf16[1,576,128]{2,1,0:T(8,128)(2,1)}, u32[]{:S(2)}, u32[]{:S(2)}) collective-permute-start(bf16[1,576,128]{2,1,0:T(8,128)(2,1)} %constant_dynamic-slice_fusion), channel_id=1, source_target_pairs={{0,32},{1,33},{8,105},{9,104},{16,48},{17,49},{24,121},{25,120},{3... | collective-permute-start | bytes 442376 | tf_op jit(solution)/shard_map/ppermute | solution.py:31
  44.7 1.2 copy-start.1
  56.9 9.3 %collective-permute-start.5 = (bf16[2,576,128]{2,1,0:T(8,128)(2,1)}, bf16[2,576,128]{2,1,0:T(8,128)(2,1)S(1)}, u32[]{:S(2)}, u32[]{:S(2)}) collective-permute-start(bf16[2,576,128]{2,1,0:T(8,128)(2,1)} %collective-permute-done.1.rest_0_), channel_id=1, source_target_pairs={{0,8},{8,0},{1,9},{9,1},{2,10},{10,2},{3,11},{11,3},{4,12},{12,4},... | collective-permute-start | bytes 884744 | tf_op jit(solution)/shard_map/ppermute | solution.py:31
  62.8 3.5 %collective-permute-start.6 = (bf16[1,576,128]{2,1,0:T(8,128)(2,1)}, bf16[1,576,128]{2,1,0:T(8,128)(2,1)S(1)}, u32[]{:S(2)}, u32[]{:S(2)}) collective-permute-start(bf16[1,576,128]{2,1,0:T(8,128)(2,1)} %collective-permute-done.2.rest_2_), channel_id=1, source_target_pairs={{0,8},{8,0},{1,9},{9,1},{2,10},{10,2},{3,11},{11,3},{4,12},{12,4},... | collective-permute-start | bytes 442376 | tf_op jit(solution)/shard_map/ppermute | solution.py:31
  90.5 16.0 %copy-start.2 = (bf16[896,1024]{1,0:T(8,128)(2,1)S(1)}, bf16[896,1024]{1,0:T(8,128)(2,1)}, u32[]{:S(2)}) copy-start(bf16[896,1024]{1,0:T(8,128)(2,1)} %all-gather.2.cloned.1.call-done) | copy-start | bytes 5505028
  90.5 17.4 %collective-permute-start.7 = (bf16[896,1024]{1,0:T(8,128)(2,1)}, bf16[896,1024]{1,0:T(8,128)(2,1)S(1)}, u32[]{:S(2)}, u32[]{:S(2)}) collective-permute-start(bf16[896,1024]{1,0:T(8,128)(2,1)} %all-gather.2.cloned.1.call-done), channel_id=1, source_target_pairs={{0,8},{8,0},{1,9},{9,1},{2,10},{10,2},{3,11},{11,3},{4,12},{12,4},... | collective-permute-start | bytes 5505032 | tf_op jit(solution)/shard_map/ppermute | solution.py:31
  109.4 15.4 %all-to-all-start.4 = ((bf16[16,8,1792]{2,1,0:T(8,128)(2,1)}), bf16[16,8,1792]{2,1,0:T(8,128)(2,1)S(1)}, u32[]{:S(2)}, u32[]{:S(2)}) async-start(bf16[16,8,1792]{2,1,0:T(8,128)(2,1)} %maximum_bitcast_fusion.1), calls=%async_computation.4 | async-start | bytes 917504 | tf_op jit(solution)/shard_map/all_to_all | solution.py:379
  124.8 13.9 %all-to-all-start.3 = ((bf16[16,8,1792]{2,1,0:T(8,128)(2,1)}), bf16[16,8,1792]{2,1,0:T(8,128)(2,1)S(1)}, u32[]{:S(2)}, u32[]{:S(2)}) async-start(bf16[16,8,1792]{2,1,0:T(8,128)(2,1)} %maximum_bitcast_fusion), calls=%async_computation.3 | async-start | bytes 917504 | tf_op jit(solution)/shard_map/all_to_all | solution.py:379
  128.4 21.4 %collective-permute-start.8 = (bf16[4,8,1792]{2,1,0:T(8,128)(2,1)S(1)}, bf16[4,8,1792]{2,1,0:T(8,128)(2,1)S(1)}, u32[]{:S(2)}, u32[]{:S(2)}) collective-permute-start(bf16[4,8,1792]{2,1,0:T(8,128)(2,1)S(1)} %bitcast_reduce_fusion), channel_id=1, source_target_pairs={{0,1},{1,0},{2,3},{3,2},{4,5},{5,4},{6,7},{7,6},{8,9},{9,8},{10,11... | collective-permute-start | bytes 344072 | tf_op jit(solution)/shard_map/ppermute | solution.py:31
Sparse Core Ops, SparseCore 0:
  9.4 73.7 all-gather.1

commit v8 on v7

--- a/solution.py
+++ b/solution.py
@@ -129,8 +129,7 @@
 def attend_kernel(
     starts, place, query, *rest, shards, coef, block, some, with_before
 ):
-    *keys, value_up, before, out, turned, lses, olds = rest
-    first = pl.program_id(0) * some
+    *keys, value_up, before, out, turned, lses = rest
     heads, tokens = lses.shape
     value_dim, latent = value_up.shape[1:]
     width = keys[0].shape[2]
@@ -145,13 +144,11 @@
     ]
     left = out.shape[1] - STATS
 
-    @pl.when(first == 0)
-    def _():
-        for n, (r, i) in enumerate(tiles):
-            turned[n * width : (n + 1) * width, :] = r[i].T
-        if with_before:
-            stats = before[:, left:].astype(jnp.float32).T
-            olds[...] = stats[:heads] + stats[heads : 2 * heads] + stats[2 * heads : 3 * heads]
+    for n, (r, i) in enumerate(tiles):
+        turned[n * width : (n + 1) * width, :] = r[i].T
+    if with_before:
+        stats = before[:, left:].astype(jnp.float32).T
+        olds = stats[:heads] + stats[heads : 2 * heads] + stats[2 * heads : 3 * heads]
 
     highest, nearest = bases[0], starts[0]
     for i in range(1, len(shards)):
@@ -160,8 +157,8 @@
         nearest = jnp.minimum(nearest, starts[i])
     sure = highest + width - 1 <= jnp.minimum(nearest, limit - 1)
 
-    def run(masked):
-        q = jnp.concatenate([query[i] for i in range(some)], axis=1)
+    def run(masked, first):
+        q = jnp.concatenate([query[first + i] for i in range(some)], axis=1)
         s = jnp.dot(turned[...], q, preferred_element_type=jnp.float32)
         if masked:
             token = lax.broadcasted_iota(jnp.int32, (1, columns), 1) % tokens
@@ -196,7 +193,7 @@
         if with_before:
             old = []
             for i in range(some):
-                past = olds[pl.ds(first + i, 1), :]
+                past = olds[first + i : first + i + 1, :]
                 peak = jnp.maximum(past, mine[i])
                 a, b = jnp.exp2(past - peak), jnp.exp2(mine[i] - peak)
                 old.append(a / (a + b))
@@ -204,38 +201,37 @@
                 mine[i] = peak + jnp.log2(a + b)
             old = jnp.concatenate(old + [jnp.zeros((8 - some, tokens), jnp.float32)], axis=0).T
         for i in range(some):
-            lses[pl.ds(first + i, 1), :] = mine[i]
+            lses[first + i : first + i + 1, :] = mine[i]
             value = jnp.dot(
-                value_up[i], mixed[:, i * tokens : (i + 1) * tokens], preferred_element_type=jnp.float32
+                value_up[first + i], mixed[:, i * tokens : (i + 1) * tokens], preferred_element_type=jnp.float32
             )
             if with_before:
                 value = value * new[i]
             value = value.T
-            cols = pl.ds(pl.multiple_of((first + i) * value_dim, value_dim), value_dim)
+            cols = slice((first + i) * value_dim, (first + i + 1) * value_dim)
             if with_before:
                 value = value + before[:, cols].astype(jnp.float32) * old[:, i : i + 1]
             out[:, cols] = value.astype(out.dtype)
 
     @pl.when(sure)
     def _():
-        run(False)
+        for first in range(0, heads, some):
+            run(False, first)
 
     @pl.when(jnp.logical_not(sure))
     def _():
-        run(True)
-
-    @pl.when(first + some == heads)
-    def _():
-        empty = jnp.zeros((STATS - 3 * heads, tokens), jnp.float32)
-        stats = jnp.concatenate(three_parts(lses[...]) + [empty], axis=0)
-        out[:, left:] = stats.T.astype(out.dtype)
+        for first in range(0, heads, some):
+            run(True, first)
+
+    empty = jnp.zeros((STATS - 3 * heads, tokens), jnp.float32)
+    stats = jnp.concatenate(three_parts(lses[...]) + [empty], axis=0)
+    out[:, left:] = stats.T.astype(out.dtype)
 
 
 def attend(starts, place, query, keys, shards, value_up, scale, before=None, some=4):
     heads, depth, tokens = query.shape
     value_dim, latent = value_up.shape[1:]
     width = keys[0].shape[2]
-    whole = lambda shape: pl.BlockSpec(shape, lambda i, *_: (0,) * len(shape))
     kernel = functools.partial(
         attend_kernel,
         shards=shards,
@@ -248,22 +244,15 @@
         before = jnp.zeros((16, STATS), jnp.bfloat16)
     return pl.pallas_call(
         kernel,
-        grid_spec=pltpu.PrefetchScalarGridSpec(
-            num_scalar_prefetch=2,
-            grid=(heads // some,),
-            in_specs=[pl.BlockSpec((some, depth, tokens), lambda i, *_: (i, 0, 0))]
-            + [whole(k.shape) for k in keys]
-            + [pl.BlockSpec((some, value_dim, latent), lambda i, *_: (i, 0, 0))]
-            + [whole(before.shape)],
-            out_specs=whole((tokens, heads * value_dim + STATS)),
-            scratch_shapes=[
-                pltpu.VMEM((len(shards) * width, depth), jnp.bfloat16),
-                pltpu.VMEM((heads, tokens), jnp.float32),
-                pltpu.VMEM((heads, tokens), jnp.float32),
-            ],
-        ),
+        in_specs=[pl.BlockSpec(memory_space=pltpu.SMEM)] * 2
+        + [pl.BlockSpec(memory_space=pltpu.VMEM)] * (len(keys) + 3),
+        out_specs=pl.BlockSpec(memory_space=pltpu.VMEM),
+        scratch_shapes=[
+            pltpu.VMEM((len(shards) * width, depth), jnp.bfloat16),
+            pltpu.VMEM((heads, tokens), jnp.float32),
+        ],
         out_shape=jax.ShapeDtypeStruct((tokens, heads * value_dim + STATS), jnp.bfloat16),
-        compiler_params=pltpu.CompilerParams(vmem_limit_bytes=48 * 1024 * 1024),
+        compiler_params=pltpu.CompilerParams(vmem_limit_bytes=40 * 1024 * 1024),
     )(starts, place, query, *keys, value_up, before)
 
 
@@ -351,7 +340,9 @@
         attend, starts, place, queries, scale=scale, value_up=value_up
     )
     pairs = lambda steps: [(step, core) for step in steps for core in (0, 1)]
-    partial = attend_part(keys=[pair, near, near_swapped], shards=pairs((0, 1, 2, -1, -2)))
+    partial = attend_part(
+        keys=[pair, near, near_swapped], shards=pairs((0, 1, 2, -1, -2))
+    )
     three, four, partial = lax.optimization_barrier((three, four, partial))
     partial = attend_part(
         keys=[three, other_core(three), four, other_core(four)],

time: 159 us -> 158 us (level)
  transfers between devices with their start and end apart: 13 -> 13, of which waited for: 3 -> 3; matrix products, arithmetic and copies ran while one was open for 6% -> 6% of each run, Pallas kernels for 16% -> 15%
where the time goes in v8:
time: 158 us; the launch traced here: 157 us
  starting transfers between devices  54.8 us (35%)
  blocking collectives  30 us (19%)
  Pallas kernels  23.8 us (15%)
  waiting for transfers between devices  22.2 us (14%)
  between operations  15 us (9%)
  local copies, waits for them, and re-layouts  6.71 us (4%)
  matrix products  2.85 us (2%)
  other arithmetic  1.87 us (1%)
    ppermute x9, starting transfers between devices, permute(): return lax.ppermute(x, names, pairs)  41.8 us
    all_to_all x2, blocking collectives, swap_y(): return lax.all_to_all(x, 'y', split_axis=0, concat_axis=0, tiled=True)  27.8 us
    pallas_call x2, Pallas kernels, attend(): pl.pallas_call(kernel, in_specs=[pl.BlockSpec(memory_space=pltpu.SMEM)] *...  17.6 us
    ppermute x9, waiting for transfers between devices, permute(): return lax.ppermute(x, names, pairs)  12.7 us
    all_to_all x2, waiting for transfers between devices, summed(): lax.all_to_all(product.reshape(16, share, -1), ('y', 'x'), split_axis=0,...  8.85 us
    all_to_all x2, starting transfers between devices, summed(): lax.all_to_all(product.reshape(16, share, -1), ('y', 'x'), split_axis=0,...  8.53 us
    all_to_all x1, starting transfers between devices, swap_y(): return lax.all_to_all(x, 'y', split_axis=0, concat_axis=0, tiled=True)  4.46 us
  transfers between devices with their start and end apart: 13, of which 3 were waited for; matrix products, arithmetic and copies ran while one was open for 6% of the time, Pallas kernels for 15%

profile of v8, /device:TPU:32, one launch (start us, length us, event | category | flops | bytes accessed | tf_op | source)
XLA Modules:
  0.0 157.2 jit_solution(13590261659217408748)
XLA Ops:
  7.3 2.2 %all_gather.6 = bf16[1152,128]{1,0:T(8,128)(2,1)S(1)} all-gather(bf16[576,128]{1,0:T(8,128)(2,1)} %param.11), channel_id=1, replica_groups=mesh['y'=4,'z'=8,'c'=2,'x'=4,'h'=2] {'c'}, dimensions={0}, use_global_device_ids=true | all-gather | bytes 442368 | tf_op jit(solution)/shard_map/all_gather | solution.py:323
  9.5 5.2 %collective-permute-start = (bf16[2,576,128]{2,1,0:T(8,128)(2,1)S(1)}, bf16[2,576,128]{2,1,0:T(8,128)(2,1)}, u32[]{:S(2)}, u32[]{:S(2)}) collective-permute-start(bf16[2,576,128]{2,1,0:T(8,128)(2,1)S(1)} %bitcast.39), channel_id=1, source_target_pairs={{0,32},{1,33},{8,105},{9,104},{16,48},{17,49},{24,121},{25,120},{3... | collective-permute-start | bytes 884744 | tf_op jit(solution)/shard_map/ppermute | solution.py:31
  14.7 5.0 %collective-permute-start.3 = (bf16[2,576,128]{2,1,0:T(8,128)(2,1)S(1)}, bf16[2,576,128]{2,1,0:T(8,128)(2,1)}, u32[]{:S(2)}, u32[]{:S(2)}) collective-permute-start(bf16[2,576,128]{2,1,0:T(8,128)(2,1)S(1)} %bitcast.40), channel_id=1, source_target_pairs={{0,16},{1,17},{8,121},{9,120},{16,32},{17,33},{24,8},{25,9},{32,48... | collective-permute-start | bytes 884744 | tf_op jit(solution)/shard_map/ppermute | solution.py:31
  19.7 2.6 %shard_map.91 = bf16[4,64,1664]{2,1,0:T(8,128)(2,1)} custom-call(s32[2]{0:T(128)} %order.1, bf16[64,8,128]{2,1,0:T(8,128)(2,1)} %content.1, bf16[64,512]{1,0:T(8,128)(2,1)} %rotary.1), custom_call_target="tpu_custom_call" | custom-call | tf_op jit(solution)/shard_map/pallas_call | solution.py:67
  22.3 4.5 %all-to-all-start = ((bf16[4,64,1664]{2,1,0:T(8,128)(2,1)}), bf16[4,64,1664]{2,1,0:T(8,128)(2,1)S(1)}, u32[]{:S(2)}, u32[]{:S(2)}) async-start(bf16[4,64,1664]{2,1,0:T(8,128)(2,1)} %shard_map.91), calls=%async_computation | async-start | bytes 1703936 | tf_op jit(solution)/shard_map/all_to_all | solution.py:47
  27.1 1.6 %copy.12 = bf16[512,8,128]{0,2,1:T(8,128)(2,1)S(1)} copy(bf16[512,8,128]{2,1,0:T(8,128)(2,1)} %param.13) | data formatting | bytes 2097152 | tf_op args[4]
  29.5 1.0 constant_dynamic-update-slice_fusion.1
  30.5 1.0 constant_dynamic-update-slice_fusion.rest_1_
  31.5 4.8 %collective-permute-start.4 = (bf16[4,576,128]{2,1,0:T(8,128)(2,1)S(1)}, bf16[4,576,128]{2,1,0:T(8,128)(2,1)}, u32[]{:S(2)}, u32[]{:S(2)}) collective-permute-start(bf16[4,576,128]{2,1,0:T(8,128)(2,1)S(1)} %constant_dynamic-update-slice_fusion.rest_1_), channel_id=1, source_target_pairs={{0,8},{8,0},{1,9},{9,1},{2,10},{10,2},{3,11},{11,3},{4,12},{12,4},... | collective-permute-start | bytes 1769480 | tf_op jit(solution)/shard_map/ppermute | solution.py:31
  36.3 3.0 %collective-permute-start.1 = (bf16[2,576,128]{2,1,0:T(8,128)(2,1)}, bf16[2,576,128]{2,1,0:T(8,128)(2,1)}, u32[]{:S(2)}, u32[]{:S(2)}) collective-permute-start(bf16[2,576,128]{2,1,0:T(8,128)(2,1)} %collective-permute-done), channel_id=1, source_target_pairs={{0,16},{1,17},{8,121},{9,120},{16,32},{17,33},{24,8},{25,9},{32,48... | collective-permute-start | bytes 884744 | tf_op jit(solution)/shard_map/ppermute | solution.py:31
  39.3 1.6 %constant_dynamic-slice_fusion = bf16[1,576,128]{2,1,0:T(8,128)(2,1)} fusion(bf16[2,576,128]{2,1,0:T(8,128)(2,1)} %collective-permute-done, s32[]{:T(128)S(6)} %select_n.12), kind=kLoop, calls=%fused_computation.15 | loop fusion | bytes 294916 | tf_op jit(solution)/shard_map/dynamic_slice | solution.py:334
  40.9 3.1 %collective-permute-start.2 = (bf16[1,576,128]{2,1,0:T(8,128)(2,1)}, bf16[1,576,128]{2,1,0:T(8,128)(2,1)}, u32[]{:S(2)}, u32[]{:S(2)}) collective-permute-start(bf16[1,576,128]{2,1,0:T(8,128)(2,1)} %constant_dynamic-slice_fusion), channel_id=1, source_target_pairs={{0,32},{1,33},{8,105},{9,104},{16,48},{17,49},{24,121},{25,120},{3... | collective-permute-start | bytes 442376 | tf_op jit(solution)/shard_map/ppermute | solution.py:31
  44.7 1.2 shard_map.92
  45.9 10.3 %shard_map.93.rest_5_ = bf16[256,1152]{1,0:T(8,128)(2,1)S(1)} custom-call(s32[8]{0:T(128)S(1)} %get-tuple-element.19.starts, s32[4]{0:T(128)S(1)} %pad_add_fusion.place, bf16[8,576,256]{2,1,0:T(8,128)(2,1)S(1)} %get-tuple-element.21.query, bf16[2,576,128]{2,1,0:T(8,128)(2,1)S(1)} %bitcast.41, ...), custom_call_target="tpu_custom_call" | custom-call | tf_op jit(solution)/shard_map/pallas_call | solution.py:245
  56.3 6.5 %collective-permute-start.5 = (bf16[2,576,128]{2,1,0:T(8,128)(2,1)}, bf16[2,576,128]{2,1,0:T(8,128)(2,1)S(1)}, u32[]{:S(2)}, u32[]{:S(2)}) collective-permute-start(bf16[2,576,128]{2,1,0:T(8,128)(2,1)} %collective-permute-done.1.rest_0_), channel_id=1, source_target_pairs={{0,8},{8,0},{1,9},{9,1},{2,10},{10,2},{3,11},{11,3},{4,12},{12,4},... | collective-permute-start | bytes 884744 | tf_op jit(solution)/shard_map/ppermute | solution.py:31
  62.8 1.9 %collective-permute-start.6 = (bf16[1,576,128]{2,1,0:T(8,128)(2,1)}, bf16[1,576,128]{2,1,0:T(8,128)(2,1)S(1)}, u32[]{:S(2)}, u32[]{:S(2)}) collective-permute-start(bf16[1,576,128]{2,1,0:T(8,128)(2,1)} %collective-permute-done.2.rest_2_), channel_id=1, source_target_pairs={{0,8},{8,0},{1,9},{9,1},{2,10},{10,2},{3,11},{11,3},{4,12},{12,4},... | collective-permute-start | bytes 442376 | tf_op jit(solution)/shard_map/ppermute | solution.py:31
  64.7 1.5 collective-permute-done.6.rest_3_
  66.3 7.3 %shard_map.94 = bf16[256,1152]{1,0:T(8,128)(2,1)S(1)} custom-call(s32[8]{0:T(128)S(1)} %get-tuple-element.19.starts, s32[4]{0:T(128)S(1)} %pad_add_fusion.place, bf16[8,576,256]{2,1,0:T(8,128)(2,1)S(1)} %get-tuple-element.21.query, bf16[2,576,128]{2,1,0:T(8,128)(2,1)} %collective-permute-done.1.rest_0_, ...), custom_call_target="tpu_custom_call" | custom-call | tf_op jit(solution)/shard_map/pallas_call | solution.py:245
  73.5 13.9 %all_to_all.25.parts = bf16[4,64,1152]{2,1,0:T(8,128)(2,1)} all-to-all(bf16[4,64,1152]{2,1,0:T(8,128)(2,1)S(1)} %bitcast.38), channel_id=1, replica_groups=mesh['y'=4,'z'=8,'c'=2,'x'=4,'h'=2] {'y'}, dimensions={0} | all-to-all | bytes 1179648 | tf_op jit(solution)/shard_map/all_to_all | solution.py:47
  87.4 2.4 %shard_map.95 = bf16[4,64,1024]{2,1,0:T(8,128)(2,1)} custom-call(s32[1]{0:T(128)} %bitcast.5.half, bf16[4,64,1152]{2,1,0:T(8,128)(2,1)} %all_to_all.25.parts), custom_call_target="tpu_custom_call" | custom-call | tf_op jit(solution)/shard_map/pallas_call | solution.py:290
  89.8 2.0 %collective-permute-start.7 = (bf16[896,1024]{1,0:T(8,128)(2,1)}, bf16[896,1024]{1,0:T(8,128)(2,1)S(1)}, u32[]{:S(2)}, u32[]{:S(2)}) collective-permute-start(bf16[896,1024]{1,0:T(8,128)(2,1)} %all-gather.2.cloned.1.call-done), channel_id=1, source_target_pairs={{0,8},{8,0},{1,9},{9,1},{2,10},{10,2},{3,11},{11,3},{4,12},{12,4},... | collective-permute-start | bytes 5505032 | tf_op jit(solution)/shard_map/ppermute | solution.py:31
  91.9 13.9 %all_to_all.26 = bf16[4,64,1024]{2,1,0:T(8,128)(2,1)S(1)} all-to-all(bf16[4,64,1024]{2,1,0:T(8,128)(2,1)} %shard_map.95), channel_id=1, replica_groups=mesh['y'=4,'z'=8,'c'=2,'x'=4,'h'=2] {'y'}, dimensions={0} | all-to-all | bytes 1048576 | tf_op jit(solution)/shard_map/all_to_all | solution.py:47
  105.8 0.7 convolution_convert_fusion.3
  106.5 0.7 convolution_convert_fusion.1
  108.0 0.8 maximum_bitcast_fusion.1
  108.8 5.0 %all-to-all-start.4 = ((bf16[16,8,1792]{2,1,0:T(8,128)(2,1)}), bf16[16,8,1792]{2,1,0:T(8,128)(2,1)S(1)}, u32[]{:S(2)}, u32[]{:S(2)}) async-start(bf16[16,8,1792]{2,1,0:T(8,128)(2,1)} %maximum_bitcast_fusion.1), calls=%async_computation.4 | async-start | bytes 917504 | tf_op jit(solution)/shard_map/all_to_all | solution.py:370
  114.5 0.8 maximum_bitcast_fusion
  115.3 8.8 %all-to-all-done.4 = bf16[16,8,1792]{2,1,0:T(8,128)(2,1)S(1)} async-done(((bf16[16,8,1792]{2,1,0:T(8,128)(2,1)}), bf16[16,8,1792]{2,1,0:T(8,128)(2,1)S(1)}, u32[]{:S(2)}, u32[]{:S(2)}) %all-to-all-start.4) | async-done | bytes 458784 | tf_op jit(solution)/shard_map/all_to_all | solution.py:370
  124.1 3.6 %all-to-all-start.3 = ((bf16[16,8,1792]{2,1,0:T(8,128)(2,1)}), bf16[16,8,1792]{2,1,0:T(8,128)(2,1)S(1)}, u32[]{:S(2)}, u32[]{:S(2)}) async-start(bf16[16,8,1792]{2,1,0:T(8,128)(2,1)} %maximum_bitcast_fusion), calls=%async_computation.3 | async-start | bytes 917504 | tf_op jit(solution)/shard_map/all_to_all | solution.py:370
  127.8 10.2 %collective-permute-start.8 = (bf16[4,8,1792]{2,1,0:T(8,128)(2,1)S(1)}, bf16[4,8,1792]{2,1,0:T(8,128)(2,1)S(1)}, u32[]{:S(2)}, u32[]{:S(2)}) collective-permute-start(bf16[4,8,1792]{2,1,0:T(8,128)(2,1)S(1)} %bitcast_reduce_fusion), channel_id=1, source_target_pairs={{0,1},{1,0},{2,3},{3,2},{4,5},{5,4},{6,7},{7,6},{8,9},{9,8},{10,11... | collective-permute-start | bytes 344072 | tf_op jit(solution)/shard_map/ppermute | solution.py:31
  138.0 11.1 %collective-permute-done.8 = bf16[4,8,1792]{2,1,0:T(8,128)(2,1)S(1)} collective-permute-done((bf16[4,8,1792]{2,1,0:T(8,128)(2,1)S(1)}, bf16[4,8,1792]{2,1,0:T(8,128)(2,1)S(1)}, u32[]{:S(2)}, u32[]{:S(2)}) %collective-permute-start.8) | collective-permute-done | bytes 114720 | tf_op jit(solution)/shard_map/ppermute | solution.py:31
  149.5 0.8 reshape.46
  (32 shorter events, 3.1 us)
Async XLA Ops:
  6.5 20.3 %copy-start.3 = (bf16[512,8,128]{2,1,0:T(8,128)(2,1)S(1)}, bf16[512,8,128]{2,1,0:T(8,128)(2,1)}, u32[]{:S(2)}) copy-start(bf16[512,8,128]{2,1,0:T(8,128)(2,1)} %param.12) | copy-start | bytes 3145732
  6.5 83.3 %all-gather.2.cloned.1.call-start = ((), (), s32[]{:S(2)}) async-start(), calls=%async_computation.5 | async-start | bytes 2064384 | tf_op jit(solution)/shard_map/all_gather | solution.py:319
  9.5 17.6 %copy-start = (bf16[1152,128]{1,0:T(8,128)(2,1)}, bf16[1152,128]{1,0:T(8,128)(2,1)S(1)}, u32[]{:S(2)}) copy-start(bf16[1152,128]{1,0:T(8,128)(2,1)S(1)} %all_gather.6) | copy-start | bytes 884740
  9.5 20.0 %collective-permute-start = (bf16[2,576,128]{2,1,0:T(8,128)(2,1)S(1)}, bf16[2,576,128]{2,1,0:T(8,128)(2,1)}, u32[]{:S(2)}, u32[]{:S(2)}) collective-permute-start(bf16[2,576,128]{2,1,0:T(8,128)(2,1)S(1)} %bitcast.39), channel_id=1, source_target_pairs={{0,32},{1,33},{8,105},{9,104},{16,48},{17,49},{24,121},{25,120},{3... | collective-permute-start | bytes 884744 | tf_op jit(solution)/shard_map/ppermute | solution.py:31
  14.7 14.8 %collective-permute-start.3 = (bf16[2,576,128]{2,1,0:T(8,128)(2,1)S(1)}, bf16[2,576,128]{2,1,0:T(8,128)(2,1)}, u32[]{:S(2)}, u32[]{:S(2)}) collective-permute-start(bf16[2,576,128]{2,1,0:T(8,128)(2,1)S(1)} %bitcast.40), channel_id=1, source_target_pairs={{0,16},{1,17},{8,121},{9,120},{16,32},{17,33},{24,8},{25,9},{32,48... | collective-permute-start | bytes 884744 | tf_op jit(solution)/shard_map/ppermute | solution.py:31
  22.3 22.3 %all-to-all-start = ((bf16[4,64,1664]{2,1,0:T(8,128)(2,1)}), bf16[4,64,1664]{2,1,0:T(8,128)(2,1)S(1)}, u32[]{:S(2)}, u32[]{:S(2)}) async-start(bf16[4,64,1664]{2,1,0:T(8,128)(2,1)} %shard_map.91), calls=%async_computation | async-start | bytes 1703936 | tf_op jit(solution)/shard_map/all_to_all | solution.py:47
  31.5 14.4 %collective-permute-start.4 = (bf16[4,576,128]{2,1,0:T(8,128)(2,1)S(1)}, bf16[4,576,128]{2,1,0:T(8,128)(2,1)}, u32[]{:S(2)}, u32[]{:S(2)}) collective-permute-start(bf16[4,576,128]{2,1,0:T(8,128)(2,1)S(1)} %constant_dynamic-update-slice_fusion.rest_1_), channel_id=1, source_target_pairs={{0,8},{8,0},{1,9},{9,1},{2,10},{10,2},{3,11},{11,3},{4,12},{12,4},... | collective-permute-start | bytes 1769480 | tf_op jit(solution)/shard_map/ppermute | solution.py:31
  36.3 19.9 %collective-permute-start.1 = (bf16[2,576,128]{2,1,0:T(8,128)(2,1)}, bf16[2,576,128]{2,1,0:T(8,128)(2,1)}, u32[]{:S(2)}, u32[]{:S(2)}) collective-permute-start(bf16[2,576,128]{2,1,0:T(8,128)(2,1)} %collective-permute-done), channel_id=1, source_target_pairs={{0,16},{1,17},{8,121},{9,120},{16,32},{17,33},{24,8},{25,9},{32,48... | collective-permute-start | bytes 884744 | tf_op jit(solution)/shard_map/ppermute | solution.py:31
  40.9 15.3 %collective-permute-start.2 = (bf16[1,576,128]{2,1,0:T(8,128)(2,1)}, bf16[1,576,128]{2,1,0:T(8,128)(2,1)}, u32[]{:S(2)}, u32[]{:S(2)}) collective-permute-start(bf16[1,576,128]{2,1,0:T(8,128)(2,1)} %constant_dynamic-slice_fusion), channel_id=1, source_target_pairs={{0,32},{1,33},{8,105},{9,104},{16,48},{17,49},{24,121},{25,120},{3... | collective-permute-start | bytes 442376 | tf_op jit(solution)/shard_map/ppermute | solution.py:31
  44.7 1.2 copy-start.1
  56.3 10.0 %collective-permute-start.5 = (bf16[2,576,128]{2,1,0:T(8,128)(2,1)}, bf16[2,576,128]{2,1,0:T(8,128)(2,1)S(1)}, u32[]{:S(2)}, u32[]{:S(2)}) collective-permute-start(bf16[2,576,128]{2,1,0:T(8,128)(2,1)} %collective-permute-done.1.rest_0_), channel_id=1, source_target_pairs={{0,8},{8,0},{1,9},{9,1},{2,10},{10,2},{3,11},{11,3},{4,12},{12,4},... | collective-permute-start | bytes 884744 | tf_op jit(solution)/shard_map/ppermute | solution.py:31
  62.8 3.5 %collective-permute-start.6 = (bf16[1,576,128]{2,1,0:T(8,128)(2,1)}, bf16[1,576,128]{2,1,0:T(8,128)(2,1)S(1)}, u32[]{:S(2)}, u32[]{:S(2)}) collective-permute-start(bf16[1,576,128]{2,1,0:T(8,128)(2,1)} %collective-permute-done.2.rest_2_), channel_id=1, source_target_pairs={{0,8},{8,0},{1,9},{9,1},{2,10},{10,2},{3,11},{11,3},{4,12},{12,4},... | collective-permute-start | bytes 442376 | tf_op jit(solution)/shard_map/ppermute | solution.py:31
  89.8 16.0 %copy-start.2 = (bf16[896,1024]{1,0:T(8,128)(2,1)S(1)}, bf16[896,1024]{1,0:T(8,128)(2,1)}, u32[]{:S(2)}) copy-start(bf16[896,1024]{1,0:T(8,128)(2,1)} %all-gather.2.cloned.1.call-done) | copy-start | bytes 5505028
  89.8 17.4 %collective-permute-start.7 = (bf16[896,1024]{1,0:T(8,128)(2,1)}, bf16[896,1024]{1,0:T(8,128)(2,1)S(1)}, u32[]{:S(2)}, u32[]{:S(2)}) collective-permute-start(bf16[896,1024]{1,0:T(8,128)(2,1)} %all-gather.2.cloned.1.call-done), channel_id=1, source_target_pairs={{0,8},{8,0},{1,9},{9,1},{2,10},{10,2},{3,11},{11,3},{4,12},{12,4},... | collective-permute-start | bytes 5505032 | tf_op jit(solution)/shard_map/ppermute | solution.py:31
  108.8 15.3 %all-to-all-start.4 = ((bf16[16,8,1792]{2,1,0:T(8,128)(2,1)}), bf16[16,8,1792]{2,1,0:T(8,128)(2,1)S(1)}, u32[]{:S(2)}, u32[]{:S(2)}) async-start(bf16[16,8,1792]{2,1,0:T(8,128)(2,1)} %maximum_bitcast_fusion.1), calls=%async_computation.4 | async-start | bytes 917504 | tf_op jit(solution)/shard_map/all_to_all | solution.py:370
  124.1 13.8 %all-to-all-start.3 = ((bf16[16,8,1792]{2,1,0:T(8,128)(2,1)}), bf16[16,8,1792]{2,1,0:T(8,128)(2,1)S(1)}, u32[]{:S(2)}, u32[]{:S(2)}) async-start(bf16[16,8,1792]{2,1,0:T(8,128)(2,1)} %maximum_bitcast_fusion), calls=%async_computation.3 | async-start | bytes 917504 | tf_op jit(solution)/shard_map/all_to_all | solution.py:370
  127.8 21.4 %collective-permute-start.8 = (bf16[4,8,1792]{2,1,0:T(8,128)(2,1)S(1)}, bf16[4,8,1792]{2,1,0:T(8,128)(2,1)S(1)}, u32[]{:S(2)}, u32[]{:S(2)}) collective-permute-start(bf16[4,8,1792]{2,1,0:T(8,128)(2,1)S(1)} %bitcast_reduce_fusion), channel_id=1, source_target_pairs={{0,1},{1,0},{2,3},{3,2},{4,5},{5,4},{6,7},{7,6},{8,9},{9,8},{10,11... | collective-permute-start | bytes 344072 | tf_op jit(solution)/shard_map/ppermute | solution.py:31
Sparse Core Ops, SparseCore 0:
  9.4 73.7 all-gather.1

commit v9 on v8

--- a/solution.py
+++ b/solution.py
@@ -329,9 +329,12 @@
     two, _, key_up, value_up, place, half = lax.optimization_barrier(
         (two, packed, key_up, value_up, place, half)
     )
-    near = jnp.concatenate([one, two], axis=0)
+    own = lax.dynamic_slice_in_dim(two, c, 1)
+    three = along_z(two, 1)
+    own, one, near_two = lax.optimization_barrier((own, one, two))
+    four = along_z(own, 2)
+    near = jnp.concatenate([one, near_two], axis=0)
     near_swapped = other_core(near)
-    three, four = along_z(two, 1), along_z(lax.dynamic_slice_in_dim(two, c, 1), 2)
 
     payload = swap_y(packed).reshape(4 * tokens, -1)
     queries, starts = latent_queries(query_start, payload, key_up, heads, nope, rope, 8)

time: 158 us -> 157 us (level)
  transfers between devices with their start and end apart: 13 -> 13, of which waited for: 3 -> 4; matrix products, arithmetic and copies ran while one was open for 6% -> 5% of each run, Pallas kernels for 15% -> 15%
where the time goes in v9:
time: 157 us; the launch traced here: 156 us
  starting transfers between devices  54.4 us (35%)
  blocking collectives  30 us (19%)
  Pallas kernels  23.8 us (15%)
  waiting for transfers between devices  22.2 us (14%)
  between operations  15 us (10%)
  local copies, waits for them, and re-layouts  5.88 us (4%)
  matrix products  2.86 us (2%)
  other arithmetic  1.87 us (1%)
    ppermute x9, starting transfers between devices, permute(): return lax.ppermute(x, names, pairs)  41.5 us
    all_to_all x2, blocking collectives, swap_y(): return lax.all_to_all(x, 'y', split_axis=0, concat_axis=0, tiled=True)  27.7 us
    pallas_call x2, Pallas kernels, attend(): pl.pallas_call(kernel, in_specs=[pl.BlockSpec(memory_space=pltpu.SMEM)] *...  17.6 us
    ppermute x9, waiting for transfers between devices, permute(): return lax.ppermute(x, names, pairs)  12.2 us
    all_to_all x2, waiting for transfers between devices, summed(): lax.all_to_all(product.reshape(16, share, -1), ('y', 'x'), split_axis=0,...  9.34 us
    all_to_all x2, starting transfers between devices, summed(): lax.all_to_all(product.reshape(16, share, -1), ('y', 'x'), split_axis=0,...  8.41 us
    all_to_all x1, starting transfers between devices, swap_y(): return lax.all_to_all(x, 'y', split_axis=0, concat_axis=0, tiled=True)  4.46 us
  transfers between devices with their start and end apart: 13, of which 4 were waited for; matrix products, arithmetic and copies ran while one was open for 5% of the time, Pallas kernels for 15%

profile of v9, /device:TPU:32, one launch (start us, length us, event | category | flops | bytes accessed | tf_op | source)
XLA Modules:
  0.0 155.9 jit_solution(4204170474226075998)
XLA Ops:
  7.3 2.2 %all_gather.6 = bf16[1152,128]{1,0:T(8,128)(2,1)S(1)} all-gather(bf16[576,128]{1,0:T(8,128)(2,1)} %param.11), channel_id=1, replica_groups=mesh['y'=4,'z'=8,'c'=2,'x'=4,'h'=2] {'c'}, dimensions={0}, use_global_device_ids=true | all-gather | bytes 442368 | tf_op jit(solution)/shard_map/all_gather | solution.py:323
  9.5 5.2 %collective-permute-start = (bf16[2,576,128]{2,1,0:T(8,128)(2,1)S(1)}, bf16[2,576,128]{2,1,0:T(8,128)(2,1)S(1)}, u32[]{:S(2)}, u32[]{:S(2)}) collective-permute-start(bf16[2,576,128]{2,1,0:T(8,128)(2,1)S(1)} %bitcast.39), channel_id=1, source_target_pairs={{0,32},{1,33},{8,105},{9,104},{16,48},{17,49},{24,121},{25,120},{3... | collective-permute-start | bytes 884744 | tf_op jit(solution)/shard_map/ppermute | solution.py:31
  14.7 5.0 %collective-permute-start.2 = (bf16[2,576,128]{2,1,0:T(8,128)(2,1)S(1)}, bf16[2,576,128]{2,1,0:T(8,128)(2,1)}, u32[]{:S(2)}, u32[]{:S(2)}) collective-permute-start(bf16[2,576,128]{2,1,0:T(8,128)(2,1)S(1)} %bitcast.40), channel_id=1, source_target_pairs={{0,16},{1,17},{8,121},{9,120},{16,32},{17,33},{24,8},{25,9},{32,48... | collective-permute-start | bytes 884744 | tf_op jit(solution)/shard_map/ppermute | solution.py:31
  19.7 2.6 %shard_map.91 = bf16[4,64,1664]{2,1,0:T(8,128)(2,1)} custom-call(s32[2]{0:T(128)} %order.1, bf16[64,8,128]{2,1,0:T(8,128)(2,1)} %content.1, bf16[64,512]{1,0:T(8,128)(2,1)} %rotary.1), custom_call_target="tpu_custom_call" | custom-call | tf_op jit(solution)/shard_map/pallas_call | solution.py:67
  22.3 4.5 %all-to-all-start = ((bf16[4,64,1664]{2,1,0:T(8,128)(2,1)}), bf16[4,64,1664]{2,1,0:T(8,128)(2,1)S(1)}, u32[]{:S(2)}, u32[]{:S(2)}) async-start(bf16[4,64,1664]{2,1,0:T(8,128)(2,1)} %shard_map.91), calls=%async_computation | async-start | bytes 1703936 | tf_op jit(solution)/shard_map/all_to_all | solution.py:47
  27.1 1.6 %copy.12 = bf16[512,8,128]{0,2,1:T(8,128)(2,1)S(1)} copy(bf16[512,8,128]{2,1,0:T(8,128)(2,1)} %param.13) | data formatting | bytes 2097152 | tf_op args[4]
  30.2 1.0 constant_dynamic-update-slice_fusion.1
  31.2 1.0 constant_dynamic-update-slice_fusion.rest_1_
  32.2 4.9 %collective-permute-start.4 = (bf16[4,576,128]{2,1,0:T(8,128)(2,1)S(1)}, bf16[4,576,128]{2,1,0:T(8,128)(2,1)}, u32[]{:S(2)}, u32[]{:S(2)}) collective-permute-start(bf16[4,576,128]{2,1,0:T(8,128)(2,1)S(1)} %constant_dynamic-update-slice_fusion.rest_1_), channel_id=1, source_target_pairs={{0,8},{8,0},{1,9},{9,1},{2,10},{10,2},{3,11},{11,3},{4,12},{12,4},... | collective-permute-start | bytes 1769480 | tf_op jit(solution)/shard_map/ppermute | solution.py:31
  37.1 3.0 %collective-permute-start.1 = (bf16[2,576,128]{2,1,0:T(8,128)(2,1)}, bf16[2,576,128]{2,1,0:T(8,128)(2,1)}, u32[]{:S(2)}, u32[]{:S(2)}) collective-permute-start(bf16[2,576,128]{2,1,0:T(8,128)(2,1)} %copy-done.4), channel_id=1, source_target_pairs={{0,16},{1,17},{8,121},{9,120},{16,32},{17,33},{24,8},{25,9},{32,48... | collective-permute-start | bytes 884744 | tf_op jit(solution)/shard_map/ppermute | solution.py:31
  40.1 3.1 %collective-permute-start.3 = (bf16[1,576,128]{2,1,0:T(8,128)(2,1)}, bf16[1,576,128]{2,1,0:T(8,128)(2,1)}, u32[]{:S(2)}, u32[]{:S(2)}) collective-permute-start(bf16[1,576,128]{2,1,0:T(8,128)(2,1)} %constant_dynamic-slice_fusion), channel_id=1, source_target_pairs={{0,32},{1,33},{8,105},{9,104},{16,48},{17,49},{24,121},{25,120},{3... | collective-permute-start | bytes 442376 | tf_op jit(solution)/shard_map/ppermute | solution.py:31
  43.8 1.2 shard_map.92
  45.1 10.3 %shard_map.93.rest_5_ = bf16[256,1152]{1,0:T(8,128)(2,1)S(1)} custom-call(s32[8]{0:T(128)S(1)} %get-tuple-element.22.starts, s32[4]{0:T(128)S(1)} %pad_add_fusion.place, bf16[8,576,256]{2,1,0:T(8,128)(2,1)S(1)} %get-tuple-element.24.query, bf16[2,576,128]{2,1,0:T(8,128)(2,1)S(1)} %bitcast.41, ...), custom_call_target="tpu_custom_call" | custom-call | tf_op jit(solution)/shard_map/pallas_call | solution.py:245
  55.4 7.3 %collective-permute-start.5 = (bf16[2,576,128]{2,1,0:T(8,128)(2,1)}, bf16[2,576,128]{2,1,0:T(8,128)(2,1)S(1)}, u32[]{:S(2)}, u32[]{:S(2)}) collective-permute-start(bf16[2,576,128]{2,1,0:T(8,128)(2,1)} %collective-permute-done.1.rest_0_), channel_id=1, source_target_pairs={{0,8},{8,0},{1,9},{9,1},{2,10},{10,2},{3,11},{11,3},{4,12},{12,4},... | collective-permute-start | bytes 884744 | tf_op jit(solution)/shard_map/ppermute | solution.py:31
  62.7 1.9 %collective-permute-start.6 = (bf16[1,576,128]{2,1,0:T(8,128)(2,1)}, bf16[1,576,128]{2,1,0:T(8,128)(2,1)S(1)}, u32[]{:S(2)}, u32[]{:S(2)}) collective-permute-start(bf16[1,576,128]{2,1,0:T(8,128)(2,1)} %collective-permute-done.3.rest_2_), channel_id=1, source_target_pairs={{0,8},{8,0},{1,9},{9,1},{2,10},{10,2},{3,11},{11,3},{4,12},{12,4},... | collective-permute-start | bytes 442376 | tf_op jit(solution)/shard_map/ppermute | solution.py:31
  64.6 1.5 collective-permute-done.6.rest_3_
  66.2 7.3 %shard_map.94 = bf16[256,1152]{1,0:T(8,128)(2,1)S(1)} custom-call(s32[8]{0:T(128)S(1)} %get-tuple-element.22.starts, s32[4]{0:T(128)S(1)} %pad_add_fusion.place, bf16[8,576,256]{2,1,0:T(8,128)(2,1)S(1)} %get-tuple-element.24.query, bf16[2,576,128]{2,1,0:T(8,128)(2,1)} %collective-permute-done.1.rest_0_, ...), custom_call_target="tpu_custom_call" | custom-call | tf_op jit(solution)/shard_map/pallas_call | solution.py:245
  73.4 13.9 %all_to_all.25.parts = bf16[4,64,1152]{2,1,0:T(8,128)(2,1)} all-to-all(bf16[4,64,1152]{2,1,0:T(8,128)(2,1)S(1)} %bitcast.38), channel_id=1, replica_groups=mesh['y'=4,'z'=8,'c'=2,'x'=4,'h'=2] {'y'}, dimensions={0} | all-to-all | bytes 1179648 | tf_op jit(solution)/shard_map/all_to_all | solution.py:47
  87.3 2.4 %shard_map.95 = bf16[4,64,1024]{2,1,0:T(8,128)(2,1)} custom-call(s32[1]{0:T(128)} %bitcast.5.half, bf16[4,64,1152]{2,1,0:T(8,128)(2,1)} %all_to_all.25.parts), custom_call_target="tpu_custom_call" | custom-call | tf_op jit(solution)/shard_map/pallas_call | solution.py:290
  89.7 2.0 %collective-permute-start.7 = (bf16[896,1024]{1,0:T(8,128)(2,1)}, bf16[896,1024]{1,0:T(8,128)(2,1)S(1)}, u32[]{:S(2)}, u32[]{:S(2)}) collective-permute-start(bf16[896,1024]{1,0:T(8,128)(2,1)} %all-gather.2.cloned.1.call-done), channel_id=1, source_target_pairs={{0,8},{8,0},{1,9},{9,1},{2,10},{10,2},{3,11},{11,3},{4,12},{12,4},... | collective-permute-start | bytes 5505032 | tf_op jit(solution)/shard_map/ppermute | solution.py:31
  91.8 13.9 %all_to_all.26 = bf16[4,64,1024]{2,1,0:T(8,128)(2,1)S(1)} all-to-all(bf16[4,64,1024]{2,1,0:T(8,128)(2,1)} %shard_map.95), channel_id=1, replica_groups=mesh['y'=4,'z'=8,'c'=2,'x'=4,'h'=2] {'y'}, dimensions={0} | all-to-all | bytes 1048576 | tf_op jit(solution)/shard_map/all_to_all | solution.py:47
  105.7 0.7 convolution_convert_fusion.3
  106.4 0.7 convolution_convert_fusion.1
  107.2 0.7 convolution_convert_fusion
  107.9 0.8 maximum_bitcast_fusion.1
  108.7 4.8 %all-to-all-start.4 = ((bf16[16,8,1792]{2,1,0:T(8,128)(2,1)}), bf16[16,8,1792]{2,1,0:T(8,128)(2,1)S(1)}, u32[]{:S(2)}, u32[]{:S(2)}) async-start(bf16[16,8,1792]{2,1,0:T(8,128)(2,1)} %maximum_bitcast_fusion.1), calls=%async_computation.4 | async-start | bytes 917504 | tf_op jit(solution)/shard_map/all_to_all | solution.py:373
  114.2 0.8 maximum_bitcast_fusion
  115.0 8.9 %all-to-all-done.4 = bf16[16,8,1792]{2,1,0:T(8,128)(2,1)S(1)} async-done(((bf16[16,8,1792]{2,1,0:T(8,128)(2,1)}), bf16[16,8,1792]{2,1,0:T(8,128)(2,1)S(1)}, u32[]{:S(2)}, u32[]{:S(2)}) %all-to-all-start.4) | async-done | bytes 458784 | tf_op jit(solution)/shard_map/all_to_all | solution.py:373
  123.9 3.6 %all-to-all-start.3 = ((bf16[16,8,1792]{2,1,0:T(8,128)(2,1)}), bf16[16,8,1792]{2,1,0:T(8,128)(2,1)S(1)}, u32[]{:S(2)}, u32[]{:S(2)}) async-start(bf16[16,8,1792]{2,1,0:T(8,128)(2,1)} %maximum_bitcast_fusion), calls=%async_computation.3 | async-start | bytes 917504 | tf_op jit(solution)/shard_map/all_to_all | solution.py:373
  127.5 9.1 %collective-permute-start.8 = (bf16[4,8,1792]{2,1,0:T(8,128)(2,1)S(1)}, bf16[4,8,1792]{2,1,0:T(8,128)(2,1)S(1)}, u32[]{:S(2)}, u32[]{:S(2)}) collective-permute-start(bf16[4,8,1792]{2,1,0:T(8,128)(2,1)S(1)} %bitcast_reduce_fusion), channel_id=1, source_target_pairs={{0,1},{1,0},{2,3},{3,2},{4,5},{5,4},{6,7},{7,6},{8,9},{9,8},{10,11... | collective-permute-start | bytes 344072 | tf_op jit(solution)/shard_map/ppermute | solution.py:31
  137.2 10.6 %collective-permute-done.8 = bf16[4,8,1792]{2,1,0:T(8,128)(2,1)S(1)} collective-permute-done((bf16[4,8,1792]{2,1,0:T(8,128)(2,1)S(1)}, bf16[4,8,1792]{2,1,0:T(8,128)(2,1)S(1)}, u32[]{:S(2)}, u32[]{:S(2)}) %collective-permute-start.8) | collective-permute-done | bytes 114720 | tf_op jit(solution)/shard_map/ppermute | solution.py:31
  148.2 0.8 reshape.46
  (34 shorter events, 3.6 us)
Async XLA Ops:
  6.5 20.3 %copy-start.3 = (bf16[512,8,128]{2,1,0:T(8,128)(2,1)S(1)}, bf16[512,8,128]{2,1,0:T(8,128)(2,1)}, u32[]{:S(2)}) copy-start(bf16[512,8,128]{2,1,0:T(8,128)(2,1)} %param.12) | copy-start | bytes 3145732
  6.5 83.2 %all-gather.2.cloned.1.call-start = ((), (), s32[]{:S(2)}) async-start(), calls=%async_computation.5 | async-start | bytes 2064384 | tf_op jit(solution)/shard_map/all_gather | solution.py:319
  9.5 17.6 %copy-start = (bf16[1152,128]{1,0:T(8,128)(2,1)}, bf16[1152,128]{1,0:T(8,128)(2,1)S(1)}, u32[]{:S(2)}) copy-start(bf16[1152,128]{1,0:T(8,128)(2,1)S(1)} %all_gather.6) | copy-start | bytes 884740
  9.5 20.0 %collective-permute-start = (bf16[2,576,128]{2,1,0:T(8,128)(2,1)S(1)}, bf16[2,576,128]{2,1,0:T(8,128)(2,1)S(1)}, u32[]{:S(2)}, u32[]{:S(2)}) collective-permute-start(bf16[2,576,128]{2,1,0:T(8,128)(2,1)S(1)} %bitcast.39), channel_id=1, source_target_pairs={{0,32},{1,33},{8,105},{9,104},{16,48},{17,49},{24,121},{25,120},{3... | collective-permute-start | bytes 884744 | tf_op jit(solution)/shard_map/ppermute | solution.py:31
  14.7 15.6 %collective-permute-start.2 = (bf16[2,576,128]{2,1,0:T(8,128)(2,1)S(1)}, bf16[2,576,128]{2,1,0:T(8,128)(2,1)}, u32[]{:S(2)}, u32[]{:S(2)}) collective-permute-start(bf16[2,576,128]{2,1,0:T(8,128)(2,1)S(1)} %bitcast.40), channel_id=1, source_target_pairs={{0,16},{1,17},{8,121},{9,120},{16,32},{17,33},{24,8},{25,9},{32,48... | collective-permute-start | bytes 884744 | tf_op jit(solution)/shard_map/ppermute | solution.py:31
  22.3 21.5 %all-to-all-start = ((bf16[4,64,1664]{2,1,0:T(8,128)(2,1)}), bf16[4,64,1664]{2,1,0:T(8,128)(2,1)S(1)}, u32[]{:S(2)}, u32[]{:S(2)}) async-start(bf16[4,64,1664]{2,1,0:T(8,128)(2,1)} %shard_map.91), calls=%async_computation | async-start | bytes 1703936 | tf_op jit(solution)/shard_map/all_to_all | solution.py:47
  29.4 0.8 copy-start.4
  32.2 12.8 %collective-permute-start.4 = (bf16[4,576,128]{2,1,0:T(8,128)(2,1)S(1)}, bf16[4,576,128]{2,1,0:T(8,128)(2,1)}, u32[]{:S(2)}, u32[]{:S(2)}) collective-permute-start(bf16[4,576,128]{2,1,0:T(8,128)(2,1)S(1)} %constant_dynamic-update-slice_fusion.rest_1_), channel_id=1, source_target_pairs={{0,8},{8,0},{1,9},{9,1},{2,10},{10,2},{3,11},{11,3},{4,12},{12,4},... | collective-permute-start | bytes 1769480 | tf_op jit(solution)/shard_map/ppermute | solution.py:31
  37.1 18.3 %collective-permute-start.1 = (bf16[2,576,128]{2,1,0:T(8,128)(2,1)}, bf16[2,576,128]{2,1,0:T(8,128)(2,1)}, u32[]{:S(2)}, u32[]{:S(2)}) collective-permute-start(bf16[2,576,128]{2,1,0:T(8,128)(2,1)} %copy-done.4), channel_id=1, source_target_pairs={{0,16},{1,17},{8,121},{9,120},{16,32},{17,33},{24,8},{25,9},{32,48... | collective-permute-start | bytes 884744 | tf_op jit(solution)/shard_map/ppermute | solution.py:31
  40.1 15.3 %collective-permute-start.3 = (bf16[1,576,128]{2,1,0:T(8,128)(2,1)}, bf16[1,576,128]{2,1,0:T(8,128)(2,1)}, u32[]{:S(2)}, u32[]{:S(2)}) collective-permute-start(bf16[1,576,128]{2,1,0:T(8,128)(2,1)} %constant_dynamic-slice_fusion), channel_id=1, source_target_pairs={{0,32},{1,33},{8,105},{9,104},{16,48},{17,49},{24,121},{25,120},{3... | collective-permute-start | bytes 442376 | tf_op jit(solution)/shard_map/ppermute | solution.py:31
  43.8 1.2 copy-start.1
  55.4 10.7 %collective-permute-start.5 = (bf16[2,576,128]{2,1,0:T(8,128)(2,1)}, bf16[2,576,128]{2,1,0:T(8,128)(2,1)S(1)}, u32[]{:S(2)}, u32[]{:S(2)}) collective-permute-start(bf16[2,576,128]{2,1,0:T(8,128)(2,1)} %collective-permute-done.1.rest_0_), channel_id=1, source_target_pairs={{0,8},{8,0},{1,9},{9,1},{2,10},{10,2},{3,11},{11,3},{4,12},{12,4},... | collective-permute-start | bytes 884744 | tf_op jit(solution)/shard_map/ppermute | solution.py:31
  62.7 3.5 %collective-permute-start.6 = (bf16[1,576,128]{2,1,0:T(8,128)(2,1)}, bf16[1,576,128]{2,1,0:T(8,128)(2,1)S(1)}, u32[]{:S(2)}, u32[]{:S(2)}) collective-permute-start(bf16[1,576,128]{2,1,0:T(8,128)(2,1)} %collective-permute-done.3.rest_2_), channel_id=1, source_target_pairs={{0,8},{8,0},{1,9},{9,1},{2,10},{10,2},{3,11},{11,3},{4,12},{12,4},... | collective-permute-start | bytes 442376 | tf_op jit(solution)/shard_map/ppermute | solution.py:31
  89.7 16.0 %copy-start.2 = (bf16[896,1024]{1,0:T(8,128)(2,1)S(1)}, bf16[896,1024]{1,0:T(8,128)(2,1)}, u32[]{:S(2)}) copy-start(bf16[896,1024]{1,0:T(8,128)(2,1)} %all-gather.2.cloned.1.call-done) | copy-start | bytes 5505028
  89.7 17.4 %collective-permute-start.7 = (bf16[896,1024]{1,0:T(8,128)(2,1)}, bf16[896,1024]{1,0:T(8,128)(2,1)S(1)}, u32[]{:S(2)}, u32[]{:S(2)}) collective-permute-start(bf16[896,1024]{1,0:T(8,128)(2,1)} %all-gather.2.cloned.1.call-done), channel_id=1, source_target_pairs={{0,8},{8,0},{1,9},{9,1},{2,10},{10,2},{3,11},{11,3},{4,12},{12,4},... | collective-permute-start | bytes 5505032 | tf_op jit(solution)/shard_map/ppermute | solution.py:31
  108.7 15.2 %all-to-all-start.4 = ((bf16[16,8,1792]{2,1,0:T(8,128)(2,1)}), bf16[16,8,1792]{2,1,0:T(8,128)(2,1)S(1)}, u32[]{:S(2)}, u32[]{:S(2)}) async-start(bf16[16,8,1792]{2,1,0:T(8,128)(2,1)} %maximum_bitcast_fusion.1), calls=%async_computation.4 | async-start | bytes 917504 | tf_op jit(solution)/shard_map/all_to_all | solution.py:373
  123.9 13.3 %all-to-all-start.3 = ((bf16[16,8,1792]{2,1,0:T(8,128)(2,1)}), bf16[16,8,1792]{2,1,0:T(8,128)(2,1)S(1)}, u32[]{:S(2)}, u32[]{:S(2)}) async-start(bf16[16,8,1792]{2,1,0:T(8,128)(2,1)} %maximum_bitcast_fusion), calls=%async_computation.3 | async-start | bytes 917504 | tf_op jit(solution)/shard_map/all_to_all | solution.py:373
  127.5 20.3 %collective-permute-start.8 = (bf16[4,8,1792]{2,1,0:T(8,128)(2,1)S(1)}, bf16[4,8,1792]{2,1,0:T(8,128)(2,1)S(1)}, u32[]{:S(2)}, u32[]{:S(2)}) collective-permute-start(bf16[4,8,1792]{2,1,0:T(8,128)(2,1)S(1)} %bitcast_reduce_fusion), channel_id=1, source_target_pairs={{0,1},{1,0},{2,3},{3,2},{4,5},{5,4},{6,7},{7,6},{8,9},{9,8},{10,11... | collective-permute-start | bytes 344072 | tf_op jit(solution)/shard_map/ppermute | solution.py:31
Sparse Core Ops, SparseCore 0:
  9.4 73.6 all-gather.1

commit v10 on v9

--- a/solution.py
+++ b/solution.py
@@ -13,6 +13,7 @@
 LOG2E = 1.4426950408889634
 SIZES = {"y": 4, "z": 8, "c": 2, "x": 4, "h": 2}
 NAMES = tuple(SIZES)
+RING = (0, 2, 4, 6, 7, 5, 3, 1)
 STATS = 128
 MINE, OTHER = 2, 3
 
@@ -297,6 +298,34 @@
     )(half, parts)
 
 
+def assemble_kernel(core, mine, got, out, *, columns):
+    ring = len(RING)
+    for y in range(mine.shape[0]):
+        total = mine[y] + got[y].astype(jnp.float32)
+        own, other = total[:, : ring * columns], total[:, ring * columns :]
+        cores = [jnp.where(core[0] == n, own, other) for n in (0, 1)]
+        pieces = []
+        for z in range(ring):
+            at = RING.index(z) * columns
+            pieces += [cores[n][:, at : at + columns] for n in (0, 1)]
+        row = jnp.concatenate(pieces, axis=1)
+        out[:, y * row.shape[1] : (y + 1) * row.shape[1]] = row.astype(out.dtype)
+
+
+def assemble(core, mine, got, columns):
+    count, share, width = mine.shape
+    return pl.pallas_call(
+        functools.partial(assemble_kernel, columns=columns),
+        in_specs=[
+            pl.BlockSpec(memory_space=pltpu.SMEM),
+            pl.BlockSpec(memory_space=pltpu.VMEM),
+            pl.BlockSpec(memory_space=pltpu.VMEM),
+        ],
+        out_specs=pl.BlockSpec(memory_space=pltpu.VMEM),
+        out_shape=jax.ShapeDtypeStruct((share, count * width), jnp.bfloat16),
+    )(core, mine, got)
+
+
 def per_device(
     query_content,
     query_rotary,
@@ -316,7 +345,9 @@
     scale = 1.0 / math.sqrt(nope + rope)
     y, z, c, h = (lax.axis_index(n) for n in ("y", "z", "c", "h"))
 
-    weight = lax.all_gather(output_weight.T, "z", axis=0, tiled=True)
+    weight = lax.all_gather(
+        output_weight.T, "z", axis=0, tiled=True, axis_index_groups=[list(RING)]
+    )
 
     packed = pack(block_order, query_content, query_rotary, block, 4)
 
@@ -331,6 +362,7 @@
     )
     own = lax.dynamic_slice_in_dim(two, c, 1)
     three = along_z(two, 1)
+
     own, one, near_two = lax.optimization_barrier((own, one, two))
     four = along_z(own, 2)
     near = jnp.concatenate([one, near_two], axis=0)
@@ -378,10 +410,7 @@
     theirs = summed(rows[:, : tokens // 2]).astype(jnp.bfloat16)
     got = permute(theirs, ("h",), lambda at: {"h": 1 - at["h"]})
     mine = summed(rows[:, tokens // 2 :])
-    total = (mine + got.astype(jnp.float32)).astype(jnp.bfloat16)
-    total = total.reshape(4, share, 2, 8, columns)
-    total = jnp.where(c == 0, total, total[:, :, ::-1])
-    return total.transpose(1, 0, 3, 2, 4).reshape(share, 16 * 4 * columns)
+    return assemble(c.astype(jnp.int32)[None], mine, got, columns)
 
 
 def solution(mesh):

time: 157 us -> 164 us (1.045)
  the two profiles are of different devices: /device:TPU:32 before, /device:TPU:162 now
where the time goes in v10:
time: 164 us; the launch traced here: 163 us
  starting transfers between devices  43.6 us (27%)
  waiting for transfers between devices  36.8 us (22%)
  blocking collectives  31.2 us (19%)
  Pallas kernels  25.6 us (16%)
  between operations  14.9 us (9%)
  local copies, waits for them, and re-layouts  5.35 us (3%)
  matrix products  2.86 us (2%)
  other arithmetic  2.51 us (2%)
    all_to_all x2, blocking collectives, swap_y(): return lax.all_to_all(x, 'y', split_axis=0, concat_axis=0, tiled=True)  28.9 us
    ppermute x9, starting transfers between devices, permute(): return lax.ppermute(x, names, pairs)  28.7 us
    ppermute x9, waiting for transfers between devices, permute(): return lax.ppermute(x, names, pairs)  24 us
    pallas_call x2, Pallas kernels, attend(): pl.pallas_call(kernel, in_specs=[pl.BlockSpec(memory_space=pltpu.SMEM)] *...  17.6 us
    all_to_all x2, waiting for transfers between devices, summed(): lax.all_to_all(product.reshape(16, share, -1), ('y', 'x'), split_axis=0,...  12.1 us
    all_to_all x2, starting transfers between devices, summed(): lax.all_to_all(product.reshape(16, share, -1), ('y', 'x'), split_axis=0,...  10.4 us
    all_to_all x1, starting transfers between devices, swap_y(): return lax.all_to_all(x, 'y', split_axis=0, concat_axis=0, tiled=True)  4.46 us
    unnamed x15, local copies, waits for them, and re-layouts  3.6 us
  transfers between devices with their start and end apart: 13, of which 5 were waited for; matrix products, arithmetic and copies ran while one was open for 5% of the time, Pallas kernels for 15%

profile of v10, /device:TPU:162, one launch (start us, length us, event | category | flops | bytes accessed | tf_op | source)
XLA Modules:
  0.0 162.8 jit_solution(4912688800694110965)
XLA Ops:
  7.3 2.2 %all_gather.6 = bf16[1152,128]{1,0:T(8,128)(2,1)S(1)} all-gather(bf16[576,128]{1,0:T(8,128)(2,1)} %param.11), channel_id=1, replica_groups=mesh['y'=4,'z'=8,'c'=2,'x'=4,'h'=2] {'c'}, dimensions={0}, use_global_device_ids=true | all-gather | bytes 442368 | tf_op jit(solution)/shard_map/all_gather | solution.py:354
  9.5 5.2 %collective-permute-start = (bf16[2,576,128]{2,1,0:T(8,128)(2,1)S(1)}, bf16[2,576,128]{2,1,0:T(8,128)(2,1)S(1)}, u32[]{:S(2)}, u32[]{:S(2)}) collective-permute-start(bf16[2,576,128]{2,1,0:T(8,128)(2,1)S(1)} %bitcast.37), channel_id=1, source_target_pairs={{0,32},{1,33},{8,105},{9,104},{16,48},{17,49},{24,121},{25,120},{3... | collective-permute-start | bytes 884744 | tf_op jit(solution)/shard_map/ppermute | solution.py:32
  14.7 5.0 %collective-permute-start.2 = (bf16[2,576,128]{2,1,0:T(8,128)(2,1)S(1)}, bf16[2,576,128]{2,1,0:T(8,128)(2,1)}, u32[]{:S(2)}, u32[]{:S(2)}) collective-permute-start(bf16[2,576,128]{2,1,0:T(8,128)(2,1)S(1)} %bitcast.38), channel_id=1, source_target_pairs={{0,16},{1,17},{8,121},{9,120},{16,32},{17,33},{24,8},{25,9},{32,48... | collective-permute-start | bytes 884744 | tf_op jit(solution)/shard_map/ppermute | solution.py:32
  19.7 2.6 %shard_map.91 = bf16[4,64,1664]{2,1,0:T(8,128)(2,1)} custom-call(s32[2]{0:T(128)} %order.1, bf16[64,8,128]{2,1,0:T(8,128)(2,1)} %content.1, bf16[64,512]{1,0:T(8,128)(2,1)} %rotary.1), custom_call_target="tpu_custom_call" | custom-call | tf_op jit(solution)/shard_map/pallas_call | solution.py:68
  22.3 4.5 %all-to-all-start = ((bf16[4,64,1664]{2,1,0:T(8,128)(2,1)}), bf16[4,64,1664]{2,1,0:T(8,128)(2,1)S(1)}, u32[]{:S(2)}, u32[]{:S(2)}) async-start(bf16[4,64,1664]{2,1,0:T(8,128)(2,1)} %shard_map.91), calls=%async_computation | async-start | bytes 1703936 | tf_op jit(solution)/shard_map/all_to_all | solution.py:48
  27.1 1.6 %copy.10 = bf16[512,8,128]{0,2,1:T(8,128)(2,1)S(1)} copy(bf16[512,8,128]{2,1,0:T(8,128)(2,1)} %param.13) | data formatting | bytes 2097152 | tf_op args[4]
  30.2 1.0 constant_dynamic-update-slice_fusion.1
  31.2 1.0 constant_dynamic-update-slice_fusion.rest_1_
  32.2 1.9 %collective-permute-start.4 = (bf16[4,576,128]{2,1,0:T(8,128)(2,1)S(1)}, bf16[4,576,128]{2,1,0:T(8,128)(2,1)}, u32[]{:S(2)}, u32[]{:S(2)}) collective-permute-start(bf16[4,576,128]{2,1,0:T(8,128)(2,1)S(1)} %constant_dynamic-update-slice_fusion.rest_1_), channel_id=1, source_target_pairs={{0,8},{8,0},{1,9},{9,1},{2,10},{10,2},{3,11},{11,3},{4,12},{12,4},... | collective-permute-start | bytes 1769480 | tf_op jit(solution)/shard_map/ppermute | solution.py:32
  34.2 2.9 %collective-permute-start.1 = (bf16[2,576,128]{2,1,0:T(8,128)(2,1)}, bf16[2,576,128]{2,1,0:T(8,128)(2,1)}, u32[]{:S(2)}, u32[]{:S(2)}) collective-permute-start(bf16[2,576,128]{2,1,0:T(8,128)(2,1)} %copy-done.4), channel_id=1, source_target_pairs={{0,16},{1,17},{8,121},{9,120},{16,32},{17,33},{24,8},{25,9},{32,48... | collective-permute-start | bytes 884744 | tf_op jit(solution)/shard_map/ppermute | solution.py:32
  37.1 3.4 %collective-permute-start.3 = (bf16[1,576,128]{2,1,0:T(8,128)(2,1)}, bf16[1,576,128]{2,1,0:T(8,128)(2,1)}, u32[]{:S(2)}, u32[]{:S(2)}) collective-permute-start(bf16[1,576,128]{2,1,0:T(8,128)(2,1)} %constant_dynamic-slice_fusion), channel_id=1, source_target_pairs={{0,32},{1,33},{8,105},{9,104},{16,48},{17,49},{24,121},{25,120},{3... | collective-permute-start | bytes 442376 | tf_op jit(solution)/shard_map/ppermute | solution.py:32
  41.1 1.2 shard_map.92
  42.4 10.3 %shard_map.93.rest_5_ = bf16[256,1152]{1,0:T(8,128)(2,1)S(1)} custom-call(s32[8]{0:T(128)S(1)} %get-tuple-element.22.starts, s32[4]{0:T(128)S(1)} %pad_add_fusion.place, bf16[8,576,256]{2,1,0:T(8,128)(2,1)S(1)} %get-tuple-element.24.query, bf16[2,576,128]{2,1,0:T(8,128)(2,1)S(1)} %bitcast.39, ...), custom_call_target="tpu_custom_call" | custom-call | tf_op jit(solution)/shard_map/pallas_call | solution.py:246
  52.7 12.0 %collective-permute-done.3.rest_2_ = bf16[1,576,128]{2,1,0:T(8,128)(2,1)} collective-permute-done((bf16[1,576,128]{2,1,0:T(8,128)(2,1)}, bf16[1,576,128]{2,1,0:T(8,128)(2,1)}, u32[]{:S(2)}, u32[]{:S(2)}) %collective-permute-start.3) | collective-permute-done | bytes 147488 | tf_op jit(solution)/shard_map/ppermute | solution.py:32
  64.7 1.9 %collective-permute-start.5 = (bf16[2,576,128]{2,1,0:T(8,128)(2,1)}, bf16[2,576,128]{2,1,0:T(8,128)(2,1)S(1)}, u32[]{:S(2)}, u32[]{:S(2)}) collective-permute-start(bf16[2,576,128]{2,1,0:T(8,128)(2,1)} %collective-permute-done.1.rest_0_), channel_id=1, source_target_pairs={{0,8},{8,0},{1,9},{9,1},{2,10},{10,2},{3,11},{11,3},{4,12},{12,4},... | collective-permute-start | bytes 884744 | tf_op jit(solution)/shard_map/ppermute | solution.py:32
  66.6 2.4 %collective-permute-start.6 = (bf16[1,576,128]{2,1,0:T(8,128)(2,1)}, bf16[1,576,128]{2,1,0:T(8,128)(2,1)S(1)}, u32[]{:S(2)}, u32[]{:S(2)}) collective-permute-start(bf16[1,576,128]{2,1,0:T(8,128)(2,1)} %collective-permute-done.3.rest_2_), channel_id=1, source_target_pairs={{0,8},{8,0},{1,9},{9,1},{2,10},{10,2},{3,11},{11,3},{4,12},{12,4},... | collective-permute-start | bytes 442376 | tf_op jit(solution)/shard_map/ppermute | solution.py:32
  69.0 1.2 collective-permute-done.6.rest_3_
  70.2 7.3 %shard_map.94 = bf16[256,1152]{1,0:T(8,128)(2,1)S(1)} custom-call(s32[8]{0:T(128)S(1)} %get-tuple-element.22.starts, s32[4]{0:T(128)S(1)} %pad_add_fusion.place, bf16[8,576,256]{2,1,0:T(8,128)(2,1)S(1)} %get-tuple-element.24.query, bf16[2,576,128]{2,1,0:T(8,128)(2,1)} %collective-permute-done.1.rest_0_, ...), custom_call_target="tpu_custom_call" | custom-call | tf_op jit(solution)/shard_map/pallas_call | solution.py:246
  77.5 15.1 %all_to_all.25.parts = bf16[4,64,1152]{2,1,0:T(8,128)(2,1)} all-to-all(bf16[4,64,1152]{2,1,0:T(8,128)(2,1)S(1)} %bitcast.36), channel_id=1, replica_groups=mesh['y'=4,'z'=8,'c'=2,'x'=4,'h'=2] {'y'}, dimensions={0} | all-to-all | bytes 1179648 | tf_op jit(solution)/shard_map/all_to_all | solution.py:48
  92.6 2.4 %shard_map.95 = bf16[4,64,1024]{2,1,0:T(8,128)(2,1)} custom-call(s32[1]{0:T(128)} %bitcast.5.half, bf16[4,64,1152]{2,1,0:T(8,128)(2,1)} %all_to_all.25.parts), custom_call_target="tpu_custom_call" | custom-call | tf_op jit(solution)/shard_map/pallas_call | solution.py:291
  95.0 2.0 %collective-permute-start.7 = (bf16[896,1024]{1,0:T(8,128)(2,1)}, bf16[896,1024]{1,0:T(8,128)(2,1)S(1)}, u32[]{:S(2)}, u32[]{:S(2)}) collective-permute-start(bf16[896,1024]{1,0:T(8,128)(2,1)} %all-gather.2.cloned.1.call-done), channel_id=1, source_target_pairs={{0,8},{8,0},{1,9},{9,1},{2,10},{10,2},{3,11},{11,3},{4,12},{12,4},... | collective-permute-start | bytes 5505032 | tf_op jit(solution)/shard_map/ppermute | solution.py:32
  97.0 13.9 %all_to_all.26 = bf16[4,64,1024]{2,1,0:T(8,128)(2,1)S(1)} all-to-all(bf16[4,64,1024]{2,1,0:T(8,128)(2,1)} %shard_map.95), channel_id=1, replica_groups=mesh['y'=4,'z'=8,'c'=2,'x'=4,'h'=2] {'y'}, dimensions={0} | all-to-all | bytes 1048576 | tf_op jit(solution)/shard_map/all_to_all | solution.py:48
  113.1 0.8 maximum_bitcast_fusion.1
  113.9 5.7 %all-to-all-start.4 = ((bf16[16,8,1792]{2,1,0:T(8,128)(2,1)}), bf16[16,8,1792]{2,1,0:T(8,128)(2,1)S(1)}, u32[]{:S(2)}, u32[]{:S(2)}) async-start(bf16[16,8,1792]{2,1,0:T(8,128)(2,1)} %maximum_bitcast_fusion.1), calls=%async_computation.4 | async-start | bytes 917504 | tf_op jit(solution)/shard_map/all_to_all | solution.py:405
  120.3 0.8 maximum_bitcast_fusion
  121.1 7.5 %all-to-all-done.4 = bf16[16,8,1792]{2,1,0:T(8,128)(2,1)S(1)} async-done(((bf16[16,8,1792]{2,1,0:T(8,128)(2,1)}), bf16[16,8,1792]{2,1,0:T(8,128)(2,1)S(1)}, u32[]{:S(2)}, u32[]{:S(2)}) %all-to-all-start.4) | async-done | bytes 458784 | tf_op jit(solution)/shard_map/all_to_all | solution.py:405
  128.7 4.8 %all-to-all-start.3 = ((bf16[16,8,1792]{2,1,0:T(8,128)(2,1)}), bf16[16,8,1792]{2,1,0:T(8,128)(2,1)S(1)}, u32[]{:S(2)}, u32[]{:S(2)}) async-start(bf16[16,8,1792]{2,1,0:T(8,128)(2,1)} %maximum_bitcast_fusion), calls=%async_computation.3 | async-start | bytes 917504 | tf_op jit(solution)/shard_map/all_to_all | solution.py:405
  133.5 3.9 %collective-permute-start.8 = (bf16[4,8,1792]{2,1,0:T(8,128)(2,1)S(1)}, bf16[4,8,1792]{2,1,0:T(8,128)(2,1)S(1)}, u32[]{:S(2)}, u32[]{:S(2)}) collective-permute-start(bf16[4,8,1792]{2,1,0:T(8,128)(2,1)S(1)} %bitcast_reduce_fusion), channel_id=1, source_target_pairs={{0,1},{1,0},{2,3},{3,2},{4,5},{5,4},{6,7},{7,6},{8,9},{9,8},{10,11... | collective-permute-start | bytes 344072 | tf_op jit(solution)/shard_map/ppermute | solution.py:32
  137.4 4.5 %all-to-all-done.3 = bf16[16,8,1792]{2,1,0:T(8,128)(2,1)S(1)} async-done(((bf16[16,8,1792]{2,1,0:T(8,128)(2,1)}), bf16[16,8,1792]{2,1,0:T(8,128)(2,1)S(1)}, u32[]{:S(2)}, u32[]{:S(2)}) %all-to-all-start.3) | async-done | bytes 458784 | tf_op jit(solution)/shard_map/all_to_all | solution.py:405
  141.9 0.8 convert_reduce_fusion.mine
  142.7 10.8 %collective-permute-done.8.got = bf16[4,8,1792]{2,1,0:T(8,128)(2,1)S(1)} collective-permute-done((bf16[4,8,1792]{2,1,0:T(8,128)(2,1)S(1)}, bf16[4,8,1792]{2,1,0:T(8,128)(2,1)S(1)}, u32[]{:S(2)}, u32[]{:S(2)}) %collective-permute-start.8) | collective-permute-done | bytes 114720 | tf_op jit(solution)/shard_map/ppermute | solution.py:32
  154.1 1.8 %shard_map.96 = bf16[8,7168]{1,0:T(8,128)(2,1)} custom-call(s32[1]{0:T(128)} %bitcast.core, f32[4,8,1792]{2,1,0:T(8,128)} %convert_reduce_fusion.mine, bf16[4,8,1792]{2,1,0:T(8,128)(2,1)} %copy-done.5), custom_call_target="tpu_custom_call" | custom-call | tf_op jit(solution)/shard_map/pallas_call | solution.py:317
  (32 shorter events, 5.5 us)
Async XLA Ops:
  6.5 20.3 %copy-start.3 = (bf16[512,8,128]{2,1,0:T(8,128)(2,1)S(1)}, bf16[512,8,128]{2,1,0:T(8,128)(2,1)}, u32[]{:S(2)}) copy-start(bf16[512,8,128]{2,1,0:T(8,128)(2,1)} %param.12) | copy-start | bytes 3145732
  6.5 88.4 %all-gather.2.cloned.1.call-start = ((), (), s32[]{:S(2)}) async-start(), calls=%async_computation.5 | async-start | bytes 2064384 | tf_op jit(solution)/shard_map/all_gather | solution.py:348
  9.5 17.6 %copy-start = (bf16[1152,128]{1,0:T(8,128)(2,1)}, bf16[1152,128]{1,0:T(8,128)(2,1)S(1)}, u32[]{:S(2)}) copy-start(bf16[1152,128]{1,0:T(8,128)(2,1)S(1)} %all_gather.6) | copy-start | bytes 884740
  9.5 20.0 %collective-permute-start = (bf16[2,576,128]{2,1,0:T(8,128)(2,1)S(1)}, bf16[2,576,128]{2,1,0:T(8,128)(2,1)S(1)}, u32[]{:S(2)}, u32[]{:S(2)}) collective-permute-start(bf16[2,576,128]{2,1,0:T(8,128)(2,1)S(1)} %bitcast.37), channel_id=1, source_target_pairs={{0,32},{1,33},{8,105},{9,104},{16,48},{17,49},{24,121},{25,120},{3... | collective-permute-start | bytes 884744 | tf_op jit(solution)/shard_map/ppermute | solution.py:32
  14.7 15.6 %collective-permute-start.2 = (bf16[2,576,128]{2,1,0:T(8,128)(2,1)S(1)}, bf16[2,576,128]{2,1,0:T(8,128)(2,1)}, u32[]{:S(2)}, u32[]{:S(2)}) collective-permute-start(bf16[2,576,128]{2,1,0:T(8,128)(2,1)S(1)} %bitcast.38), channel_id=1, source_target_pairs={{0,16},{1,17},{8,121},{9,120},{16,32},{17,33},{24,8},{25,9},{32,48... | collective-permute-start | bytes 884744 | tf_op jit(solution)/shard_map/ppermute | solution.py:32
  22.3 18.8 %all-to-all-start = ((bf16[4,64,1664]{2,1,0:T(8,128)(2,1)}), bf16[4,64,1664]{2,1,0:T(8,128)(2,1)S(1)}, u32[]{:S(2)}, u32[]{:S(2)}) async-start(bf16[4,64,1664]{2,1,0:T(8,128)(2,1)} %shard_map.91), calls=%async_computation | async-start | bytes 1703936 | tf_op jit(solution)/shard_map/all_to_all | solution.py:48
  29.5 0.8 copy-start.4
  32.2 10.1 %collective-permute-start.4 = (bf16[4,576,128]{2,1,0:T(8,128)(2,1)S(1)}, bf16[4,576,128]{2,1,0:T(8,128)(2,1)}, u32[]{:S(2)}, u32[]{:S(2)}) collective-permute-start(bf16[4,576,128]{2,1,0:T(8,128)(2,1)S(1)} %constant_dynamic-update-slice_fusion.rest_1_), channel_id=1, source_target_pairs={{0,8},{8,0},{1,9},{9,1},{2,10},{10,2},{3,11},{11,3},{4,12},{12,4},... | collective-permute-start | bytes 1769480 | tf_op jit(solution)/shard_map/ppermute | solution.py:32
  34.2 30.6 %collective-permute-start.1 = (bf16[2,576,128]{2,1,0:T(8,128)(2,1)}, bf16[2,576,128]{2,1,0:T(8,128)(2,1)}, u32[]{:S(2)}, u32[]{:S(2)}) collective-permute-start(bf16[2,576,128]{2,1,0:T(8,128)(2,1)} %copy-done.4), channel_id=1, source_target_pairs={{0,16},{1,17},{8,121},{9,120},{16,32},{17,33},{24,8},{25,9},{32,48... | collective-permute-start | bytes 884744 | tf_op jit(solution)/shard_map/ppermute | solution.py:32
  37.1 27.6 %collective-permute-start.3 = (bf16[1,576,128]{2,1,0:T(8,128)(2,1)}, bf16[1,576,128]{2,1,0:T(8,128)(2,1)}, u32[]{:S(2)}, u32[]{:S(2)}) collective-permute-start(bf16[1,576,128]{2,1,0:T(8,128)(2,1)} %constant_dynamic-slice_fusion), channel_id=1, source_target_pairs={{0,32},{1,33},{8,105},{9,104},{16,48},{17,49},{24,121},{25,120},{3... | collective-permute-start | bytes 442376 | tf_op jit(solution)/shard_map/ppermute | solution.py:32
  41.1 1.2 copy-start.1
  64.7 5.5 %collective-permute-start.5 = (bf16[2,576,128]{2,1,0:T(8,128)(2,1)}, bf16[2,576,128]{2,1,0:T(8,128)(2,1)S(1)}, u32[]{:S(2)}, u32[]{:S(2)}) collective-permute-start(bf16[2,576,128]{2,1,0:T(8,128)(2,1)} %collective-permute-done.1.rest_0_), channel_id=1, source_target_pairs={{0,8},{8,0},{1,9},{9,1},{2,10},{10,2},{3,11},{11,3},{4,12},{12,4},... | collective-permute-start | bytes 884744 | tf_op jit(solution)/shard_map/ppermute | solution.py:32
  66.6 3.6 %collective-permute-start.6 = (bf16[1,576,128]{2,1,0:T(8,128)(2,1)}, bf16[1,576,128]{2,1,0:T(8,128)(2,1)S(1)}, u32[]{:S(2)}, u32[]{:S(2)}) collective-permute-start(bf16[1,576,128]{2,1,0:T(8,128)(2,1)} %collective-permute-done.3.rest_2_), channel_id=1, source_target_pairs={{0,8},{8,0},{1,9},{9,1},{2,10},{10,2},{3,11},{11,3},{4,12},{12,4},... | collective-permute-start | bytes 442376 | tf_op jit(solution)/shard_map/ppermute | solution.py:32
  95.0 16.0 %copy-start.2 = (bf16[896,1024]{1,0:T(8,128)(2,1)S(1)}, bf16[896,1024]{1,0:T(8,128)(2,1)}, u32[]{:S(2)}) copy-start(bf16[896,1024]{1,0:T(8,128)(2,1)} %all-gather.2.cloned.1.call-done) | copy-start | bytes 5505028
  95.0 17.4 %collective-permute-start.7 = (bf16[896,1024]{1,0:T(8,128)(2,1)}, bf16[896,1024]{1,0:T(8,128)(2,1)S(1)}, u32[]{:S(2)}, u32[]{:S(2)}) collective-permute-start(bf16[896,1024]{1,0:T(8,128)(2,1)} %all-gather.2.cloned.1.call-done), channel_id=1, source_target_pairs={{0,8},{8,0},{1,9},{9,1},{2,10},{10,2},{3,11},{11,3},{4,12},{12,4},... | collective-permute-start | bytes 5505032 | tf_op jit(solution)/shard_map/ppermute | solution.py:32
  113.9 14.7 %all-to-all-start.4 = ((bf16[16,8,1792]{2,1,0:T(8,128)(2,1)}), bf16[16,8,1792]{2,1,0:T(8,128)(2,1)S(1)}, u32[]{:S(2)}, u32[]{:S(2)}) async-start(bf16[16,8,1792]{2,1,0:T(8,128)(2,1)} %maximum_bitcast_fusion.1), calls=%async_computation.4 | async-start | bytes 917504 | tf_op jit(solution)/shard_map/all_to_all | solution.py:405
  128.7 13.2 %all-to-all-start.3 = ((bf16[16,8,1792]{2,1,0:T(8,128)(2,1)}), bf16[16,8,1792]{2,1,0:T(8,128)(2,1)S(1)}, u32[]{:S(2)}, u32[]{:S(2)}) async-start(bf16[16,8,1792]{2,1,0:T(8,128)(2,1)} %maximum_bitcast_fusion), calls=%async_computation.3 | async-start | bytes 917504 | tf_op jit(solution)/shard_map/all_to_all | solution.py:405
  133.5 20.0 %collective-permute-start.8 = (bf16[4,8,1792]{2,1,0:T(8,128)(2,1)S(1)}, bf16[4,8,1792]{2,1,0:T(8,128)(2,1)S(1)}, u32[]{:S(2)}, u32[]{:S(2)}) collective-permute-start(bf16[4,8,1792]{2,1,0:T(8,128)(2,1)S(1)} %bitcast_reduce_fusion), channel_id=1, source_target_pairs={{0,1},{1,0},{2,3},{3,2},{4,5},{5,4},{6,7},{7,6},{8,9},{9,8},{10,11... | collective-permute-start | bytes 344072 | tf_op jit(solution)/shard_map/ppermute | solution.py:32
  153.5 0.6 copy-start.5
Sparse Core Ops, SparseCore 0:
  9.4 62.8 all-gather.1

commit v11 on v9

--- a/solution.py
+++ b/solution.py
@@ -48,21 +48,19 @@
 
 
 def pack_kernel(order, content, rotary, out, *, block):
-    heads, nope = content.shape[1:]
-    left = heads * nope
+    left = content.shape[1]
     width = left + rotary.shape[1]
     row = lax.broadcasted_iota(jnp.int32, (out.shape[1], STATS), 0)
     number = jnp.where(row < block, order[0], order[1]).astype(jnp.float32).astype(out.dtype)
     for i in range(out.shape[0]):
-        for h in range(heads):
-            out[i, :, h * nope : (h + 1) * nope] = content[:, h, :]
+        out[i, :, :left] = content[...]
         out[i, :, left:width] = rotary[...]
         out[i, :, width:] = number
 
 
 def pack(order, content, rotary, block, copies):
-    rows, heads, nope = content.shape
-    width = heads * nope + rotary.shape[1] + STATS
+    rows = content.shape[0]
+    width = content.shape[1] + rotary.shape[1] + STATS
     vmem = pl.BlockSpec(memory_space=pltpu.VMEM)
     return pl.pallas_call(
         functools.partial(pack_kernel, block=block),
@@ -318,7 +316,8 @@
 
     weight = lax.all_gather(output_weight.T, "z", axis=0, tiled=True)
 
-    packed = pack(block_order, query_content, query_rotary, block, 4)
+    content = query_content.reshape(tokens, heads * nope)
+    packed = pack(block_order, content, query_rotary, block, 4)
 
     pair = lax.all_gather(key_cache, "c", axis=0, tiled=True).reshape(2, *key_cache.shape)
     one, two = along_z(pair, 1), along_z(pair, 2)

time: 157 us -> 157 us (level)
  the two profiles are of different devices: /device:TPU:32 before, /device:TPU:98 now
where the time goes in v11:
time: 157 us
  starting transfers between devices  53.6 us (34%)
  blocking collectives  31.3 us (20%)
  Pallas kernels  23.1 us (15%)
  waiting for transfers between devices  21.4 us (14%)
  between operations  14.9 us (9%)
  local copies, waits for them, and re-layouts  7.45 us (5%)
  matrix products  2.86 us (2%)
  other arithmetic  1.87 us (1%)
    ppermute x9, starting transfers between devices, permute(): return lax.ppermute(x, names, pairs)  39 us
    all_to_all x2, blocking collectives, swap_y(): return lax.all_to_all(x, 'y', split_axis=0, concat_axis=0, tiled=True)  29.1 us
    pallas_call x2, Pallas kernels, attend(): pl.pallas_call(kernel, in_specs=[pl.BlockSpec(memory_space=pltpu.SMEM)] *...  17.6 us
    ppermute x9, waiting for transfers between devices, permute(): return lax.ppermute(x, names, pairs)  13.2 us
    all_to_all x2, starting transfers between devices, summed(): lax.all_to_all(product.reshape(16, share, -1), ('y', 'x'), split_axis=0,...  10.2 us
    all_to_all x2, waiting for transfers between devices, summed(): lax.all_to_all(product.reshape(16, share, -1), ('y', 'x'), split_axis=0,...  7.54 us
    unnamed x14, local copies, waits for them, and re-layouts  4.55 us
    all_to_all x1, starting transfers between devices, swap_y(): return lax.all_to_all(x, 'y', split_axis=0, concat_axis=0, tiled=True)  4.46 us
  transfers between devices with their start and end apart: 13, of which 4 were waited for; matrix products, arithmetic and copies ran while one was open for 6% of the time, Pallas kernels for 15%

profile of v11, /device:TPU:98, one launch (start us, length us, event | category | flops | bytes accessed | tf_op | source)
XLA Modules:
  0.0 156.5 jit_solution(1457025031837291854)
XLA Ops:
  7.3 2.2 %all_gather.6 = bf16[1152,128]{1,0:T(8,128)(2,1)S(1)} all-gather(bf16[576,128]{1,0:T(8,128)(2,1)} %param.11), channel_id=1, replica_groups=mesh['y'=4,'z'=8,'c'=2,'x'=4,'h'=2] {'c'}, dimensions={0}, use_global_device_ids=true | all-gather | bytes 442368 | tf_op jit(solution)/shard_map/all_gather | solution.py:322
  9.5 6.4 %collective-permute-start = (bf16[2,576,128]{2,1,0:T(8,128)(2,1)S(1)}, bf16[2,576,128]{2,1,0:T(8,128)(2,1)S(1)}, u32[]{:S(2)}, u32[]{:S(2)}) collective-permute-start(bf16[2,576,128]{2,1,0:T(8,128)(2,1)S(1)} %bitcast.43), channel_id=1, source_target_pairs={{0,32},{1,33},{8,105},{9,104},{16,48},{17,49},{24,121},{25,120},{3... | collective-permute-start | bytes 884744 | tf_op jit(solution)/shard_map/ppermute | solution.py:31
  15.9 3.8 %collective-permute-start.2 = (bf16[2,576,128]{2,1,0:T(8,128)(2,1)S(1)}, bf16[2,576,128]{2,1,0:T(8,128)(2,1)}, u32[]{:S(2)}, u32[]{:S(2)}) collective-permute-start(bf16[2,576,128]{2,1,0:T(8,128)(2,1)S(1)} %bitcast.44), channel_id=1, source_target_pairs={{0,16},{1,17},{8,121},{9,120},{16,32},{17,33},{24,8},{25,9},{32,48... | collective-permute-start | bytes 884744 | tf_op jit(solution)/shard_map/ppermute | solution.py:31
  19.7 1.6 %copy.19 = bf16[8,8,8,128]{3,1,2,0:T(8,128)(2,1)} copy(bf16[8,8,8,128]{3,2,1,0:T(8,128)(2,1)} %bitcast.53) | data formatting | bytes 262144
  21.3 1.9 %shard_map.91 = bf16[4,64,1664]{2,1,0:T(8,128)(2,1)} custom-call(s32[2]{0:T(128)} %order.1, bf16[64,1024]{1,0:T(8,128)(2,1)} %bitcast.51, bf16[64,512]{1,0:T(8,128)(2,1)} %rotary.1), custom_call_target="tpu_custom_call" | custom-call | tf_op jit(solution)/shard_map/pallas_call | solution.py:65
  23.2 4.5 %all-to-all-start = ((bf16[4,64,1664]{2,1,0:T(8,128)(2,1)}), bf16[4,64,1664]{2,1,0:T(8,128)(2,1)S(1)}, u32[]{:S(2)}, u32[]{:S(2)}) async-start(bf16[4,64,1664]{2,1,0:T(8,128)(2,1)} %shard_map.91), calls=%async_computation | async-start | bytes 1703936 | tf_op jit(solution)/shard_map/all_to_all | solution.py:47
  27.9 1.6 %copy.12 = bf16[512,8,128]{0,2,1:T(8,128)(2,1)S(1)} copy(bf16[512,8,128]{2,1,0:T(8,128)(2,1)} %param.13) | data formatting | bytes 2097152 | tf_op args[4]
  31.1 1.0 constant_dynamic-update-slice_fusion.1
  32.1 1.0 constant_dynamic-update-slice_fusion.rest_1_
  33.1 1.9 %collective-permute-start.4 = (bf16[4,576,128]{2,1,0:T(8,128)(2,1)S(1)}, bf16[4,576,128]{2,1,0:T(8,128)(2,1)}, u32[]{:S(2)}, u32[]{:S(2)}) collective-permute-start(bf16[4,576,128]{2,1,0:T(8,128)(2,1)S(1)} %constant_dynamic-update-slice_fusion.rest_1_), channel_id=1, source_target_pairs={{0,8},{8,0},{1,9},{9,1},{2,10},{10,2},{3,11},{11,3},{4,12},{12,4},... | collective-permute-start | bytes 1769480 | tf_op jit(solution)/shard_map/ppermute | solution.py:31
  35.0 3.8 %collective-permute-start.1 = (bf16[2,576,128]{2,1,0:T(8,128)(2,1)}, bf16[2,576,128]{2,1,0:T(8,128)(2,1)}, u32[]{:S(2)}, u32[]{:S(2)}) collective-permute-start(bf16[2,576,128]{2,1,0:T(8,128)(2,1)} %copy-done.4), channel_id=1, source_target_pairs={{0,16},{1,17},{8,121},{9,120},{16,32},{17,33},{24,8},{25,9},{32,48... | collective-permute-start | bytes 884744 | tf_op jit(solution)/shard_map/ppermute | solution.py:31
  38.8 5.5 %collective-permute-start.3 = (bf16[1,576,128]{2,1,0:T(8,128)(2,1)}, bf16[1,576,128]{2,1,0:T(8,128)(2,1)}, u32[]{:S(2)}, u32[]{:S(2)}) collective-permute-start(bf16[1,576,128]{2,1,0:T(8,128)(2,1)} %constant_dynamic-slice_fusion), channel_id=1, source_target_pairs={{0,32},{1,33},{8,105},{9,104},{16,48},{17,49},{24,121},{25,120},{3... | collective-permute-start | bytes 442376 | tf_op jit(solution)/shard_map/ppermute | solution.py:31
  45.0 1.2 shard_map.92
  46.2 10.3 %shard_map.93.rest_5_ = bf16[256,1152]{1,0:T(8,128)(2,1)S(1)} custom-call(s32[8]{0:T(128)S(1)} %get-tuple-element.22.starts, s32[4]{0:T(128)S(1)} %pad_add_fusion.place, bf16[8,576,256]{2,1,0:T(8,128)(2,1)S(1)} %get-tuple-element.24.query, bf16[2,576,128]{2,1,0:T(8,128)(2,1)S(1)} %bitcast.45, ...), custom_call_target="tpu_custom_call" | custom-call | tf_op jit(solution)/shard_map/pallas_call | solution.py:243
  56.7 3.4 %collective-permute-start.5 = (bf16[2,576,128]{2,1,0:T(8,128)(2,1)}, bf16[2,576,128]{2,1,0:T(8,128)(2,1)S(1)}, u32[]{:S(2)}, u32[]{:S(2)}) collective-permute-start(bf16[2,576,128]{2,1,0:T(8,128)(2,1)} %collective-permute-done.1.rest_0_), channel_id=1, source_target_pairs={{0,8},{8,0},{1,9},{9,1},{2,10},{10,2},{3,11},{11,3},{4,12},{12,4},... | collective-permute-start | bytes 884744 | tf_op jit(solution)/shard_map/ppermute | solution.py:31
  60.1 1.9 %collective-permute-start.6 = (bf16[1,576,128]{2,1,0:T(8,128)(2,1)}, bf16[1,576,128]{2,1,0:T(8,128)(2,1)S(1)}, u32[]{:S(2)}, u32[]{:S(2)}) collective-permute-start(bf16[1,576,128]{2,1,0:T(8,128)(2,1)} %collective-permute-done.3.rest_2_), channel_id=1, source_target_pairs={{0,8},{8,0},{1,9},{9,1},{2,10},{10,2},{3,11},{11,3},{4,12},{12,4},... | collective-permute-start | bytes 442376 | tf_op jit(solution)/shard_map/ppermute | solution.py:31
  62.0 1.5 collective-permute-done.6.rest_3_
  63.6 7.3 %shard_map.94 = bf16[256,1152]{1,0:T(8,128)(2,1)S(1)} custom-call(s32[8]{0:T(128)S(1)} %get-tuple-element.22.starts, s32[4]{0:T(128)S(1)} %pad_add_fusion.place, bf16[8,576,256]{2,1,0:T(8,128)(2,1)S(1)} %get-tuple-element.24.query, bf16[2,576,128]{2,1,0:T(8,128)(2,1)} %collective-permute-done.1.rest_0_, ...), custom_call_target="tpu_custom_call" | custom-call | tf_op jit(solution)/shard_map/pallas_call | solution.py:243
  70.9 15.2 %all_to_all.25.parts = bf16[4,64,1152]{2,1,0:T(8,128)(2,1)} all-to-all(bf16[4,64,1152]{2,1,0:T(8,128)(2,1)S(1)} %bitcast.42), channel_id=1, replica_groups=mesh['y'=4,'z'=8,'c'=2,'x'=4,'h'=2] {'y'}, dimensions={0} | all-to-all | bytes 1179648 | tf_op jit(solution)/shard_map/all_to_all | solution.py:47
  86.1 2.4 %shard_map.95 = bf16[4,64,1024]{2,1,0:T(8,128)(2,1)} custom-call(s32[1]{0:T(128)} %bitcast.5.half, bf16[4,64,1152]{2,1,0:T(8,128)(2,1)} %all_to_all.25.parts), custom_call_target="tpu_custom_call" | custom-call | tf_op jit(solution)/shard_map/pallas_call | solution.py:288
  88.5 2.0 %collective-permute-start.7 = (bf16[896,1024]{1,0:T(8,128)(2,1)}, bf16[896,1024]{1,0:T(8,128)(2,1)S(1)}, u32[]{:S(2)}, u32[]{:S(2)}) collective-permute-start(bf16[896,1024]{1,0:T(8,128)(2,1)} %all-gather.2.cloned.1.call-done), channel_id=1, source_target_pairs={{0,8},{8,0},{1,9},{9,1},{2,10},{10,2},{3,11},{11,3},{4,12},{12,4},... | collective-permute-start | bytes 5505032 | tf_op jit(solution)/shard_map/ppermute | solution.py:31
  90.5 13.9 %all_to_all.26 = bf16[4,64,1024]{2,1,0:T(8,128)(2,1)S(1)} all-to-all(bf16[4,64,1024]{2,1,0:T(8,128)(2,1)} %shard_map.95), channel_id=1, replica_groups=mesh['y'=4,'z'=8,'c'=2,'x'=4,'h'=2] {'y'}, dimensions={0} | all-to-all | bytes 1048576 | tf_op jit(solution)/shard_map/all_to_all | solution.py:47
  104.4 0.7 convolution_convert_fusion.3
  105.2 0.7 convolution_convert_fusion.1
  106.6 0.8 maximum_bitcast_fusion.1
  107.4 5.4 %all-to-all-start.4 = ((bf16[16,8,1792]{2,1,0:T(8,128)(2,1)}), bf16[16,8,1792]{2,1,0:T(8,128)(2,1)S(1)}, u32[]{:S(2)}, u32[]{:S(2)}) async-start(bf16[16,8,1792]{2,1,0:T(8,128)(2,1)} %maximum_bitcast_fusion.1), calls=%async_computation.4 | async-start | bytes 917504 | tf_op jit(solution)/shard_map/all_to_all | solution.py:372
  113.5 0.8 maximum_bitcast_fusion
  114.4 7.5 %all-to-all-done.4 = bf16[16,8,1792]{2,1,0:T(8,128)(2,1)S(1)} async-done(((bf16[16,8,1792]{2,1,0:T(8,128)(2,1)}), bf16[16,8,1792]{2,1,0:T(8,128)(2,1)S(1)}, u32[]{:S(2)}, u32[]{:S(2)}) %all-to-all-start.4) | async-done | bytes 458784 | tf_op jit(solution)/shard_map/all_to_all | solution.py:372
  121.9 4.8 %all-to-all-start.3 = ((bf16[16,8,1792]{2,1,0:T(8,128)(2,1)}), bf16[16,8,1792]{2,1,0:T(8,128)(2,1)S(1)}, u32[]{:S(2)}, u32[]{:S(2)}) async-start(bf16[16,8,1792]{2,1,0:T(8,128)(2,1)} %maximum_bitcast_fusion), calls=%async_computation.3 | async-start | bytes 917504 | tf_op jit(solution)/shard_map/all_to_all | solution.py:372
  126.7 10.2 %collective-permute-start.8 = (bf16[4,8,1792]{2,1,0:T(8,128)(2,1)S(1)}, bf16[4,8,1792]{2,1,0:T(8,128)(2,1)S(1)}, u32[]{:S(2)}, u32[]{:S(2)}) collective-permute-start(bf16[4,8,1792]{2,1,0:T(8,128)(2,1)S(1)} %bitcast_reduce_fusion), channel_id=1, source_target_pairs={{0,1},{1,0},{2,3},{3,2},{4,5},{5,4},{6,7},{7,6},{8,9},{9,8},{10,11... | collective-permute-start | bytes 344072 | tf_op jit(solution)/shard_map/ppermute | solution.py:31
  137.0 11.4 %collective-permute-done.8 = bf16[4,8,1792]{2,1,0:T(8,128)(2,1)S(1)} collective-permute-done((bf16[4,8,1792]{2,1,0:T(8,128)(2,1)S(1)}, bf16[4,8,1792]{2,1,0:T(8,128)(2,1)S(1)}, u32[]{:S(2)}, u32[]{:S(2)}) %collective-permute-start.8) | collective-permute-done | bytes 114720 | tf_op jit(solution)/shard_map/ppermute | solution.py:31
  148.8 0.8 reshape.50
  (35 shorter events, 4.0 us)
Async XLA Ops:
  6.5 81.9 %all-gather.2.cloned.1.call-start = ((), (), s32[]{:S(2)}) async-start(), calls=%async_computation.5 | async-start | bytes 2064384 | tf_op jit(solution)/shard_map/all_gather | solution.py:317
  6.5 21.1 %copy-start.3 = (bf16[512,8,128]{2,1,0:T(8,128)(2,1)S(1)}, bf16[512,8,128]{2,1,0:T(8,128)(2,1)}, u32[]{:S(2)}) copy-start(bf16[512,8,128]{2,1,0:T(8,128)(2,1)} %param.12) | copy-start | bytes 3145732
  9.5 18.4 %copy-start = (bf16[1152,128]{1,0:T(8,128)(2,1)}, bf16[1152,128]{1,0:T(8,128)(2,1)S(1)}, u32[]{:S(2)}) copy-start(bf16[1152,128]{1,0:T(8,128)(2,1)S(1)} %all_gather.6) | copy-start | bytes 884740
  9.5 20.8 %collective-permute-start = (bf16[2,576,128]{2,1,0:T(8,128)(2,1)S(1)}, bf16[2,576,128]{2,1,0:T(8,128)(2,1)S(1)}, u32[]{:S(2)}, u32[]{:S(2)}) collective-permute-start(bf16[2,576,128]{2,1,0:T(8,128)(2,1)S(1)} %bitcast.43), channel_id=1, source_target_pairs={{0,32},{1,33},{8,105},{9,104},{16,48},{17,49},{24,121},{25,120},{3... | collective-permute-start | bytes 884744 | tf_op jit(solution)/shard_map/ppermute | solution.py:31
  15.9 15.2 %collective-permute-start.2 = (bf16[2,576,128]{2,1,0:T(8,128)(2,1)S(1)}, bf16[2,576,128]{2,1,0:T(8,128)(2,1)}, u32[]{:S(2)}, u32[]{:S(2)}) collective-permute-start(bf16[2,576,128]{2,1,0:T(8,128)(2,1)S(1)} %bitcast.44), channel_id=1, source_target_pairs={{0,16},{1,17},{8,121},{9,120},{16,32},{17,33},{24,8},{25,9},{32,48... | collective-permute-start | bytes 884744 | tf_op jit(solution)/shard_map/ppermute | solution.py:31
  23.2 21.8 %all-to-all-start = ((bf16[4,64,1664]{2,1,0:T(8,128)(2,1)}), bf16[4,64,1664]{2,1,0:T(8,128)(2,1)S(1)}, u32[]{:S(2)}, u32[]{:S(2)}) async-start(bf16[4,64,1664]{2,1,0:T(8,128)(2,1)} %shard_map.91), calls=%async_computation | async-start | bytes 1703936 | tf_op jit(solution)/shard_map/all_to_all | solution.py:47
  30.3 0.8 copy-start.4
  33.1 13.1 %collective-permute-start.4 = (bf16[4,576,128]{2,1,0:T(8,128)(2,1)S(1)}, bf16[4,576,128]{2,1,0:T(8,128)(2,1)}, u32[]{:S(2)}, u32[]{:S(2)}) collective-permute-start(bf16[4,576,128]{2,1,0:T(8,128)(2,1)S(1)} %constant_dynamic-update-slice_fusion.rest_1_), channel_id=1, source_target_pairs={{0,8},{8,0},{1,9},{9,1},{2,10},{10,2},{3,11},{11,3},{4,12},{12,4},... | collective-permute-start | bytes 1769480 | tf_op jit(solution)/shard_map/ppermute | solution.py:31
  35.0 21.7 %collective-permute-start.1 = (bf16[2,576,128]{2,1,0:T(8,128)(2,1)}, bf16[2,576,128]{2,1,0:T(8,128)(2,1)}, u32[]{:S(2)}, u32[]{:S(2)}) collective-permute-start(bf16[2,576,128]{2,1,0:T(8,128)(2,1)} %copy-done.4), channel_id=1, source_target_pairs={{0,16},{1,17},{8,121},{9,120},{16,32},{17,33},{24,8},{25,9},{32,48... | collective-permute-start | bytes 884744 | tf_op jit(solution)/shard_map/ppermute | solution.py:31
  38.8 17.9 %collective-permute-start.3 = (bf16[1,576,128]{2,1,0:T(8,128)(2,1)}, bf16[1,576,128]{2,1,0:T(8,128)(2,1)}, u32[]{:S(2)}, u32[]{:S(2)}) collective-permute-start(bf16[1,576,128]{2,1,0:T(8,128)(2,1)} %constant_dynamic-slice_fusion), channel_id=1, source_target_pairs={{0,32},{1,33},{8,105},{9,104},{16,48},{17,49},{24,121},{25,120},{3... | collective-permute-start | bytes 442376 | tf_op jit(solution)/shard_map/ppermute | solution.py:31
  45.0 1.2 copy-start.1
  56.7 6.9 %collective-permute-start.5 = (bf16[2,576,128]{2,1,0:T(8,128)(2,1)}, bf16[2,576,128]{2,1,0:T(8,128)(2,1)S(1)}, u32[]{:S(2)}, u32[]{:S(2)}) collective-permute-start(bf16[2,576,128]{2,1,0:T(8,128)(2,1)} %collective-permute-done.1.rest_0_), channel_id=1, source_target_pairs={{0,8},{8,0},{1,9},{9,1},{2,10},{10,2},{3,11},{11,3},{4,12},{12,4},... | collective-permute-start | bytes 884744 | tf_op jit(solution)/shard_map/ppermute | solution.py:31
  60.1 3.5 %collective-permute-start.6 = (bf16[1,576,128]{2,1,0:T(8,128)(2,1)}, bf16[1,576,128]{2,1,0:T(8,128)(2,1)S(1)}, u32[]{:S(2)}, u32[]{:S(2)}) collective-permute-start(bf16[1,576,128]{2,1,0:T(8,128)(2,1)} %collective-permute-done.3.rest_2_), channel_id=1, source_target_pairs={{0,8},{8,0},{1,9},{9,1},{2,10},{10,2},{3,11},{11,3},{4,12},{12,4},... | collective-permute-start | bytes 442376 | tf_op jit(solution)/shard_map/ppermute | solution.py:31
  88.5 16.0 %copy-start.2 = (bf16[896,1024]{1,0:T(8,128)(2,1)S(1)}, bf16[896,1024]{1,0:T(8,128)(2,1)}, u32[]{:S(2)}) copy-start(bf16[896,1024]{1,0:T(8,128)(2,1)} %all-gather.2.cloned.1.call-done) | copy-start | bytes 5505028
  88.5 17.4 %collective-permute-start.7 = (bf16[896,1024]{1,0:T(8,128)(2,1)}, bf16[896,1024]{1,0:T(8,128)(2,1)S(1)}, u32[]{:S(2)}, u32[]{:S(2)}) collective-permute-start(bf16[896,1024]{1,0:T(8,128)(2,1)} %all-gather.2.cloned.1.call-done), channel_id=1, source_target_pairs={{0,8},{8,0},{1,9},{9,1},{2,10},{10,2},{3,11},{11,3},{4,12},{12,4},... | collective-permute-start | bytes 5505032 | tf_op jit(solution)/shard_map/ppermute | solution.py:31
  107.4 14.5 %all-to-all-start.4 = ((bf16[16,8,1792]{2,1,0:T(8,128)(2,1)}), bf16[16,8,1792]{2,1,0:T(8,128)(2,1)S(1)}, u32[]{:S(2)}, u32[]{:S(2)}) async-start(bf16[16,8,1792]{2,1,0:T(8,128)(2,1)} %maximum_bitcast_fusion.1), calls=%async_computation.4 | async-start | bytes 917504 | tf_op jit(solution)/shard_map/all_to_all | solution.py:372
  121.9 15.0 %all-to-all-start.3 = ((bf16[16,8,1792]{2,1,0:T(8,128)(2,1)}), bf16[16,8,1792]{2,1,0:T(8,128)(2,1)S(1)}, u32[]{:S(2)}, u32[]{:S(2)}) async-start(bf16[16,8,1792]{2,1,0:T(8,128)(2,1)} %maximum_bitcast_fusion), calls=%async_computation.3 | async-start | bytes 917504 | tf_op jit(solution)/shard_map/all_to_all | solution.py:372
  126.7 21.7 %collective-permute-start.8 = (bf16[4,8,1792]{2,1,0:T(8,128)(2,1)S(1)}, bf16[4,8,1792]{2,1,0:T(8,128)(2,1)S(1)}, u32[]{:S(2)}, u32[]{:S(2)}) collective-permute-start(bf16[4,8,1792]{2,1,0:T(8,128)(2,1)S(1)} %bitcast_reduce_fusion), channel_id=1, source_target_pairs={{0,1},{1,0},{2,3},{3,2},{4,5},{5,4},{6,7},{7,6},{8,9},{9,8},{10,11... | collective-permute-start | bytes 344072 | tf_op jit(solution)/shard_map/ppermute | solution.py:31
Sparse Core Ops, SparseCore 0:
  9.4 66.1 all-gather.1
